TPU v7x, 128 devices: a whole 4x4x4 slice. The times are simulated.
128 devices in a mesh: grp: 4 (over y_hi, core), pen: 32 (over x, y_lo, z).
Axes of the slice: x: 4, y: 4 (y_hi: 2, y_lo: 2; y = y_hi * 2 + y_lo), z: 4, core: 2. Of those that a mesh axis runs over, the one named last changes fastest.
Arguments:
- pressure_source: float32 [16, 1024, 4096], P('grp', None, 'pen'), may hold values from -15 to 15
- solid_temp: float32 [16, 1024, 4096], P(None, 'grp', 'pen'), may hold values from -6 to 6
- gas_wall_temp: float32 [1024, 4096], P('grp', 'pen'), may hold values from -6 to 6
- phase_map: int32 [16, 1024, 4096], P(None, 'grp', 'pen'), may hold values 0 or 1
- phase_conductivity: float32 [2], replicated, may hold values from 0.3 to 1
Outputs:
- pressure: float32 [16, 1024, 4096], P('grp', None, 'pen')
- solid_final: float32 [16, 1024, 4096], P(None, 'grp', 'pen')
All inputs are finite; a program needn't handle non-finite values. No bound on the sum of `phase_map` on one device may be relied on, other than what follows from the above.
Results may differ from a plain program's by a relative error of at most 0.0003.
Values sent between devices are 32-bit elements; how exact they have to be, the bound alone decides.
No kernel may reach another device: no remote copies, remote signals or barrier semaphores. Data moves between devices by JAX's collectives and lax.ppermute only.
A program may use at most 128 MiB of HBM per device.

v0:
```python
import functools
import math

import jax
import jax.numpy as jnp
import numpy as np
from jax import lax
from jax.experimental import pallas as pl
from jax.experimental.pallas import tpu as pltpu
from jax.sharding import PartitionSpec as P

HIGHEST = lax.Precision.HIGHEST
HEAT_TRANSFER = 1.0
PRESSURE_WORK = 0.5
STEP_RATE = 0.12
Z_RING, Y_PAIR, X_RING = 4, 2, 4
VMEM_LIMIT = 48 * 1024 * 1024
LANES = 256


def halves(value):
    high = np.asarray(value, np.float32).astype(jnp.bfloat16)
    low = (np.asarray(value, np.float64) - high.astype(np.float64)).astype(jnp.bfloat16)
    return high, low


def make_tables(span_len, width, depth):
    half = span_len // 2
    waves = np.stack([2 * np.arange(half), 2 * np.arange(half) + 1]).astype(np.float64)
    rows = np.arange(half)
    angle = 2 * np.pi * ((rows[None, :, None] * waves[:, None, :]) % span_len) / span_len
    span = np.cos(angle) + np.sin(angle)
    lam = -4 * np.sin(np.pi * waves / span_len) ** 2
    order = np.concatenate([np.arange(0, width, 2), np.arange(1, width, 2)]) + 1.0
    cells = np.arange(width) + 1.0
    sine = np.sqrt(2 / (width + 1)) * np.sin(np.pi * cells[:, None] * order[None, :] / (width + 1))
    sigma = -4 * np.sin(np.pi * order / (2 * (width + 1))) ** 2
    modes = np.arange(depth)
    theta = np.pi * (2 * modes + 1) / (2 * depth + 1)
    basis = np.cos(theta[None, :] * (np.arange(depth)[:, None] + 0.5)) / np.sqrt((2 * depth + 1) / 4)
    mu = -4 * np.sin(theta / 2) ** 2
    stretch = -(mu[None, :, None] + lam[:, None, :])
    log_rho = -2 * np.arcsinh(np.sqrt(stretch) / 2)
    down = np.arange(depth // 2)
    up = depth - 1 - down
    ordered = np.stack([basis[np.concatenate([down, up])], basis[np.concatenate([up, down])]])
    pair = np.kron(np.eye(2), sine)
    f32 = lambda v: np.asarray(v, np.float32)
    lanes = min(LANES, half)
    return {
        "span": halves(span),
        "into": halves(pair / span_len),
        "back": halves(pair.T),
        "lam": f32(lam)[:, None, :],
        "sigma": f32(np.repeat(sigma[:, None], lanes, 1)),
        "edge": f32(np.repeat(sine[0][:, None], lanes, 1)),
        "basis": f32(ordered),
        "basis_t": f32(np.swapaxes(ordered, 1, 2)),
        "log_rho": f32(log_rho),
        "far": f32(np.exp(log_rho * (width + 1))),
    }


def product(first, second):
    return jnp.dot(first, second, preferred_element_type=jnp.float32)


def split(value):
    high = value.astype(jnp.bfloat16)
    return high, (value - high.astype(jnp.float32)).astype(jnp.bfloat16)


def times(value, high, low):
    value_high, value_low = split(value)
    return product(value_high, high) + (product(value_high, low) + product(value_low, high))


def times_turned(high, low, value):
    value_high, value_low = split(value)
    turned = lambda a, b: lax.dot_general(
        a, b, (((1,), (1,)), ((), ())), preferred_element_type=jnp.float32
    )
    return turned(high, value_high) + (turned(low, value_high) + turned(high, value_low))


def whole(array):
    return pl.BlockSpec(array.shape, lambda i, s: (0,) * len(array.shape))


def chosen(array, place):
    rest = array.shape[1:]
    return pl.BlockSpec((1,) + rest, lambda i, s: (s[place],) + (0,) * len(rest))


def run(body, scalars, arrays, specs, outs, out_specs=None, scratch=(), aliases=None, flops=0):
    outs = [jax.ShapeDtypeStruct(shape, jnp.float32) for shape in outs]
    moved = sum(math.prod(a.shape) * 4 for a in arrays) + sum(math.prod(o.shape) * 4 for o in outs)
    return pl.pallas_call(
        body,
        out_shape=outs,
        grid_spec=pltpu.PrefetchScalarGridSpec(
            num_scalar_prefetch=1,
            grid=(1,),
            in_specs=specs,
            out_specs=out_specs or [whole(o) for o in outs],
            scratch_shapes=list(scratch),
        ),
        input_output_aliases=aliases or {},
        compiler_params=pltpu.CompilerParams(vmem_limit_bytes=VMEM_LIMIT),
        cost_estimate=pl.CostEstimate(flops=flops, bytes_accessed=moved, transcendentals=0),
    )(scalars, *arrays)


def spectral(planes, into_high, into_low, span_high, span_low):
    turned = []
    for pair in range(0, len(planes), 2):
        cells = jnp.concatenate(planes[pair : pair + 2], axis=1)
        turned.append(times(cells, into_high, into_low).T)
    return times(jnp.concatenate(turned, axis=0), span_high, span_low)


def held_body(s_ref, source, into_high, into_low, span_high, span_low, out):
    count, span_len, _ = source.shape
    half = span_len // 2
    sign = (1 - 2 * s_ref[0]).astype(jnp.float32)
    planes = [source[z, :half] + sign * source[z, half:] for z in range(count)]
    out[...] = spectral(
        planes, into_high[...], into_low[...], span_high[0], span_low[0]
    ).reshape(out.shape)


def continuants(centre, first, count):
    values = [jnp.ones_like(centre), centre + first]
    for _ in range(1, count):
        values.append(centre * values[-1] - values[-2])
    return values


def arrived_body(
    s_ref, arrived, held, into_high, into_low, span_high, span_low, lam, sigma, edge, basis_t, far,
    planes, edges, sent, sums,
):
    count = held.shape[0]
    own = 2 * count
    width, half = held.shape[1:]
    lanes = sigma.shape[1]
    pieces = half // lanes
    planes[:count] = held[...]
    planes[count:] = spectral(
        [arrived[z] for z in range(count)], into_high[...], into_low[...], span_high[0], span_low[0]
    ).reshape(held.shape)
    sums[...] = jnp.zeros_like(sums)
    low = s_ref[1].astype(jnp.float32)
    code = s_ref[2]
    side = width // 16

    def tile(t, nothing):
        group = t // pieces
        rows = pl.ds(pl.multiple_of(group * 8, 8), 8)
        cols = pl.ds(pl.multiple_of(t % pieces * lanes, lanes), lanes)
        parity = group // side
        centre = lam[0, :, cols] + sigma[rows] - 2.0
        mine = continuants(centre, 1.0 - low, own)
        other = continuants(centre, low, own)
        carry = planes[code, rows, cols]
        carries = [carry]
        for i in range(1, own):
            carry = mine[i] * planes[jnp.bitwise_xor(i, code), rows, cols] - carry
            carries.append(carry)
        sent[0, rows, cols] = carry
        shared = carry / (mine[own] * other[own] - mine[own - 1] * other[own - 1])
        scale = edge[rows]
        value = shared * other[own]
        sums[parity, own - 1, :, cols] += scale * value
        for i in range(own - 2, -1, -1):
            value = (carries[i] - mine[i] * value) / mine[i + 1]
            sums[parity, i, :, cols] += scale * value
        sent[1, rows, cols] = value + other[own - 1] * shared / mine[own]
        shared = scale * shared
        for i in range(own):
            term = other[i] * shared
            sums[parity, own + i, :, cols] += term if (own - i) % 2 == 0 else -term
        return nothing

    lax.fori_loop(0, (width // 8) * pieces, tile, 0)
    total = jnp.sum(sums[...], axis=2)
    modal = lambda v: jnp.dot(basis_t[0], v, precision=HIGHEST, preferred_element_type=jnp.float32)
    even = modal(total[0])
    odd = modal(total[1])
    edge_low = even + odd
    edge_high = even - odd
    edges[0] = edge_high + far[0] * edge_low
    edges[1] = edge_low + far[0] * edge_high


def solve_body(
    s_ref, planes, got, gains, span_high, span_low, back_high, back_low, lam, sigma, edge, basis,
    wall, away, keep, solved, both, first,
):
    own, width, half = planes.shape
    count = own // 2
    lanes = sigma.shape[1]
    pieces = half // lanes
    low = s_ref[1].astype(jnp.float32)
    is_low = s_ref[1] == 1
    code = s_ref[2]
    depthwise = lambda v: jnp.dot(basis[0], v, precision=HIGHEST, preferred_element_type=jnp.float32)
    gain_low = depthwise(gains[0])
    gain_high = depthwise(gains[1])
    both[0] = gain_low + gain_high
    both[1] = gain_low - gain_high
    first[...] = jnp.zeros_like(first)
    first[width : width + 1] = jnp.where(is_low, gain_low[own : own + 1], gain_low[:1])
    first[width + 1 : width + 2] = jnp.where(is_low, gain_high[own : own + 1], gain_high[:1])
    side = width // 16

    def tile(t, nothing):
        group = t // pieces
        rows = pl.ds(pl.multiple_of(group * 8, 8), 8)
        cols = pl.ds(pl.multiple_of(t % pieces * lanes, lanes), lanes)
        parity = group // side
        centre = lam[0, :, cols] + sigma[rows] - 2.0
        mine = continuants(centre, 1.0 - low, own)
        other = continuants(centre, low, own)
        scale = edge[rows]
        rhs = lambda i: scale * both[parity, i : i + 1, cols]
        carry = planes[code, rows, cols] - rhs(0)
        carries = [carry]
        for i in range(1, own):
            carry = mine[i] * (planes[jnp.bitwise_xor(i, code), rows, cols] - rhs(i)) - carry
            carries.append(carry)
        right = rhs(own)
        there = -right
        direct = -mine[own - 1] * right
        for i in range(1, own):
            right = rhs(own + i)
            there = -other[i] * right - there
            term = mine[own - 1 - i] * right
            direct = direct - term if i % 2 == 0 else direct + term
        there = there + got[0, rows, cols]
        value = (carry * other[own] - mine[own - 1] * there) / (
            mine[own] * other[own] - mine[own - 1] * other[own - 1]
        )
        far_first = got[1, rows, cols] + (direct + value) / other[own]
        solved[jnp.bitwise_xor(own - 1, code), rows, cols] = value
        for i in range(own - 2, -1, -1):
            value = (carries[i] - mine[i] * value) / mine[i + 1]
            solved[jnp.bitwise_xor(i, code), rows, cols] = value
        first[rows, cols] = jnp.where(is_low, far_first, value)
        return nothing

    lax.fori_loop(0, (width // 8) * pieces, tile, 0)
    table_high = span_high[0]
    table_low = span_low[0]
    line = times_turned(table_high, table_low, first[...])
    main = times(line[:, :width], back_high[:width, :width], back_low[:width, :width])
    wall[...] = jnp.concatenate([main, line[:, width:]], axis=1)
    for pair in range(0, count, 2):
        values = solved[count + pair : count + pair + 2].reshape(2 * width, half)
        cells = times(times_turned(table_high, table_low, values), back_high[...], back_low[...])
        away[pair] = cells[:, :width]
        away[pair + 1] = cells[:, width:]
    keep[...] = solved[:count]


def cells_body(s_ref, keep, span_high, span_low, back_high, back_low, mine):
    count, width, half = keep.shape
    for pair in range(0, count, 2):
        values = keep[pair : pair + 2].reshape(2 * width, half)
        cells = times(times_turned(span_high[0], span_low[0], values), back_high[...], back_low[...])
        mine[pair] = cells[:, :width]
        mine[pair + 1] = cells[:, width:]


def join_body(s_ref, mine, came, out):
    half = mine.shape[1]
    sign = (1 - 2 * s_ref[0]).astype(jnp.float32)
    ours = mine[...]
    theirs = came[...]
    out[:, :half] = ours + theirs
    out[:, half:] = sign * (ours - theirs)


def edge_body(s_ref, temp, phase, conductivity, across, along):
    depth, rows, width = temp.shape
    lane = lax.broadcasted_iota(jnp.int32, (rows, width), 1)
    cold, warm = conductivity[0], conductivity[1]

    def plane(z, packed):
        cond = jnp.where(phase[z] == 1, warm, cold)
        both = (temp[z], cond)
        for k in range(2):
            at = k * depth + z
            packed = jnp.where(lane == at, pltpu.roll(both[k], at + 1, 1), packed)
            at = (2 + k) * depth + z
            packed = jnp.where(lane == at, pltpu.roll(both[k], at, 1), packed)
            place = pl.ds(k * depth + z, 1)
            along[0, place] = both[k][rows - 1 :]
            along[1, place] = both[k][:1]
        return packed

    packed = lax.fori_loop(0, depth, plane, jnp.zeros((rows, width), jnp.float32)).T
    across[0] = packed[: 2 * depth]
    across[1] = packed[2 * depth : 4 * depth]


def faces(value, row, lane, up, down, left, right):
    rows, width = value.shape
    return (
        jnp.where(row == 0, up, pltpu.roll(value, 1, 0)),
        jnp.where(row == rows - 1, down, pltpu.roll(value, rows - 1, 0)),
        jnp.where(lane == 0, left, pltpu.roll(value, 1, 1)),
        jnp.where(lane == width - 1, right, pltpu.roll(value, width - 1, 1)),
    )


def stage_columns(columns, sides, used):
    columns[...] = jnp.zeros_like(columns)
    at = 0
    for side in sides:
        columns[at : at + used] = side[...]
        at += used
    return columns[...].T


def first_body(
    s_ref, temp, phase, gas, conductivity, from_left, from_right, from_up, from_down,
    out, across, along, columns,
):
    depth, rows, width = temp.shape
    row = lax.broadcasted_iota(jnp.int32, (rows, width), 0)
    lane = lax.broadcasted_iota(jnp.int32, (rows, width), 1)
    cold, warm = conductivity[0], conductivity[1]
    halo = stage_columns(columns, (from_left, from_right), 2 * depth)
    conduct = lambda z: jnp.where(phase[z] == 1, warm, cold)

    def plane(z, packed):
        here = temp[z]
        cond = conduct(z)
        near = lambda k: (
            from_up[pl.ds(k * depth + z, 1)],
            from_down[pl.ds(k * depth + z, 1)],
            pltpu.roll(halo, width - (k * depth + z), 1),
            pltpu.roll(halo, width - 1 - ((2 + k) * depth + z), 1),
        )
        total = jnp.zeros_like(here)
        for side_temp, side_cond in zip(
            faces(here, row, lane, *near(0)), faces(cond, row, lane, *near(1))
        ):
            total = total + (cond + side_cond) * (side_temp - here)
        for beside in (jnp.maximum(z - 1, 0), jnp.minimum(z + 1, depth - 1)):
            total = total + (cond + conduct(beside)) * (temp[beside] - here)
        surface = jnp.where(z == 0, STEP_RATE * HEAT_TRANSFER, 0.0) * (gas[...] - temp[0])
        value = here + (0.5 * STEP_RATE) * total + surface
        out[z] = value
        packed = jnp.where(lane == z, pltpu.roll(value, z + 1, 1), packed)
        packed = jnp.where(lane == depth + z, pltpu.roll(value, depth + z, 1), packed)
        along[0, pl.ds(z, 1)] = value[rows - 1 :]
        along[1, pl.ds(z, 1)] = value[:1]
        return packed

    packed = lax.fori_loop(0, depth, plane, jnp.zeros((rows, width), jnp.float32)).T
    across[0] = packed[:depth]
    across[1] = packed[depth : 2 * depth]


def second_body(
    s_ref, base, temp, phase, gas, conductivity, from_left, from_right, from_up, from_down,
    base_left, base_right, base_up, base_down, out, weights, columns,
):
    depth, rows, width = base.shape
    row = lax.broadcasted_iota(jnp.int32, (rows, width), 0)
    lane = lax.broadcasted_iota(jnp.int32, (rows, width), 1)
    cold, warm = conductivity[0], conductivity[1]
    halo = stage_columns(columns, (from_left, from_right), 2 * depth)
    base_halo = stage_columns(columns, (base_left, base_right), depth)
    conduct = lambda z: jnp.where(phase[z] == 1, warm, cold)

    def plane(z, nothing):
        here = base[z]
        cond = conduct(z)
        near_base = (
            base_up[pl.ds(z, 1)],
            base_down[pl.ds(z, 1)],
            pltpu.roll(base_halo, width - z, 1),
            pltpu.roll(base_halo, width - 1 - (depth + z), 1),
        )
        near_cond = (
            from_up[pl.ds(depth + z, 1)],
            from_down[pl.ds(depth + z, 1)],
            pltpu.roll(halo, width - (depth + z), 1),
            pltpu.roll(halo, width - 1 - (3 * depth + z), 1),
        )
        total = jnp.zeros_like(here)
        pairs = []
        for side_base, side_cond in zip(
            faces(here, row, lane, *near_base), faces(cond, row, lane, *near_cond)
        ):
            pair = cond + side_cond
            pairs.append(pair)
            total = total + pair * (side_base - here)
        for beside in (jnp.maximum(z - 1, 0), jnp.minimum(z + 1, depth - 1)):
            pair = cond + conduct(beside)
            total = total + pair * (base[beside] - here)
        pairs.append(pair)
        surface = jnp.where(z == 0, STEP_RATE * HEAT_TRANSFER, 0.0) * (gas[...] - temp[0])
        out[z] = here + (0.5 * STEP_RATE) * total + surface

        @pl.when(z == 0)
        def _():
            for k in range(5):
                weights[k] = (0.5 * STEP_RATE) * pairs[k]

        return nothing

    lax.fori_loop(0, depth, plane, 0)


def wall_body(s_ref, ours, theirs, weights, base, out):
    half = ours.shape[0]
    rows, width = weights.shape[1:]
    sign = (1 - 2 * s_ref[0]).astype(jnp.float32)
    bottom = (1 - 2 * s_ref[3]).astype(jnp.float32)
    second = s_ref[4] == 1
    factor = STEP_RATE * HEAT_TRANSFER * PRESSURE_WORK

    def lines(start, count, minus):
        our_sign = jnp.where(s_ref[0] == 0, 1.0, minus) * factor
        their_sign = jnp.where(s_ref[0] == 0, minus, 1.0) * factor
        at = pl.ds(start, count)
        return our_sign * ours[at] + their_sign * theirs[at]

    begin = pl.multiple_of(s_ref[4] * rows, rows)
    middle = lines(begin, rows, bottom)
    above = lines(jnp.where(second, rows - 1, half - 1), 1, jnp.where(second, bottom, -bottom))
    below = lines(jnp.where(second, 0, rows), 1, jnp.where(second, -bottom, bottom))
    share = middle[:, :width]
    row = lax.broadcasted_iota(jnp.int32, (rows, width), 0)
    lane = lax.broadcasted_iota(jnp.int32, (rows, width), 1)
    around = faces(
        share, row, lane, above[:, :width], below[:, :width],
        middle[:, width : width + 1], middle[:, width + 1 : width + 2],
    )
    added = 2.0 * share
    for k in range(4):
        added = added + weights[k] * (around[k] - share)
    down = weights[4] * share
    out[0] = base[0] + added - down
    out[1] = base[1] + down


def mover(groups, pencils):
    def move(value, target):
        pairs = []
        for g in range(groups):
            for p in range(pencils):
                to = target(g, p)
                pairs.append((g * pencils + p, to[0] * pencils + to[1]))
        return lax.ppermute(value, ("grp", "pen"), pairs)

    return move


def per_device(pressure_source, solid_temp, gas_wall_temp, phase_map, phase_conductivity):
    groups = lax.axis_size("grp")
    pencils = lax.axis_size("pen")
    group_idx = lax.axis_index("grp")
    pencil_idx = lax.axis_index("pen")
    depth_loc, span_len, width = pressure_source.shape
    depth = depth_loc * groups
    half = span_len // 2
    own = depth // 2
    core = group_idx % 2
    low = group_idx // 2
    zi = pencil_idx % Z_RING
    yl = pencil_idx // Z_RING % Y_PAIR
    place = pencil_idx % (Z_RING * Y_PAIR)
    move = mover(groups, pencils)
    tab = make_tables(span_len, width, depth)
    const = {k: tuple(map(jnp.asarray, v)) if isinstance(v, tuple) else jnp.asarray(v) for k, v in tab.items()}
    code = jnp.where(low == 0, core * 4, 7 - 4 * core)
    scalars = jnp.stack([core, low, code, low, core]).astype(jnp.int32)
    span = list(const["span"])
    into = list(const["into"])
    back = list(const["back"])
    span_specs = [chosen(a, 0) for a in span]
    into_specs = [whole(a) for a in into]
    back_specs = [whole(a) for a in back]
    strip = [const["lam"], const["sigma"], const["edge"]]
    strip_specs = [chosen(strip[0], 0), whole(strip[1]), whole(strip[2])]
    smem = pl.BlockSpec(memory_space=pltpu.SMEM)

    tile_rows = span_len // groups
    right_on = lambda g, p: (g, (p + 1) % pencils)
    left_on = lambda g, p: (g, (p - 1) % pencils)
    down_on = lambda g, p: ((g + 1) % groups, p)
    up_on = lambda g, p: ((g - 1) % groups, p)

    def exchange(across, along):
        return [
            move(across[0], right_on), move(across[1], left_on),
            move(along[0], down_on), move(along[1], up_on),
        ]

    other_core = lambda g, p: (g ^ 1, p)
    other_half = lambda g, p: (g ^ 2, p)
    sign = jnp.where(core == 0, 1.0, -1.0).astype(jnp.float32)
    arrived = move(pressure_source[:, :half] - sign * pressure_source[:, half:], other_core)
    spectral_flops = 6 * depth_loc * width * half * (half + width)
    (held,) = run(
        held_body, scalars, [pressure_source, *into, *span],
        [whole(pressure_source), *into_specs, *span_specs],
        [(depth_loc, width, half)], flops=spectral_flops,
    )
    planes, edges, sent = run(
        arrived_body, scalars,
        [arrived, held, *into, *span, *strip, const["basis_t"], const["far"]],
        [whole(arrived), whole(held), *into_specs, *span_specs, *strip_specs,
         chosen(const["basis_t"], 1), chosen(const["far"], 0)],
        [(own, width, half), (2, depth, half), (2, width, half)],
        scratch=[pltpu.VMEM((2, depth, 8, half), jnp.float32)], flops=spectral_flops,
    )
    sent = move(sent, other_half)

    solid = [solid_temp, phase_map]
    solid_specs = [whole(solid_temp), whole(phase_map)]
    across, along = run(
        edge_body, scalars, [*solid, phase_conductivity], [*solid_specs, smem],
        [(2, 2 * depth, tile_rows), (2, 2 * depth, width)], flops=10**8,
    )
    near = exchange(across, along)
    near_specs = [whole(a) for a in near]
    column_scratch = [pltpu.VMEM((width, tile_rows), jnp.float32)]
    base, across, along = run(
        first_body, scalars, [*solid, gas_wall_temp, phase_conductivity, *near],
        [*solid_specs, whole(gas_wall_temp), smem, *near_specs],
        [(depth, tile_rows, width), (2, depth, tile_rows), (2, depth, width)],
        scratch=column_scratch, flops=10**9,
    )
    near_base = exchange(across, along)
    first_plane = pl.BlockSpec((1, tile_rows, width), lambda i, s: (0, 0, 0))
    base, weights = run(
        second_body, scalars,
        [base, solid_temp, phase_map, gas_wall_temp, phase_conductivity, *near, *near_base],
        [whole(base), first_plane, solid_specs[1], whole(gas_wall_temp), smem, *near_specs,
         *[whole(a) for a in near_base]],
        [(depth, tile_rows, width), (5, tile_rows, width)],
        scratch=column_scratch, flops=10**9,
    )

    log_rho = const["log_rho"][core]
    power = lambda n: jnp.exp(log_rho * n)
    wide = float(width)
    hop = power(wide)
    rho = power(1.0)
    per_rho = power(-1.0)
    right, left = edges[0], edges[1]

    low_sum = jnp.zeros_like(right)
    high_sum = jnp.zeros_like(right)
    right4 = power(wide * (Z_RING - 1 - zi)) * right
    left4 = power(wide * zi) * left
    for d in range(1, Z_RING):
        got = move(edges, lambda g, p, d=d: (g, p // Z_RING * Z_RING + (p + d) % Z_RING))
        source = (zi - d) % Z_RING
        before = zi >= d
        low_sum = low_sum + jnp.where(before, power(wide * (d - 1)), 0.0) * got[0]
        high_sum = high_sum + jnp.where(before, 0.0, power(wide * (Z_RING - 1 - d))) * got[1]
        right4 = right4 + power(wide * (Z_RING - 1 - source)) * got[0]
        left4 = left4 + power(wide * source) * got[1]
    into_low = per_rho * low_sum + left + hop * high_sum
    into_high = per_rho * high_sum + right + hop * low_sum

    first = move(jnp.stack([into_low, into_high, right4, left4]), other_half)
    group4 = jnp.stack([right4, left4])
    other = move(group4, lambda g, p: (g, p ^ Z_RING)) + move(group4, lambda g, p: (g ^ 2, p ^ Z_RING))
    into_low = into_low + first[0]
    into_high = into_high + first[1]
    right4 = right4 + first[2]
    left4 = left4 + first[3]
    after = yl == 1
    low_sum = jnp.where(after, power(wide * zi), 0.0) * other[0]
    high_sum = jnp.where(after, 0.0, power(wide * (Z_RING - 1 - zi))) * other[1]
    run4 = power(wide * Z_RING)
    right8 = jnp.where(after, run4 * other[0] + right4, run4 * right4 + other[0])
    left8 = jnp.where(after, other[1] + run4 * left4, left4 + run4 * other[1])

    packed = jnp.stack([right8, left8])
    block = Z_RING * Y_PAIR
    right_sum = power(wide * block * (X_RING - 1)) * right8
    left_sum = power(wide * block * (X_RING - 1)) * left8
    for d in range(1, X_RING):
        got = move(packed, lambda g, p, d=d: (g, (p + block * d) % pencils))
        right_sum = right_sum + power(wide * block * (d - 1)) * got[0]
        left_sum = left_sum + power(wide * block * (X_RING - 1 - d)) * got[1]
    periodic = 1.0 / (1.0 - power(wide * block * X_RING))
    low_sum = low_sum + power(wide * place) * right_sum * periodic
    high_sum = high_sum + power(wide * (block - 1 - place)) * left_sum * periodic
    gain = rho / (1.0 - rho * rho)
    into_low = gain * (into_low + per_rho * low_sum + hop * high_sum)
    into_high = gain * (into_high + per_rho * high_sum + hop * low_sum)
    gains = jnp.stack([into_low, into_high])

    wall, away, keep = run(
        solve_body, scalars,
        [planes, sent, gains, *span, *back, *strip, const["basis"]],
        [whole(planes), whole(sent), whole(gains), *span_specs, *back_specs, *strip_specs,
         chosen(const["basis"], 1)],
        [(half, 2 * width), (depth_loc, half, width), (depth_loc, width, half)],
        scratch=[
            pltpu.VMEM((own, width, half), jnp.float32),
            pltpu.VMEM((2, depth, half), jnp.float32),
            pltpu.VMEM((2 * width, half), jnp.float32),
        ],
        flops=spectral_flops,
    )
    wall_came = move(wall, other_core)
    came = move(away, other_core)
    (mine,) = run(
        cells_body, scalars, [keep, *span, *back], [whole(keep), *span_specs, *back_specs],
        [(depth_loc, half, width)], flops=spectral_flops,
    )
    (pressure,) = run(
        join_body, scalars, [mine, came], [whole(mine), whole(came)], [pressure_source.shape]
    )
    top_planes = pl.BlockSpec((2, tile_rows, width), lambda i, s: (0, 0, 0))
    (final,) = run(
        wall_body, scalars, [wall, wall_came, weights, base],
        [whole(wall), whole(wall_came), whole(weights), top_planes],
        [solid_temp.shape], out_specs=[top_planes], aliases={4: 0},
    )
    return (pressure, final)


def solution(mesh):
    in_specs = (
        P("grp", None, "pen"),
        P(None, "grp", "pen"),
        P("grp", "pen"),
        P(None, "grp", "pen"),
        P(),
    )
    out_specs = (P("grp", None, "pen"), P(None, "grp", "pen"))
    return jax.shard_map(
        per_device, mesh=mesh, in_specs=in_specs, out_specs=out_specs, check_vma=False
    )
```

profile of v0, /device:TPU:1, one launch (start us, length us, event | category | flops | bytes accessed | tf_op | source)
XLA Modules:
  0.0 129.7 jit_solution(1982114944174100852)
XLA Ops:
  0.6 0.0 copy-start.2
  0.6 0.0 copy-start.3
  0.7 0.0 copy-start.11
  0.7 2.8 %multiply_subtract_fusion = f32[4,512,128]{2,1,0:T(8,128)} fusion(f32[4,1024,128]{2,1,0:T(8,128)} %source.1, f32[]{:T(128)S(6)} %select_n.139), kind=kLoop, calls=%fused_computation | loop fusion | flops 524288 | bytes 3145732 | tf_op jit(solution)/shard_map/sub | solution.py:508
  3.5 1.4 %collective-permute-start = (f32[4,512,128]{2,1,0:T(8,128)}, f32[4,512,128]{2,1,0:T(8,128)}, u32[]{:S(2)}, u32[]{:S(2)}) collective-permute-start(f32[4,512,128]{2,1,0:T(8,128)} %multiply_subtract_fusion), channel_id=1, source_target_pairs={{0,32},{1,33},{2,34},{3,35},{4,36},{5,37},{6,38},{7,39},{8,40},{9,... | collective-permute-start | bytes 3145736 | tf_op jit(solution)/shard_map/ppermute | solution.py:459
  4.9 0.1 stack.19.s_ref
  5.0 1.6 %copy-done.5 = f32[4,1024,128]{2,1,0:T(8,128)S(1)} copy-done((f32[4,1024,128]{2,1,0:T(8,128)S(1)}, f32[4,1024,128]{2,1,0:T(8,128)}, u32[]{:S(2)}) %copy-start.5) | copy-done | bytes 2097176
  6.6 0.9 copy-done.12
  7.5 0.0 copy-start.16
  7.5 0.0 copy-start.17
  7.5 2.1 %shard_map.185.held = f32[4,128,512]{2,1,0:T(8,128)S(1)} custom-call(s32[5]{0:T(128)S(1)} %stack.19.s_ref, f32[4,1024,128]{2,1,0:T(8,128)S(1)} %copy-done.5, bf16[256,256]{1,0:T(8,128)(2,1)S(1)} %copy-done.11, bf16[256,256]{1,0:T(8,128)(2,1)S(1)} %copy-done.12, bf16[2,512,512]{2,1,0:T(8,128)(2,1)S(1)} %copy-done.2, bf16[2,512,512]{2,1,0:T(8,128)(2,1)S(1)} %copy-done.3), custom_call_target="tpu_custom_call" | custom-call | flops 1006632960 | bytes 7864320 | tf_op jit(solution)/shard_map/pallas_call | solution.py:98
  9.6 0.0 copy-start.21
  9.6 0.0 collective-permute-done.arrived
  9.7 6.6 %shard_map.186 = (f32[8,128,512]{2,1,0:T(8,128)}, f32[2,16,512]{2,1,0:T(8,128)}, f32[2,128,512]{2,1,0:T(8,128)S(1)}) custom-call(s32[5]{0:T(128)S(1)} %stack.19.s_ref, f32[4,512,128]{2,1,0:T(8,128)} %collective-permute-done.arrived, f32[4,128,512]{2,1,0:T(8,128)S(1)} %shard_map.185.held, bf16[256,256]{1,0:T(8,128)(2,1)S(1)} %copy-done.11, ...), custom_call_target="tpu_custom_call" | custom-call | flops 1006632960 | bytes 9836544 | tf_op jit(solution)/shard_map/pallas_call | solution.py:98
  16.3 0.8 copy-done.19
  17.1 1.7 %collective-permute-start.2 = (f32[2,16,512]{2,1,0:T(8,128)}, f32[2,16,512]{2,1,0:T(8,128)S(1)}, u32[]{:S(2)}, u32[]{:S(2)}) collective-permute-start(f32[2,16,512]{2,1,0:T(8,128)} %get-tuple-element.17), channel_id=1, source_target_pairs={{0,1},{1,2},{2,3},{3,0},{4,5},{5,6},{6,7},{7,4},{8,9},{9,10},{10,1... | collective-permute-start | bytes 196616 | tf_op jit(solution)/shard_map/ppermute | solution.py:459
  18.8 3.3 %collective-permute-start.3 = (f32[2,16,512]{2,1,0:T(8,128)}, f32[2,16,512]{2,1,0:T(8,128)}, u32[]{:S(2)}, u32[]{:S(2)}) collective-permute-start(f32[2,16,512]{2,1,0:T(8,128)} %get-tuple-element.17), channel_id=1, source_target_pairs={{0,2},{1,3},{2,0},{3,1},{4,6},{5,7},{6,4},{7,5},{8,10},{9,11},{10,... | collective-permute-start | bytes 196616 | tf_op jit(solution)/shard_map/ppermute | solution.py:459
  22.1 0.7 collective-permute-start.4
  22.9 0.8 collective-permute-done.2
  23.6 2.5 %collective-permute-done.3 = f32[2,16,512]{2,1,0:T(8,128)} collective-permute-done((f32[2,16,512]{2,1,0:T(8,128)}, f32[2,16,512]{2,1,0:T(8,128)}, u32[]{:S(2)}, u32[]{:S(2)}) %collective-permute-start.3) | collective-permute-done | bytes 65568 | tf_op jit(solution)/shard_map/ppermute | solution.py:459
  26.1 0.0 collective-permute-done.4
  26.1 0.9 fusion.9
  27.0 0.8 fusion.11
  27.8 0.9 fusion.58
  28.7 0.7 pad_maximum_fusion
  29.4 2.9 %collective-permute-start.5 = (f32[4,16,512]{2,1,0:T(8,128)}, f32[4,16,512]{2,1,0:T(8,128)}, u32[]{:S(2)}, u32[]{:S(2)}) collective-permute-start(f32[4,16,512]{2,1,0:T(8,128)} %pad_maximum_fusion), channel_id=1, source_target_pairs={{0,64},{1,65},{2,66},{3,67},{4,68},{5,69},{6,70},{7,71},{8,72},{9,... | collective-permute-start | bytes 393224 | tf_op jit(solution)/shard_map/ppermute | solution.py:459
  32.3 0.6 pad_maximum_fusion.1
  33.0 0.4 collective-permute-start.6
  33.4 0.4 collective-permute-start.7
  33.8 3.6 %collective-permute-done.6 = f32[2,16,512]{2,1,0:T(8,128)S(1)} collective-permute-done((f32[2,16,512]{2,1,0:T(8,128)}, f32[2,16,512]{2,1,0:T(8,128)S(1)}, u32[]{:S(2)}, u32[]{:S(2)}) %collective-permute-start.6) | collective-permute-done | bytes 65568 | tf_op jit(solution)/shard_map/ppermute | solution.py:459
  37.4 0.6 copy-done.32
  38.0 0.9 add.245
  38.9 0.8 fusion.91
  39.8 0.6 copy-done.24
  40.4 0.6 pad_maximum_fusion.2
  41.0 2.5 %collective-permute-start.10 = (f32[2,16,512]{2,1,0:T(8,128)}, f32[2,16,512]{2,1,0:T(8,128)}, u32[]{:S(2)}, u32[]{:S(2)}) collective-permute-start(f32[2,16,512]{2,1,0:T(8,128)} %pad_maximum_fusion.2), channel_id=1, source_target_pairs={{0,24},{1,25},{2,26},{3,27},{4,28},{5,29},{6,30},{7,31},{8,0},{9,1... | collective-permute-start | bytes 196616 | tf_op jit(solution)/shard_map/ppermute | solution.py:459
  43.5 1.7 %collective-permute-start.9 = (f32[2,16,512]{2,1,0:T(8,128)}, f32[2,16,512]{2,1,0:T(8,128)}, u32[]{:S(2)}, u32[]{:S(2)}) collective-permute-start(f32[2,16,512]{2,1,0:T(8,128)} %pad_maximum_fusion.2), channel_id=1, source_target_pairs={{0,16},{1,17},{2,18},{3,19},{4,20},{5,21},{6,22},{7,23},{8,24},{9,... | collective-permute-start | bytes 196616 | tf_op jit(solution)/shard_map/ppermute | solution.py:459
  45.2 1.6 %copy-done.1 = s32[16,256,128]{2,1,0:T(8,128)S(1)} copy-done((s32[16,256,128]{2,1,0:T(8,128)S(1)}, s32[16,256,128]{2,1,0:T(8,128)}, u32[]{:S(2)}) %copy-start.1) | copy-done | bytes 2097176
  46.9 0.0 copy-start.4
  46.9 0.0 copy-start.7
  46.9 0.0 copy-start.8
  46.9 0.0 copy-start.15
  46.9 4.4 %shard_map.190 = (f32[2,32,256]{2,1,0:T(8,128)S(1)}, f32[2,32,128]{2,1,0:T(8,128)S(1)}) custom-call(s32[5]{0:T(128)S(1)} %stack.19.s_ref, f32[16,256,128]{2,1,0:T(8,128)S(1)} %copy-done, s32[16,256,128]{2,1,0:T(8,128)S(1)} %copy-done.1, f32[2]{0:T(128)S(1)} %copy-done.18), custom_call_target="tpu_custom_call" | custom-call | flops 100000000 | bytes 4292616 | tf_op jit(solution)/shard_map/pallas_call | solution.py:98
  51.4 1.4 %collective-permute-start.1 = (f32[2,128,512]{2,1,0:T(8,128)S(1)}, f32[2,128,512]{2,1,0:T(8,128)S(1)}, u32[]{:S(2)}, u32[]{:S(2)}) collective-permute-start(f32[2,128,512]{2,1,0:T(8,128)S(1)} %copy-done.20), channel_id=1, source_target_pairs={{0,64},{1,65},{2,66},{3,67},{4,68},{5,69},{6,70},{7,71},{8,72},{9,... | collective-permute-start | bytes 1572872 | tf_op jit(solution)/shard_map/ppermute | solution.py:459
  52.8 1.0 fusion.14
  53.8 0.8 fusion.17
  54.6 8.0 %collective-permute-done.1.got = f32[2,128,512]{2,1,0:T(8,128)S(1)} collective-permute-done((f32[2,128,512]{2,1,0:T(8,128)S(1)}, f32[2,128,512]{2,1,0:T(8,128)S(1)}, u32[]{:S(2)}, u32[]{:S(2)}) %collective-permute-start.1) | collective-permute-done | bytes 524320 | tf_op jit(solution)/shard_map/ppermute | solution.py:459
  62.7 0.0 copy-start.6
  62.7 8.0 %shard_map.187 = (f32[512,256]{1,0:T(8,128)S(1)}, f32[4,512,128]{2,1,0:T(8,128)S(1)}, f32[4,128,512]{2,1,0:T(8,128)S(1)}) custom-call(s32[5]{0:T(128)S(1)} %stack.19.s_ref, f32[8,128,512]{2,1,0:T(8,128)} %get-tuple-element.15.planes, f32[2,128,512]{2,1,0:T(8,128)S(1)} %collective-permute-done.1.got, f32[2,16,512]{2,1,0:T(8,128)S(1)} %pad_maximum_fusion.3.gains, ...), custom_call_target="tpu_custom_call" | custom-call | flops 1006632960 | bytes 10295296 | tf_op jit(solution)/shard_map/pallas_call | solution.py:98
  70.7 4.7 %collective-permute-start.11 = (f32[4,512,128]{2,1,0:T(8,128)S(1)}, f32[4,512,128]{2,1,0:T(8,128)S(1)}, u32[]{:S(2)}, u32[]{:S(2)}) collective-permute-start(f32[4,512,128]{2,1,0:T(8,128)S(1)} %get-tuple-element.19), channel_id=1, source_target_pairs={{0,32},{1,33},{2,34},{3,35},{4,36},{5,37},{6,38},{7,39},{8,40},{9,... | collective-permute-start | bytes 3145736 | tf_op jit(solution)/shard_map/ppermute | solution.py:459
  75.4 0.5 collective-permute-start.13
  75.9 5.2 %collective-permute-start.14 = (f32[32,256]{1,0:T(8,128)S(1)}, f32[32,256]{1,0:T(8,128)S(1)}, u32[]{:S(2)}, u32[]{:S(2)}) collective-permute-start(f32[32,256]{1,0:T(8,128)S(1)} %get-tuple-element.38), channel_id=1, source_target_pairs={{0,31},{1,0},{2,1},{3,2},{4,3},{5,4},{6,5},{7,6},{8,7},{9,8},{10,9... | collective-permute-start | bytes 98312 | tf_op jit(solution)/shard_map/ppermute | solution.py:459
  81.1 1.9 %collective-permute-start.15 = (f32[32,128]{1,0:T(8,128)S(1)}, f32[32,128]{1,0:T(8,128)S(1)}, u32[]{:S(2)}, u32[]{:S(2)}) collective-permute-start(f32[32,128]{1,0:T(8,128)S(1)} %get-tuple-element.43), channel_id=1, source_target_pairs={{0,32},{1,33},{2,34},{3,35},{4,36},{5,37},{6,38},{7,39},{8,40},{9,... | collective-permute-start | bytes 49160 | tf_op jit(solution)/shard_map/ppermute | solution.py:459
  83.0 0.9 collective-permute-done.15.from_up
  83.8 3.8 %collective-permute-done.16.from_down = f32[32,128]{1,0:T(8,128)S(1)} collective-permute-done((f32[32,128]{1,0:T(8,128)S(1)}, f32[32,128]{1,0:T(8,128)S(1)}, u32[]{:S(2)}, u32[]{:S(2)}) %collective-permute-start.16) | collective-permute-done | bytes 16416 | tf_op jit(solution)/shard_map/ppermute | solution.py:459
  87.6 11.1 %shard_map.191 = (f32[16,256,128]{2,1,0:T(8,128)S(1)}, f32[2,16,256]{2,1,0:T(8,128)S(1)}, f32[2,16,128]{2,1,0:T(8,128)S(1)}) custom-call(s32[5]{0:T(128)S(1)} %stack.19.s_ref, f32[16,256,128]{2,1,0:T(8,128)S(1)} %copy-done, s32[16,256,128]{2,1,0:T(8,128)} %phase.5, f32[256,128]{1,0:T(8,128)S(1)} %copy-done.6, f32[2]{0:T(128)S(1)} %copy-done.18, ...), custom_call_target="tpu_custom_call" | custom-call | flops 1000000000 | bytes 6569992 | tf_op jit(solution)/shard_map/pallas_call | solution.py:98
  98.8 0.1 collective-permute-start.12
  98.9 2.0 %collective-permute-start.19 = (f32[16,128]{1,0:T(8,128)S(1)}, f32[16,128]{1,0:T(8,128)S(1)}, u32[]{:S(2)}, u32[]{:S(2)}) collective-permute-start(f32[16,128]{1,0:T(8,128)S(1)} %get-tuple-element.45), channel_id=1, source_target_pairs={{0,32},{1,33},{2,34},{3,35},{4,36},{5,37},{6,38},{7,39},{8,40},{9,... | collective-permute-start | bytes 24584 | tf_op jit(solution)/shard_map/ppermute | solution.py:459
  100.8 5.7 %collective-permute-start.18 = (f32[16,256]{1,0:T(8,128)S(1)}, f32[16,256]{1,0:T(8,128)S(1)}, u32[]{:S(2)}, u32[]{:S(2)}) collective-permute-start(f32[16,256]{1,0:T(8,128)S(1)} %get-tuple-element.40), channel_id=1, source_target_pairs={{0,31},{1,0},{2,1},{3,2},{4,3},{5,4},{6,5},{7,6},{8,7},{9,8},{10,9... | collective-permute-start | bytes 49160 | tf_op jit(solution)/shard_map/ppermute | solution.py:459
  106.5 4.6 %collective-permute-done.20.base_down = f32[16,128]{1,0:T(8,128)S(1)} collective-permute-done((f32[16,128]{1,0:T(8,128)S(1)}, f32[16,128]{1,0:T(8,128)S(1)}, u32[]{:S(2)}, u32[]{:S(2)}) %collective-permute-start.20) | collective-permute-done | bytes 8224 | tf_op jit(solution)/shard_map/ppermute | solution.py:459
  111.1 10.9 %shard_map.192 = (f32[16,256,128]{2,1,0:T(8,128)}, f32[5,256,128]{2,1,0:T(8,128)S(1)}) custom-call(s32[5]{0:T(128)S(1)} %stack.19.s_ref, f32[16,256,128]{2,1,0:T(8,128)S(1)} %get-tuple-element.23.base, f32[16,256,128]{2,1,0:T(8,128)S(1)} %copy-done, s32[16,256,128]{2,1,0:T(8,128)} %phase.5, f32[256,128]{1,0:T(8,128)S(1)} %copy-done.6, f32[2]{0:T(128)S(1)} %copy-done.18, ...), custom_call_target="tpu_custom_call" | custom-call | flops 1000000000 | bytes 9322504 | tf_op jit(solution)/shard_map/pallas_call | solution.py:98
  122.0 3.1 %shard_map.188.mine = f32[4,512,128]{2,1,0:T(8,128)S(1)} custom-call(s32[5]{0:T(128)S(1)} %stack.19.s_ref, f32[4,128,512]{2,1,0:T(8,128)S(1)} %get-tuple-element.18.keep, bf16[2,512,512]{2,1,0:T(8,128)(2,1)S(1)} %copy-done.2, bf16[2,512,512]{2,1,0:T(8,128)(2,1)S(1)} %copy-done.4, bf16[256,256]{1,0:T(8,128)(2,1)S(1)} %copy-done.7, bf16[256,256]{1,0:T(8,128)(2,1)S(1)} %copy-done.8), custom_call_target="tpu_custom_call" | custom-call | flops 1006632960 | bytes 6815744 | tf_op jit(solution)/shard_map/pallas_call | solution.py:98
  125.2 2.4 %shard_map.193 = f32[16,256,128]{2,1,0:T(8,128)} custom-call(s32[5]{0:T(128)S(1)} %stack.19.s_ref, f32[512,256]{1,0:T(8,128)S(1)} %get-tuple-element.20.ours, f32[512,256]{1,0:T(8,128)S(1)} %collective-permute-done.12.theirs, f32[5,256,128]{2,1,0:T(8,128)S(1)} %get-tuple-element.26.weights, ...), custom_call_target="tpu_custom_call", output_to_operand_aliasing={{}: (4, {})} | custom-call | bytes 5898240 | tf_op jit(solution)/shard_map/pallas_call | solution.py:98
  127.6 2.1 %shard_map.189 = f32[4,1024,128]{2,1,0:T(8,128)} custom-call(s32[5]{0:T(128)S(1)} %stack.19.s_ref, f32[4,512,128]{2,1,0:T(8,128)S(1)} %shard_map.188.mine, f32[4,512,128]{2,1,0:T(8,128)S(1)} %collective-permute-done.11.came), custom_call_target="tpu_custom_call" | custom-call | bytes 4194304 | tf_op jit(solution)/shard_map/pallas_call | solution.py:98
  (70 shorter events, 0.2 us)
Async XLA Ops:
  0.6 4.3 %copy-start.2 = (bf16[2,512,512]{2,1,0:T(8,128)(2,1)S(1)}, bf16[2,512,512]{2,1,0:T(8,128)(2,1)}, u32[]{:S(2)}) copy-start(bf16[2,512,512]{2,1,0:T(8,128)(2,1)} %constant.136.clone.span_high) | copy-start | bytes 3145732
  0.6 4.3 %copy-start.3 = (bf16[2,512,512]{2,1,0:T(8,128)(2,1)S(1)}, bf16[2,512,512]{2,1,0:T(8,128)(2,1)}, u32[]{:S(2)}) copy-start(bf16[2,512,512]{2,1,0:T(8,128)(2,1)} %constant.137.clone.span_low) | copy-start | bytes 3145732
  0.7 4.3 %copy-start.11 = (bf16[256,256]{1,0:T(8,128)(2,1)S(1)}, bf16[256,256]{1,0:T(8,128)(2,1)}, u32[]{:S(2)}) copy-start(bf16[256,256]{1,0:T(8,128)(2,1)} %constant.138.clone.into_high) | copy-start | bytes 393220
  3.5 6.2 %collective-permute-start = (f32[4,512,128]{2,1,0:T(8,128)}, f32[4,512,128]{2,1,0:T(8,128)}, u32[]{:S(2)}, u32[]{:S(2)}) collective-permute-start(f32[4,512,128]{2,1,0:T(8,128)} %multiply_subtract_fusion), channel_id=1, source_target_pairs={{0,32},{1,33},{2,34},{3,35},{4,36},{5,37},{6,38},{7,39},{8,40},{9,... | collective-permute-start | bytes 3145736 | tf_op jit(solution)/shard_map/ppermute | solution.py:459
  5.0 1.6 %copy-start.5 = (f32[4,1024,128]{2,1,0:T(8,128)S(1)}, f32[4,1024,128]{2,1,0:T(8,128)}, u32[]{:S(2)}) copy-start(f32[4,1024,128]{2,1,0:T(8,128)} %source.1) | copy-start | bytes 6291460
  6.6 0.9 copy-start.12
  7.5 2.2 %copy-start.9 = (f32[128,256]{1,0:T(8,128)S(1)}, f32[128,256]{1,0:T(8,128)}, u32[]{:S(2)}) copy-start(f32[128,256]{1,0:T(8,128)} %constant.143.clone.sigma) | copy-start | bytes 393220
  7.5 2.2 %copy-start.10 = (f32[128,256]{1,0:T(8,128)S(1)}, f32[128,256]{1,0:T(8,128)}, u32[]{:S(2)}) copy-start(f32[128,256]{1,0:T(8,128)} %constant.144.clone.edge) | copy-start | bytes 393220
  7.5 2.2 %copy-start.13 = (bf16[256,256]{1,0:T(8,128)(2,1)S(1)}, bf16[256,256]{1,0:T(8,128)(2,1)}, u32[]{:S(2)}) copy-start(bf16[256,256]{1,0:T(8,128)(2,1)} %constant.139.clone.into_low) | copy-start | bytes 393220
  7.5 2.2 %copy-start.14 = (f32[2,16,512]{2,1,0:T(8,128)S(1)}, f32[2,16,512]{2,1,0:T(8,128)}, u32[]{:S(2)}) copy-start(f32[2,16,512]{2,1,0:T(8,128)} %constant.148.clone.far) | copy-start | bytes 196612
  7.5 2.2 %copy-start.16 = (f32[2,16,16]{2,1,0:T(8,128)S(1)}, f32[2,16,16]{2,1,0:T(8,128)}, u32[]{:S(2)}) copy-start(f32[2,16,16]{2,1,0:T(8,128)} %constant.146.clone.basis_t) | copy-start | bytes 6148
  7.5 2.2 %copy-start.17 = (f32[2,1,512]{2,1,0:T(1,128)S(1)}, f32[2,1,512]{2,1,0:T(1,128)}, u32[]{:S(2)}) copy-start(f32[2,1,512]{2,1,0:T(1,128)} %constant.142.clone.lam) | copy-start | bytes 12292
  9.6 16.5 %copy-start.21 = (f32[2,16,512]{2,1,0:T(8,128)S(1)}, f32[2,16,512]{2,1,0:T(8,128)}, u32[]{:S(2)}) copy-start(f32[2,16,512]{2,1,0:T(8,128)} %constant.147.clone) | copy-start | bytes 196612
  16.3 0.8 copy-start.19
  17.1 28.1 %copy-start = (f32[16,256,128]{2,1,0:T(8,128)S(1)}, f32[16,256,128]{2,1,0:T(8,128)}, u32[]{:S(2)}) copy-start(f32[16,256,128]{2,1,0:T(8,128)} %temp.5) | copy-start | bytes 6291460
  17.1 28.1 %copy-start.18 = (f32[2]{0:T(128)S(1)}, f32[2]{0:T(128)}, u32[]{:S(2)}) copy-start(f32[2]{0:T(128)} %conductivity.5) | copy-start | bytes 28
  17.1 6.5 %collective-permute-start.2 = (f32[2,16,512]{2,1,0:T(8,128)}, f32[2,16,512]{2,1,0:T(8,128)S(1)}, u32[]{:S(2)}, u32[]{:S(2)}) collective-permute-start(f32[2,16,512]{2,1,0:T(8,128)} %get-tuple-element.17), channel_id=1, source_target_pairs={{0,1},{1,2},{2,3},{3,0},{4,5},{5,6},{6,7},{7,4},{8,9},{9,10},{10,1... | collective-permute-start | bytes 196616 | tf_op jit(solution)/shard_map/ppermute | solution.py:459
  18.8 7.3 %collective-permute-start.3 = (f32[2,16,512]{2,1,0:T(8,128)}, f32[2,16,512]{2,1,0:T(8,128)}, u32[]{:S(2)}, u32[]{:S(2)}) collective-permute-start(f32[2,16,512]{2,1,0:T(8,128)} %get-tuple-element.17), channel_id=1, source_target_pairs={{0,2},{1,3},{2,0},{3,1},{4,6},{5,7},{6,4},{7,5},{8,10},{9,11},{10,... | collective-permute-start | bytes 196616 | tf_op jit(solution)/shard_map/ppermute | solution.py:459
  22.1 4.0 %collective-permute-start.4 = (f32[2,16,512]{2,1,0:T(8,128)}, f32[2,16,512]{2,1,0:T(8,128)}, u32[]{:S(2)}, u32[]{:S(2)}) collective-permute-start(f32[2,16,512]{2,1,0:T(8,128)} %get-tuple-element.17), channel_id=1, source_target_pairs={{0,3},{1,0},{2,1},{3,2},{4,7},{5,4},{6,5},{7,6},{8,11},{9,8},{10,9... | collective-permute-start | bytes 196616 | tf_op jit(solution)/shard_map/ppermute | solution.py:459
  27.0 6.4 %copy-start.30 = (f32[1,16,512]{2,1,0:T(8,128)}, f32[1,16,512]{2,1,0:T(8,128)S(1)}, u32[]{:S(2)}) copy-start(f32[1,16,512]{2,1,0:T(8,128)S(1)} %get-tuple-element.31) | copy-start | bytes 98308
  27.8 5.6 %copy-start.28 = (f32[1,16,512]{2,1,0:T(8,128)}, f32[1,16,512]{2,1,0:T(8,128)S(1)}, u32[]{:S(2)}) copy-start(f32[1,16,512]{2,1,0:T(8,128)S(1)} %fusion.11) | copy-start | bytes 98308
  28.7 3.6 %copy-start.22 = (f32[1,16,512]{2,1,0:T(8,128)}, f32[1,16,512]{2,1,0:T(8,128)S(1)}, u32[]{:S(2)}) copy-start(f32[1,16,512]{2,1,0:T(8,128)S(1)} %get-tuple-element.34) | copy-start | bytes 98308
  28.7 4.2 %copy-start.23 = (f32[1,16,512]{2,1,0:T(8,128)}, f32[1,16,512]{2,1,0:T(8,128)S(1)}, u32[]{:S(2)}) copy-start(f32[1,16,512]{2,1,0:T(8,128)S(1)} %get-tuple-element.35) | copy-start | bytes 98308
  29.4 9.5 %collective-permute-start.5 = (f32[4,16,512]{2,1,0:T(8,128)}, f32[4,16,512]{2,1,0:T(8,128)}, u32[]{:S(2)}, u32[]{:S(2)}) collective-permute-start(f32[4,16,512]{2,1,0:T(8,128)} %pad_maximum_fusion), channel_id=1, source_target_pairs={{0,64},{1,65},{2,66},{3,67},{4,68},{5,69},{6,70},{7,71},{8,72},{9,... | collective-permute-start | bytes 393224 | tf_op jit(solution)/shard_map/ppermute | solution.py:459
  33.0 4.4 %collective-permute-start.6 = (f32[2,16,512]{2,1,0:T(8,128)}, f32[2,16,512]{2,1,0:T(8,128)S(1)}, u32[]{:S(2)}, u32[]{:S(2)}) collective-permute-start(f32[2,16,512]{2,1,0:T(8,128)} %pad_maximum_fusion.1), channel_id=1, source_target_pairs={{0,4},{1,5},{2,6},{3,7},{4,0},{5,1},{6,2},{7,3},{8,12},{9,13},{10,... | collective-permute-start | bytes 196616 | tf_op jit(solution)/shard_map/ppermute | solution.py:459
  33.4 4.7 %collective-permute-start.7 = (f32[2,16,512]{2,1,0:T(8,128)}, f32[2,16,512]{2,1,0:T(8,128)}, u32[]{:S(2)}, u32[]{:S(2)}) collective-permute-start(f32[2,16,512]{2,1,0:T(8,128)} %pad_maximum_fusion.1), channel_id=1, source_target_pairs={{0,68},{1,69},{2,70},{3,71},{4,64},{5,65},{6,66},{7,67},{8,76},{9,... | collective-permute-start | bytes 196616 | tf_op jit(solution)/shard_map/ppermute | solution.py:459
  37.4 0.6 copy-start.32
  39.8 0.6 copy-start.24
  39.8 1.2 copy-start.26
  41.0 11.8 %collective-permute-start.10 = (f32[2,16,512]{2,1,0:T(8,128)}, f32[2,16,512]{2,1,0:T(8,128)}, u32[]{:S(2)}, u32[]{:S(2)}) collective-permute-start(f32[2,16,512]{2,1,0:T(8,128)} %pad_maximum_fusion.2), channel_id=1, source_target_pairs={{0,24},{1,25},{2,26},{3,27},{4,28},{5,29},{6,30},{7,31},{8,0},{9,1... | collective-permute-start | bytes 196616 | tf_op jit(solution)/shard_map/ppermute | solution.py:459
  43.5 9.3 %collective-permute-start.8 = (f32[2,16,512]{2,1,0:T(8,128)}, f32[2,16,512]{2,1,0:T(8,128)}, u32[]{:S(2)}, u32[]{:S(2)}) collective-permute-start(f32[2,16,512]{2,1,0:T(8,128)} %pad_maximum_fusion.2), channel_id=1, source_target_pairs={{0,8},{1,9},{2,10},{3,11},{4,12},{5,13},{6,14},{7,15},{8,16},{9,17... | collective-permute-start | bytes 196616 | tf_op jit(solution)/shard_map/ppermute | solution.py:459
  43.5 9.3 %collective-permute-start.9 = (f32[2,16,512]{2,1,0:T(8,128)}, f32[2,16,512]{2,1,0:T(8,128)}, u32[]{:S(2)}, u32[]{:S(2)}) collective-permute-start(f32[2,16,512]{2,1,0:T(8,128)} %pad_maximum_fusion.2), channel_id=1, source_target_pairs={{0,16},{1,17},{2,18},{3,19},{4,20},{5,21},{6,22},{7,23},{8,24},{9,... | collective-permute-start | bytes 196616 | tf_op jit(solution)/shard_map/ppermute | solution.py:459
  45.2 1.6 %copy-start.1 = (s32[16,256,128]{2,1,0:T(8,128)S(1)}, s32[16,256,128]{2,1,0:T(8,128)}, u32[]{:S(2)}) copy-start(s32[16,256,128]{2,1,0:T(8,128)} %phase.5) | copy-start | bytes 6291460
  46.8 4.5 %copy-start.20 = (f32[2,128,512]{2,1,0:T(8,128)S(1)}, f32[2,128,512]{2,1,0:T(8,128)}, u32[]{:S(2)}) copy-start(f32[2,128,512]{2,1,0:T(8,128)} %copy-done.19) | copy-start | bytes 1572868
  46.8 6.0 %copy-start.25 = (f32[1,16,512]{2,1,0:T(8,128)S(1)}, f32[1,16,512]{2,1,0:T(8,128)}, u32[]{:S(2)}) copy-start(f32[1,16,512]{2,1,0:T(8,128)} %copy-done.24) | copy-start | bytes 98308
  46.8 6.0 %copy-start.27 = (f32[1,16,512]{2,1,0:T(8,128)S(1)}, f32[1,16,512]{2,1,0:T(8,128)}, u32[]{:S(2)}) copy-start(f32[1,16,512]{2,1,0:T(8,128)} %copy-done.26) | copy-start | bytes 98308
  46.8 6.0 %copy-start.31 = (f32[1,16,512]{2,1,0:T(8,128)S(1)}, f32[1,16,512]{2,1,0:T(8,128)}, u32[]{:S(2)}) copy-start(f32[1,16,512]{2,1,0:T(8,128)} %copy-done.30) | copy-start | bytes 98308
  46.8 7.0 %copy-start.29 = (f32[1,16,512]{2,1,0:T(8,128)S(1)}, f32[1,16,512]{2,1,0:T(8,128)}, u32[]{:S(2)}) copy-start(f32[1,16,512]{2,1,0:T(8,128)} %copy-done.28) | copy-start | bytes 98308
  46.9 15.8 %copy-start.4 = (bf16[2,512,512]{2,1,0:T(8,128)(2,1)S(1)}, bf16[2,512,512]{2,1,0:T(8,128)(2,1)}, u32[]{:S(2)}) copy-start(bf16[2,512,512]{2,1,0:T(8,128)(2,1)} %constant.137.clone.span_low) | copy-start | bytes 3145732
  46.9 15.8 %copy-start.7 = (bf16[256,256]{1,0:T(8,128)(2,1)S(1)}, bf16[256,256]{1,0:T(8,128)(2,1)}, u32[]{:S(2)}) copy-start(bf16[256,256]{1,0:T(8,128)(2,1)} %constant.140.clone.back_high) | copy-start | bytes 393220
  46.9 15.8 %copy-start.8 = (bf16[256,256]{1,0:T(8,128)(2,1)S(1)}, bf16[256,256]{1,0:T(8,128)(2,1)}, u32[]{:S(2)}) copy-start(bf16[256,256]{1,0:T(8,128)(2,1)} %constant.141.clone.back_low) | copy-start | bytes 393220
  46.9 15.8 %copy-start.15 = (f32[2,16,16]{2,1,0:T(8,128)S(1)}, f32[2,16,16]{2,1,0:T(8,128)}, u32[]{:S(2)}) copy-start(f32[2,16,16]{2,1,0:T(8,128)} %constant.145.clone.basis) | copy-start | bytes 6148
  51.4 11.3 %collective-permute-start.1 = (f32[2,128,512]{2,1,0:T(8,128)S(1)}, f32[2,128,512]{2,1,0:T(8,128)S(1)}, u32[]{:S(2)}, u32[]{:S(2)}) collective-permute-start(f32[2,128,512]{2,1,0:T(8,128)S(1)} %copy-done.20), channel_id=1, source_target_pairs={{0,64},{1,65},{2,66},{3,67},{4,68},{5,69},{6,70},{7,71},{8,72},{9,... | collective-permute-start | bytes 1572872 | tf_op jit(solution)/shard_map/ppermute | solution.py:459
  62.7 24.9 %copy-start.6 = (f32[256,128]{1,0:T(8,128)S(1)}, f32[256,128]{1,0:T(8,128)}, u32[]{:S(2)}) copy-start(f32[256,128]{1,0:T(8,128)} %gas.3) | copy-start | bytes 393220
  70.7 56.9 %collective-permute-start.11 = (f32[4,512,128]{2,1,0:T(8,128)S(1)}, f32[4,512,128]{2,1,0:T(8,128)S(1)}, u32[]{:S(2)}, u32[]{:S(2)}) collective-permute-start(f32[4,512,128]{2,1,0:T(8,128)S(1)} %get-tuple-element.19), channel_id=1, source_target_pairs={{0,32},{1,33},{2,34},{3,35},{4,36},{5,37},{6,38},{7,39},{8,40},{9,... | collective-permute-start | bytes 3145736 | tf_op jit(solution)/shard_map/ppermute | solution.py:459
  75.4 12.3 %collective-permute-start.13 = (f32[32,256]{1,0:T(8,128)S(1)}, f32[32,256]{1,0:T(8,128)S(1)}, u32[]{:S(2)}, u32[]{:S(2)}) collective-permute-start(f32[32,256]{1,0:T(8,128)S(1)} %get-tuple-element.39), channel_id=1, source_target_pairs={{0,1},{1,2},{2,3},{3,4},{4,5},{5,6},{6,7},{7,8},{8,9},{9,10},{10,1... | collective-permute-start | bytes 98312 | tf_op jit(solution)/shard_map/ppermute | solution.py:459
  75.9 11.8 %collective-permute-start.14 = (f32[32,256]{1,0:T(8,128)S(1)}, f32[32,256]{1,0:T(8,128)S(1)}, u32[]{:S(2)}, u32[]{:S(2)}) collective-permute-start(f32[32,256]{1,0:T(8,128)S(1)} %get-tuple-element.38), channel_id=1, source_target_pairs={{0,31},{1,0},{2,1},{3,2},{4,3},{5,4},{6,5},{7,6},{8,7},{9,8},{10,9... | collective-permute-start | bytes 98312 | tf_op jit(solution)/shard_map/ppermute | solution.py:459
  81.1 2.8 %collective-permute-start.15 = (f32[32,128]{1,0:T(8,128)S(1)}, f32[32,128]{1,0:T(8,128)S(1)}, u32[]{:S(2)}, u32[]{:S(2)}) collective-permute-start(f32[32,128]{1,0:T(8,128)S(1)} %get-tuple-element.43), channel_id=1, source_target_pairs={{0,32},{1,33},{2,34},{3,35},{4,36},{5,37},{6,38},{7,39},{8,40},{9,... | collective-permute-start | bytes 49160 | tf_op jit(solution)/shard_map/ppermute | solution.py:459
  83.0 4.7 %collective-permute-start.16 = (f32[32,128]{1,0:T(8,128)S(1)}, f32[32,128]{1,0:T(8,128)S(1)}, u32[]{:S(2)}, u32[]{:S(2)}) collective-permute-start(f32[32,128]{1,0:T(8,128)S(1)} %get-tuple-element.42), channel_id=1, source_target_pairs={{0,96},{1,97},{2,98},{3,99},{4,100},{5,101},{6,102},{7,103},{8,104... | collective-permute-start | bytes 49160 | tf_op jit(solution)/shard_map/ppermute | solution.py:459
  98.8 26.4 %collective-permute-start.12 = (f32[512,256]{1,0:T(8,128)S(1)}, f32[512,256]{1,0:T(8,128)S(1)}, u32[]{:S(2)}, u32[]{:S(2)}) collective-permute-start(f32[512,256]{1,0:T(8,128)S(1)} %get-tuple-element.20.ours), channel_id=1, source_target_pairs={{0,32},{1,33},{2,34},{3,35},{4,36},{5,37},{6,38},{7,39},{8,40},{9,... | collective-permute-start | bytes 1572872 | tf_op jit(solution)/shard_map/ppermute | solution.py:459
  98.9 7.7 %collective-permute-start.19 = (f32[16,128]{1,0:T(8,128)S(1)}, f32[16,128]{1,0:T(8,128)S(1)}, u32[]{:S(2)}, u32[]{:S(2)}) collective-permute-start(f32[16,128]{1,0:T(8,128)S(1)} %get-tuple-element.45), channel_id=1, source_target_pairs={{0,32},{1,33},{2,34},{3,35},{4,36},{5,37},{6,38},{7,39},{8,40},{9,... | collective-permute-start | bytes 24584 | tf_op jit(solution)/shard_map/ppermute | solution.py:459
  100.8 10.3 %collective-permute-start.17 = (f32[16,256]{1,0:T(8,128)S(1)}, f32[16,256]{1,0:T(8,128)S(1)}, u32[]{:S(2)}, u32[]{:S(2)}) collective-permute-start(f32[16,256]{1,0:T(8,128)S(1)} %get-tuple-element.41), channel_id=1, source_target_pairs={{0,1},{1,2},{2,3},{3,4},{4,5},{5,6},{6,7},{7,8},{8,9},{9,10},{10,1... | collective-permute-start | bytes 49160 | tf_op jit(solution)/shard_map/ppermute | solution.py:459
  100.8 10.3 %collective-permute-start.18 = (f32[16,256]{1,0:T(8,128)S(1)}, f32[16,256]{1,0:T(8,128)S(1)}, u32[]{:S(2)}, u32[]{:S(2)}) collective-permute-start(f32[16,256]{1,0:T(8,128)S(1)} %get-tuple-element.40), channel_id=1, source_target_pairs={{0,31},{1,0},{2,1},{3,2},{4,3},{5,4},{6,5},{7,6},{8,7},{9,8},{10,9... | collective-permute-start | bytes 49160 | tf_op jit(solution)/shard_map/ppermute | solution.py:459
  106.5 4.6 %collective-permute-start.20 = (f32[16,128]{1,0:T(8,128)S(1)}, f32[16,128]{1,0:T(8,128)S(1)}, u32[]{:S(2)}, u32[]{:S(2)}) collective-permute-start(f32[16,128]{1,0:T(8,128)S(1)} %get-tuple-element.44), channel_id=1, source_target_pairs={{0,96},{1,97},{2,98},{3,99},{4,100},{5,101},{6,102},{7,103},{8,104... | collective-permute-start | bytes 24584 | tf_op jit(solution)/shard_map/ppermute | solution.py:459
where the time goes:
time: 131 us; the launch traced here: 130 us
  Pallas kernels  50.8 us (39%)
  starting transfers between devices  36.6 us (28%)
  waiting for transfers between devices  24.1 us (18%)
  other arithmetic  10.8 us (8%)
  local copies, waits for them, and re-layouts  6.33 us (5%)
    pallas_call x9, Pallas kernels, run(): pl.pallas_call(body, out_shape=outs, grid_spec=pltpu.PrefetchScalarGridSp...  50.8 us
    ppermute x21, starting transfers between devices, move(): return lax.ppermute(value, ('grp', 'pen'), pairs)  36.6 us
    ppermute x21, waiting for transfers between devices, move(): return lax.ppermute(value, ('grp', 'pen'), pairs)  24.1 us
    unnamed x66, local copies, waits for them, and re-layouts  6.23 us
    sub x1, other arithmetic, per_device(): pressure_source[:, :half] - sign * pressure_source[:, half:]  2.77 us
  transfers between devices with their start and end apart: 21, of which 7 were waited for; matrix products, arithmetic and copies ran while one was open for 3% of the time, Pallas kernels for 26%

commit v1 on v0

--- a/solution.py
+++ b/solution.py
@@ -16,6 +16,7 @@
 Z_RING, Y_PAIR, X_RING = 4, 2, 4
 VMEM_LIMIT = 48 * 1024 * 1024
 LANES = 256
+CHUNK = 32
 
 
 def halves(value):
@@ -92,23 +93,40 @@
     return pl.BlockSpec((1,) + rest, lambda i, s: (s[place],) + (0,) * len(rest))
 
 
-def run(body, scalars, arrays, specs, outs, out_specs=None, scratch=(), aliases=None, flops=0):
+def plane_of(array):
+    rest = array.shape[1:]
+    return pl.BlockSpec((1,) + rest, lambda i, s: (i,) + (0,) * len(rest))
+
+
+ORDER = pl.BlockSpec(memory_space=pl.ANY)
+
+
+def run(
+    body, scalars, arrays, specs, outs, out_specs=None, scratch=(), aliases=None, flops=0, steps=1
+):
     outs = [jax.ShapeDtypeStruct(shape, jnp.float32) for shape in outs]
     moved = sum(math.prod(a.shape) * 4 for a in arrays) + sum(math.prod(o.shape) * 4 for o in outs)
+    out_specs = out_specs or [whole(o) for o in outs]
     return pl.pallas_call(
         body,
         out_shape=outs,
         grid_spec=pltpu.PrefetchScalarGridSpec(
             num_scalar_prefetch=1,
-            grid=(1,),
+            grid=(steps,),
             in_specs=specs,
-            out_specs=out_specs or [whole(o) for o in outs],
+            out_specs=out_specs,
             scratch_shapes=list(scratch),
         ),
         input_output_aliases=aliases or {},
         compiler_params=pltpu.CompilerParams(vmem_limit_bytes=VMEM_LIMIT),
         cost_estimate=pl.CostEstimate(flops=flops, bytes_accessed=moved, transcendentals=0),
     )(scalars, *arrays)
+
+
+def fold_body(s_ref, source, away):
+    half = source.shape[1] // 2
+    sign = (1 - 2 * s_ref[0]).astype(jnp.float32)
+    away[...] = source[:, :half] - sign * source[:, half:]
 
 
 def spectral(planes, into_high, into_low, span_high, span_low):
@@ -138,7 +156,7 @@
 
 def arrived_body(
     s_ref, arrived, held, into_high, into_low, span_high, span_low, lam, sigma, edge, basis_t, far,
-    planes, edges, sent, sums,
+    planes, edges, carried, opening, sums,
 ):
     count = held.shape[0]
     own = 2 * count
@@ -167,7 +185,7 @@
         for i in range(1, own):
             carry = mine[i] * planes[jnp.bitwise_xor(i, code), rows, cols] - carry
             carries.append(carry)
-        sent[0, rows, cols] = carry
+        carried[rows, cols] = carry
         shared = carry / (mine[own] * other[own] - mine[own - 1] * other[own - 1])
         scale = edge[rows]
         value = shared * other[own]
@@ -175,7 +193,7 @@
         for i in range(own - 2, -1, -1):
             value = (carries[i] - mine[i] * value) / mine[i + 1]
             sums[parity, i, :, cols] += scale * value
-        sent[1, rows, cols] = value + other[own - 1] * shared / mine[own]
+        opening[rows, cols] = value + other[own - 1] * shared / mine[own]
         shared = scale * shared
         for i in range(own):
             term = other[i] * shared
@@ -193,8 +211,85 @@
     edges[1] = edge_low + far[0] * edge_high
 
 
+def powers(log_rho):
+    return lambda n: jnp.exp(log_rho[0] * n)
+
+
+def scalar(value):
+    return value.astype(jnp.float32)
+
+
+def z_body(s_ref, wall_there, after, edges, got1, got2, got3, log_rho, four, two, *, width):
+    power = powers(log_rho)
+    zi = s_ref[5]
+    wide = float(width)
+    right, left = edges[0], edges[1]
+    low_sum = jnp.zeros_like(right)
+    high_sum = jnp.zeros_like(right)
+    right4 = power(wide * scalar(Z_RING - 1 - zi)) * right
+    left4 = power(wide * scalar(zi)) * left
+    for d, got in ((1, got1), (2, got2), (3, got3)):
+        before = scalar(zi >= d)
+        source = jnp.where(zi >= d, zi - d, zi - d + Z_RING)
+        low_sum = low_sum + before * power(wide * (d - 1)) * got[0]
+        high_sum = high_sum + (1.0 - before) * power(wide * (Z_RING - 1 - d)) * got[1]
+        right4 = right4 + power(wide * scalar(Z_RING - 1 - source)) * got[0]
+        left4 = left4 + power(wide * scalar(source)) * got[1]
+    hop = power(wide)
+    per_rho = power(-1.0)
+    four[0] = per_rho * low_sum + left + hop * high_sum
+    four[1] = per_rho * high_sum + right + hop * low_sum
+    four[2] = right4
+    four[3] = left4
+    two[0] = right4
+    two[1] = left4
+
+
+def y_body(s_ref, after, four, there, beside1, beside2, log_rho, run8, part, *, width):
+    power = powers(log_rho)
+    zi = s_ref[5]
+    wide = float(width)
+    behind = scalar(s_ref[6])
+    other0 = beside1[0] + beside2[0]
+    other1 = beside1[1] + beside2[1]
+    right4 = four[2] + there[2]
+    left4 = four[3] + there[3]
+    low_sum = behind * power(wide * scalar(zi)) * other0
+    high_sum = (1.0 - behind) * power(wide * scalar(Z_RING - 1 - zi)) * other1
+    run4 = power(wide * Z_RING)
+    is_behind = s_ref[6] == 1
+    run8[0] = jnp.where(is_behind, run4 * other0 + right4, run4 * right4 + other0)
+    run8[1] = jnp.where(is_behind, other1 + run4 * left4, left4 + run4 * other1)
+    hop = power(wide)
+    per_rho = power(-1.0)
+    part[0] = four[0] + there[0] + per_rho * low_sum + hop * high_sum
+    part[1] = four[1] + there[1] + per_rho * high_sum + hop * low_sum
+
+
+def x_sums(s_ref, run8, part, gots, log_rho, width):
+    power = powers(log_rho)
+    wide = float(width)
+    block = Z_RING * Y_PAIR
+    right_sum = power(wide * block * (X_RING - 1)) * run8[0]
+    left_sum = power(wide * block * (X_RING - 1)) * run8[1]
+    for d, got in enumerate(gots, 1):
+        right_sum = right_sum + power(wide * block * (d - 1)) * got[0]
+        left_sum = left_sum + power(wide * block * (X_RING - 1 - d)) * got[1]
+    periodic = 1.0 / (1.0 - power(wide * block * X_RING))
+    low_sum = power(wide * scalar(s_ref[7])) * right_sum * periodic
+    high_sum = power(wide * scalar(block - 1 - s_ref[7])) * left_sum * periodic
+    rho = power(1.0)
+    per_rho = power(-1.0)
+    hop = power(wide)
+    gain = rho / (1.0 - rho * rho)
+    into_low = gain * (part[0] + per_rho * low_sum + hop * high_sum)
+    into_high = gain * (part[1] + per_rho * high_sum + hop * low_sum)
+    return into_low, into_high
+
+
 def solve_body(
-    s_ref, planes, got, gains, span_high, span_low, back_high, back_low, lam, sigma, edge, basis,
+    s_ref, after, planes, carried, first_there, run8, part, got1, got2, got3, log_rho,
+    span_high, span_low, back_high, back_low, lam, sigma, edge, basis,
     wall, away, keep, solved, both, first,
 ):
     own, width, half = planes.shape
@@ -205,8 +300,9 @@
     is_low = s_ref[1] == 1
     code = s_ref[2]
     depthwise = lambda v: jnp.dot(basis[0], v, precision=HIGHEST, preferred_element_type=jnp.float32)
-    gain_low = depthwise(gains[0])
-    gain_high = depthwise(gains[1])
+    into_low, into_high = x_sums(s_ref, run8, part, (got1, got2, got3), log_rho, width)
+    gain_low = depthwise(into_low)
+    gain_high = depthwise(into_high)
     both[0] = gain_low + gain_high
     both[1] = gain_low - gain_high
     first[...] = jnp.zeros_like(first)
@@ -237,11 +333,11 @@
             there = -other[i] * right - there
             term = mine[own - 1 - i] * right
             direct = direct - term if i % 2 == 0 else direct + term
-        there = there + got[0, rows, cols]
+        there = there + carried[rows, cols]
         value = (carry * other[own] - mine[own - 1] * there) / (
             mine[own] * other[own] - mine[own - 1] * other[own - 1]
         )
-        far_first = got[1, rows, cols] + (direct + value) / other[own]
+        far_first = first_there[rows, cols] + (direct + value) / other[own]
         solved[jnp.bitwise_xor(own - 1, code), rows, cols] = value
         for i in range(own - 2, -1, -1):
             value = (carries[i] - mine[i] * value) / mine[i + 1]
@@ -281,27 +377,161 @@
     out[:, half:] = sign * (ours - theirs)
 
 
-def edge_body(s_ref, temp, phase, conductivity, across, along):
+def edge_body(s_ref, after, temp, phase, conductivity, cond, across, along, packed):
     depth, rows, width = temp.shape
-    lane = lax.broadcasted_iota(jnp.int32, (rows, width), 1)
+    lane = lax.broadcasted_iota(jnp.int32, (CHUNK, width), 1)
     cold, warm = conductivity[0], conductivity[1]
-
-    def plane(z, packed):
-        cond = jnp.where(phase[z] == 1, warm, cold)
-        both = (temp[z], cond)
-        for k in range(2):
-            at = k * depth + z
-            packed = jnp.where(lane == at, pltpu.roll(both[k], at + 1, 1), packed)
-            at = (2 + k) * depth + z
-            packed = jnp.where(lane == at, pltpu.roll(both[k], at, 1), packed)
-            place = pl.ds(k * depth + z, 1)
-            along[0, place] = both[k][rows - 1 :]
-            along[1, place] = both[k][:1]
-        return packed
-
-    packed = lax.fori_loop(0, depth, plane, jnp.zeros((rows, width), jnp.float32)).T
-    across[0] = packed[: 2 * depth]
-    across[1] = packed[2 * depth : 4 * depth]
+    packed[...] = jnp.zeros_like(packed)
+
+    def plane(z, nothing):
+        for start in range(0, rows, CHUNK):
+            at = slice(start, start + CHUNK)
+            kept = packed[at]
+            value = jnp.where(phase[z, at] == 1, warm, cold)
+            cond[z, at] = value
+            for k, part in enumerate((temp[z, at], value)):
+                spot = 2 * (k * depth + z)
+                chosen_lane = (lane == spot) | (lane == spot + 1)
+                kept = jnp.where(chosen_lane, pltpu.roll(part, spot + 1, 1), kept)
+                if start == 0:
+                    along[1, pl.ds(k * depth + z, 1)] = part[:1]
+                if start + CHUNK == rows:
+                    along[0, pl.ds(k * depth + z, 1)] = part[CHUNK - 1 :]
+            packed[at] = kept
+        return nothing
+
+    lax.fori_loop(0, depth, plane, 0)
+    across[...] = packed[...].T[: 4 * depth]
+
+
+def beside(ours, from_left, from_right):
+    row = lax.broadcasted_iota(jnp.int32, ours.shape, 0)
+    count = ours.shape[0]
+    return jnp.where(
+        row % 2 == 1, pltpu.roll(from_left, 1, 0), pltpu.roll(from_right, count - 1, 0)
+    )
+
+
+def to_columns(packed, values):
+    count = values.shape[0]
+    packed[:count] = values
+    return packed[...].T
+
+
+def step_planes(temp, cond, up, down, cond_up, cond_down, inflow, emit):
+    depth, rows, width = temp.shape
+    lane = lax.broadcasted_iota(jnp.int32, (CHUNK, width), 1)
+    end = width - 1
+
+    def shifted(ref, z, start, above, below):
+        if start == 0:
+            upper = jnp.concatenate([above[pl.ds(z, 1)], ref[z, : CHUNK - 1]], axis=0)
+        else:
+            upper = ref[z, start - 1 : start + CHUNK - 1]
+        if start + CHUNK == rows:
+            lower = jnp.concatenate([ref[z, start + 1 :], below[pl.ds(z, 1)]], axis=0)
+        else:
+            lower = ref[z, start + 1 : start + CHUNK + 1]
+        return upper, lower
+
+    def plane(z, first):
+        before = jnp.maximum(z - 1, 0)
+        after = jnp.minimum(z + 1, depth - 1)
+        for start in range(0, rows, CHUNK):
+            at = slice(start, start + CHUNK)
+            here = temp[z, at]
+            own = cond[z, at]
+            pairs = []
+            total = None
+            sides = list(zip(shifted(temp, z, start, up, down), shifted(cond, z, start, cond_up, cond_down)))
+            sides += [(temp[before, at], cond[before, at]), (temp[after, at], cond[after, at])]
+            for side_temp, side_cond in sides:
+                pair = own + side_cond
+                pairs.append(pair)
+                term = pair * (side_temp - here)
+                total = term if total is None else total + term
+            pair = own + pltpu.roll(own, end, 1)
+            pairs.append(pair)
+            flow = jnp.where(lane == end, 0.0, pair * (pltpu.roll(here, end, 1) - here))
+            total = total + (flow - pltpu.roll(flow, 1, 1))
+            spot = width - (2 * z + 1)
+            entering = pltpu.roll(inflow[at], spot, 1)
+            total = total + jnp.where((lane == 0) | (lane == end), entering, 0.0)
+            emit(z, start, first, here + (0.5 * STEP_RATE) * total, pairs)
+
+    plane(0, True)
+
+    def later(z, nothing):
+        plane(z, False)
+        return nothing
+
+    lax.fori_loop(1, depth, later, 0)
+
+
+def first_body(
+    s_ref, after, temp, cond, gas, packs, from_left, from_right, from_up, from_down,
+    out, across, along, packed, inflow, turned,
+):
+    depth, rows, width = temp.shape
+    lane = lax.broadcasted_iota(jnp.int32, (CHUNK, width), 1)
+    packed[...] = jnp.zeros_like(packed)
+    halo = beside(packs[...], from_left[...], from_right[...])
+    ours = packs[...]
+    half = 2 * depth
+    flow = (ours[half:] + halo[half:]) * (halo[:half] - ours[:half])
+    inflow[...] = to_columns(packed, flow)
+
+    def emit(z, start, first, value, pairs):
+        at = slice(start, start + CHUNK)
+        if first:
+            value = value + (STEP_RATE * HEAT_TRANSFER) * (gas[at] - temp[0, at])
+        out[z, at] = value
+        spot = 2 * z
+        kept = jnp.where((lane == spot) | (lane == spot + 1), pltpu.roll(value, spot + 1, 1), turned[at])
+        turned[at] = kept
+        if start == 0:
+            along[1, pl.ds(z, 1)] = value[:1]
+        if start + CHUNK == rows:
+            along[0, pl.ds(z, 1)] = value[CHUNK - 1 :]
+
+    turned[...] = jnp.zeros_like(turned)
+    step_planes(
+        temp, cond, from_up.at[:depth], from_down.at[:depth], from_up.at[depth:], from_down.at[depth:],
+        inflow, emit,
+    )
+    across[...] = turned[...].T[:half]
+
+
+def second_body(
+    s_ref, after, base, cond, temp, gas, packs, from_left, from_right, from_up, from_down,
+    base_packs, base_left, base_right, base_up, base_down, out, weights, packed, inflow, face,
+):
+    depth, rows, width = base.shape
+    lane = lax.broadcasted_iota(jnp.int32, (CHUNK, width), 1)
+    end = width - 1
+    packed[...] = jnp.zeros_like(packed)
+    half = 2 * depth
+    pair = packs[half:] + beside(packs[half:], from_left[half:], from_right[half:])
+    ours = base_packs[...]
+    halo = beside(ours, base_left[...], base_right[...])
+    inflow[...] = to_columns(packed, pair * (halo - ours))
+    face[...] = to_columns(packed, pair)
+
+    def emit(z, start, first, value, pairs):
+        at = slice(start, start + CHUNK)
+        if first:
+            value = value + (STEP_RATE * HEAT_TRANSFER) * (gas[at] - temp[0, at])
+            edge = pltpu.roll(face[at], end, 1)
+            across = pairs[4]
+            left = jnp.where(lane == 0, edge, pltpu.roll(across, 1, 1))
+            right = jnp.where(lane == end, edge, across)
+            for k, pair in enumerate((pairs[0], pairs[1], left, right, pairs[3])):
+                weights[k, at] = (0.5 * STEP_RATE) * pair
+        out[z, at] = value
+
+    step_planes(
+        base, cond, base_up, base_down, from_up.at[depth:], from_down.at[depth:], inflow, emit
+    )
 
 
 def faces(value, row, lane, up, down, left, right):
@@ -312,108 +542,6 @@
         jnp.where(lane == 0, left, pltpu.roll(value, 1, 1)),
         jnp.where(lane == width - 1, right, pltpu.roll(value, width - 1, 1)),
     )
-
-
-def stage_columns(columns, sides, used):
-    columns[...] = jnp.zeros_like(columns)
-    at = 0
-    for side in sides:
-        columns[at : at + used] = side[...]
-        at += used
-    return columns[...].T
-
-
-def first_body(
-    s_ref, temp, phase, gas, conductivity, from_left, from_right, from_up, from_down,
-    out, across, along, columns,
-):
-    depth, rows, width = temp.shape
-    row = lax.broadcasted_iota(jnp.int32, (rows, width), 0)
-    lane = lax.broadcasted_iota(jnp.int32, (rows, width), 1)
-    cold, warm = conductivity[0], conductivity[1]
-    halo = stage_columns(columns, (from_left, from_right), 2 * depth)
-    conduct = lambda z: jnp.where(phase[z] == 1, warm, cold)
-
-    def plane(z, packed):
-        here = temp[z]
-        cond = conduct(z)
-        near = lambda k: (
-            from_up[pl.ds(k * depth + z, 1)],
-            from_down[pl.ds(k * depth + z, 1)],
-            pltpu.roll(halo, width - (k * depth + z), 1),
-            pltpu.roll(halo, width - 1 - ((2 + k) * depth + z), 1),
-        )
-        total = jnp.zeros_like(here)
-        for side_temp, side_cond in zip(
-            faces(here, row, lane, *near(0)), faces(cond, row, lane, *near(1))
-        ):
-            total = total + (cond + side_cond) * (side_temp - here)
-        for beside in (jnp.maximum(z - 1, 0), jnp.minimum(z + 1, depth - 1)):
-            total = total + (cond + conduct(beside)) * (temp[beside] - here)
-        surface = jnp.where(z == 0, STEP_RATE * HEAT_TRANSFER, 0.0) * (gas[...] - temp[0])
-        value = here + (0.5 * STEP_RATE) * total + surface
-        out[z] = value
-        packed = jnp.where(lane == z, pltpu.roll(value, z + 1, 1), packed)
-        packed = jnp.where(lane == depth + z, pltpu.roll(value, depth + z, 1), packed)
-        along[0, pl.ds(z, 1)] = value[rows - 1 :]
-        along[1, pl.ds(z, 1)] = value[:1]
-        return packed
-
-    packed = lax.fori_loop(0, depth, plane, jnp.zeros((rows, width), jnp.float32)).T
-    across[0] = packed[:depth]
-    across[1] = packed[depth : 2 * depth]
-
-
-def second_body(
-    s_ref, base, temp, phase, gas, conductivity, from_left, from_right, from_up, from_down,
-    base_left, base_right, base_up, base_down, out, weights, columns,
-):
-    depth, rows, width = base.shape
-    row = lax.broadcasted_iota(jnp.int32, (rows, width), 0)
-    lane = lax.broadcasted_iota(jnp.int32, (rows, width), 1)
-    cold, warm = conductivity[0], conductivity[1]
-    halo = stage_columns(columns, (from_left, from_right), 2 * depth)
-    base_halo = stage_columns(columns, (base_left, base_right), depth)
-    conduct = lambda z: jnp.where(phase[z] == 1, warm, cold)
-
-    def plane(z, nothing):
-        here = base[z]
-        cond = conduct(z)
-        near_base = (
-            base_up[pl.ds(z, 1)],
-            base_down[pl.ds(z, 1)],
-            pltpu.roll(base_halo, width - z, 1),
-            pltpu.roll(base_halo, width - 1 - (depth + z), 1),
-        )
-        near_cond = (
-            from_up[pl.ds(depth + z, 1)],
-            from_down[pl.ds(depth + z, 1)],
-            pltpu.roll(halo, width - (depth + z), 1),
-            pltpu.roll(halo, width - 1 - (3 * depth + z), 1),
-        )
-        total = jnp.zeros_like(here)
-        pairs = []
-        for side_base, side_cond in zip(
-            faces(here, row, lane, *near_base), faces(cond, row, lane, *near_cond)
-        ):
-            pair = cond + side_cond
-            pairs.append(pair)
-            total = total + pair * (side_base - here)
-        for beside in (jnp.maximum(z - 1, 0), jnp.minimum(z + 1, depth - 1)):
-            pair = cond + conduct(beside)
-            total = total + pair * (base[beside] - here)
-        pairs.append(pair)
-        surface = jnp.where(z == 0, STEP_RATE * HEAT_TRANSFER, 0.0) * (gas[...] - temp[0])
-        out[z] = here + (0.5 * STEP_RATE) * total + surface
-
-        @pl.when(z == 0)
-        def _():
-            for k in range(5):
-                weights[k] = (0.5 * STEP_RATE) * pairs[k]
-
-        return nothing
-
-    lax.fori_loop(0, depth, plane, 0)
 
 
 def wall_body(s_ref, ours, theirs, weights, base, out):
@@ -479,7 +607,7 @@
     tab = make_tables(span_len, width, depth)
     const = {k: tuple(map(jnp.asarray, v)) if isinstance(v, tuple) else jnp.asarray(v) for k, v in tab.items()}
     code = jnp.where(low == 0, core * 4, 7 - 4 * core)
-    scalars = jnp.stack([core, low, code, low, core]).astype(jnp.int32)
+    scalars = jnp.stack([core, low, code, low, core, zi, yl, place]).astype(jnp.int32)
     span = list(const["span"])
     into = list(const["into"])
     back = list(const["back"])
@@ -498,113 +626,95 @@
 
     def exchange(across, along):
         return [
-            move(across[0], right_on), move(across[1], left_on),
+            move(across, right_on), move(across, left_on),
             move(along[0], down_on), move(along[1], up_on),
         ]
 
     other_core = lambda g, p: (g ^ 1, p)
     other_half = lambda g, p: (g ^ 2, p)
-    sign = jnp.where(core == 0, 1.0, -1.0).astype(jnp.float32)
-    arrived = move(pressure_source[:, :half] - sign * pressure_source[:, half:], other_core)
+    folded_shape = (depth_loc, half, width)
+    folded = jax.ShapeDtypeStruct(folded_shape, jnp.float32)
+    (sent,) = run(
+        fold_body, scalars, [pressure_source], [plane_of(pressure_source)], [folded_shape],
+        out_specs=[plane_of(folded)], steps=depth_loc,
+    )
+    arrived = move(sent, other_core)
     spectral_flops = 6 * depth_loc * width * half * (half + width)
     (held,) = run(
         held_body, scalars, [pressure_source, *into, *span],
         [whole(pressure_source), *into_specs, *span_specs],
         [(depth_loc, width, half)], flops=spectral_flops,
     )
-    planes, edges, sent = run(
+    planes, edges, carried, opening = run(
         arrived_body, scalars,
         [arrived, held, *into, *span, *strip, const["basis_t"], const["far"]],
         [whole(arrived), whole(held), *into_specs, *span_specs, *strip_specs,
          chosen(const["basis_t"], 1), chosen(const["far"], 0)],
-        [(own, width, half), (2, depth, half), (2, width, half)],
+        [(own, width, half), (2, depth, half), (width, half), (width, half)],
         scratch=[pltpu.VMEM((2, depth, 8, half), jnp.float32)], flops=spectral_flops,
     )
-    sent = move(sent, other_half)
-
-    solid = [solid_temp, phase_map]
-    solid_specs = [whole(solid_temp), whole(phase_map)]
-    across, along = run(
-        edge_body, scalars, [*solid, phase_conductivity], [*solid_specs, smem],
-        [(2, 2 * depth, tile_rows), (2, 2 * depth, width)], flops=10**8,
-    )
-    near = exchange(across, along)
+    carried_there = move(carried, other_half)
+    opening_there = move(opening, other_half)
+    z_got = [
+        move(edges, lambda g, p, d=d: (g, p // Z_RING * Z_RING + (p + d) % Z_RING))
+        for d in range(1, Z_RING)
+    ]
+
+    column_scratch = pltpu.VMEM((tile_rows, width), jnp.float32)
+    row_scratch = pltpu.VMEM((width, tile_rows), jnp.float32)
+    cond, packs, along = run(
+        edge_body, scalars, [edges, solid_temp, phase_map, phase_conductivity],
+        [ORDER, whole(solid_temp), whole(phase_map), smem],
+        [(depth, tile_rows, width), (4 * depth, tile_rows), (2, 2 * depth, width)],
+        scratch=[column_scratch], flops=10**9,
+    )
+    near = exchange(packs, along)
     near_specs = [whole(a) for a in near]
-    column_scratch = [pltpu.VMEM((width, tile_rows), jnp.float32)]
-    base, across, along = run(
-        first_body, scalars, [*solid, gas_wall_temp, phase_conductivity, *near],
-        [*solid_specs, whole(gas_wall_temp), smem, *near_specs],
-        [(depth, tile_rows, width), (2, depth, tile_rows), (2, depth, width)],
-        scratch=column_scratch, flops=10**9,
-    )
-    near_base = exchange(across, along)
+
+    log_rho = const["log_rho"]
+    log_spec = chosen(log_rho, 0)
+    pair_shape = edges.shape
+    four, two = run(
+        functools.partial(z_body, width=width), scalars,
+        [carried_there, along, edges, *z_got, log_rho],
+        [ORDER, ORDER, whole(edges), *[whole(a) for a in z_got], log_spec],
+        [(4,) + pair_shape[1:], pair_shape],
+    )
+    there = move(four, other_half)
+    beside1 = move(two, lambda g, p: (g, p ^ Z_RING))
+    beside2 = move(two, lambda g, p: (g ^ 2, p ^ Z_RING))
+
+    base, base_packs, base_along = run(
+        first_body, scalars, [two, solid_temp, cond, gas_wall_temp, packs, *near],
+        [ORDER, whole(solid_temp), whole(cond), whole(gas_wall_temp), whole(packs), *near_specs],
+        [(depth, tile_rows, width), (2 * depth, tile_rows), (2, depth, width)],
+        scratch=[row_scratch, column_scratch, column_scratch], flops=3 * 10**9,
+    )
+    near_base = exchange(base_packs, base_along)
+    run8, part = run(
+        functools.partial(y_body, width=width), scalars,
+        [base_along, four, there, beside1, beside2, log_rho],
+        [ORDER, whole(four), whole(there), whole(beside1), whole(beside2), log_spec],
+        [pair_shape, pair_shape],
+    )
+    block = Z_RING * Y_PAIR
+    x_got = [move(run8, lambda g, p, d=d: (g, (p + block * d) % pencils)) for d in range(1, X_RING)]
     first_plane = pl.BlockSpec((1, tile_rows, width), lambda i, s: (0, 0, 0))
     base, weights = run(
         second_body, scalars,
-        [base, solid_temp, phase_map, gas_wall_temp, phase_conductivity, *near, *near_base],
-        [whole(base), first_plane, solid_specs[1], whole(gas_wall_temp), smem, *near_specs,
-         *[whole(a) for a in near_base]],
+        [run8, base, cond, solid_temp, gas_wall_temp, packs, *near, base_packs, *near_base],
+        [ORDER, whole(base), whole(cond), first_plane, whole(gas_wall_temp), whole(packs), *near_specs,
+         whole(base_packs), *[whole(a) for a in near_base]],
         [(depth, tile_rows, width), (5, tile_rows, width)],
-        scratch=column_scratch, flops=10**9,
-    )
-
-    log_rho = const["log_rho"][core]
-    power = lambda n: jnp.exp(log_rho * n)
-    wide = float(width)
-    hop = power(wide)
-    rho = power(1.0)
-    per_rho = power(-1.0)
-    right, left = edges[0], edges[1]
-
-    low_sum = jnp.zeros_like(right)
-    high_sum = jnp.zeros_like(right)
-    right4 = power(wide * (Z_RING - 1 - zi)) * right
-    left4 = power(wide * zi) * left
-    for d in range(1, Z_RING):
-        got = move(edges, lambda g, p, d=d: (g, p // Z_RING * Z_RING + (p + d) % Z_RING))
-        source = (zi - d) % Z_RING
-        before = zi >= d
-        low_sum = low_sum + jnp.where(before, power(wide * (d - 1)), 0.0) * got[0]
-        high_sum = high_sum + jnp.where(before, 0.0, power(wide * (Z_RING - 1 - d))) * got[1]
-        right4 = right4 + power(wide * (Z_RING - 1 - source)) * got[0]
-        left4 = left4 + power(wide * source) * got[1]
-    into_low = per_rho * low_sum + left + hop * high_sum
-    into_high = per_rho * high_sum + right + hop * low_sum
-
-    first = move(jnp.stack([into_low, into_high, right4, left4]), other_half)
-    group4 = jnp.stack([right4, left4])
-    other = move(group4, lambda g, p: (g, p ^ Z_RING)) + move(group4, lambda g, p: (g ^ 2, p ^ Z_RING))
-    into_low = into_low + first[0]
-    into_high = into_high + first[1]
-    right4 = right4 + first[2]
-    left4 = left4 + first[3]
-    after = yl == 1
-    low_sum = jnp.where(after, power(wide * zi), 0.0) * other[0]
-    high_sum = jnp.where(after, 0.0, power(wide * (Z_RING - 1 - zi))) * other[1]
-    run4 = power(wide * Z_RING)
-    right8 = jnp.where(after, run4 * other[0] + right4, run4 * right4 + other[0])
-    left8 = jnp.where(after, other[1] + run4 * left4, left4 + run4 * other[1])
-
-    packed = jnp.stack([right8, left8])
-    block = Z_RING * Y_PAIR
-    right_sum = power(wide * block * (X_RING - 1)) * right8
-    left_sum = power(wide * block * (X_RING - 1)) * left8
-    for d in range(1, X_RING):
-        got = move(packed, lambda g, p, d=d: (g, (p + block * d) % pencils))
-        right_sum = right_sum + power(wide * block * (d - 1)) * got[0]
-        left_sum = left_sum + power(wide * block * (X_RING - 1 - d)) * got[1]
-    periodic = 1.0 / (1.0 - power(wide * block * X_RING))
-    low_sum = low_sum + power(wide * place) * right_sum * periodic
-    high_sum = high_sum + power(wide * (block - 1 - place)) * left_sum * periodic
-    gain = rho / (1.0 - rho * rho)
-    into_low = gain * (into_low + per_rho * low_sum + hop * high_sum)
-    into_high = gain * (into_high + per_rho * high_sum + hop * low_sum)
-    gains = jnp.stack([into_low, into_high])
+        scratch=[row_scratch, column_scratch, column_scratch], flops=3 * 10**9,
+    )
 
     wall, away, keep = run(
         solve_body, scalars,
-        [planes, sent, gains, *span, *back, *strip, const["basis"]],
-        [whole(planes), whole(sent), whole(gains), *span_specs, *back_specs, *strip_specs,
+        [weights, planes, carried_there, opening_there, run8, part, *x_got, log_rho, *span, *back,
+         *strip, const["basis"]],
+        [ORDER, whole(planes), whole(carried_there), whole(opening_there), whole(run8), whole(part),
+         *[whole(a) for a in x_got], log_spec, *span_specs, *back_specs, *strip_specs,
          chosen(const["basis"], 1)],
         [(half, 2 * width), (depth_loc, half, width), (depth_loc, width, half)],
         scratch=[
@@ -621,7 +731,8 @@
         [(depth_loc, half, width)], flops=spectral_flops,
     )
     (pressure,) = run(
-        join_body, scalars, [mine, came], [whole(mine), whole(came)], [pressure_source.shape]
+        join_body, scalars, [mine, came], [plane_of(mine), plane_of(came)], [pressure_source.shape],
+        out_specs=[plane_of(pressure_source)], steps=depth_loc,
     )
     top_planes = pl.BlockSpec((2, tile_rows, width), lambda i, s: (0, 0, 0))
     (final,) = run(

time: 131 us -> 87.7 us (0.67)
  waiting for transfers between devices: 24.1 us -> 5.07 us
  other arithmetic: 10.8 us -> 0 us
  starting transfers between devices: 36.6 us -> 31.8 us
  Pallas kernels: 50.8 us -> 46.5 us
  local copies, waits for them, and re-layouts: 6.33 us -> 3.22 us
    ppermute x21 -> x22, waiting for transfers between devices: 24.1 us -> 5.07 us  [move(): return lax.ppermute(value, ('grp', 'pen'), pairs)]
    ppermute x21 -> x22, starting transfers between devices: 36.6 us -> 31.8 us  [move(): return lax.ppermute(value, ('grp', 'pen'), pairs)]
    pallas_call x9 -> x12, Pallas kernels: 50.8 us -> 46.5 us  [run(): pl.pallas_call(body, out_shape=outs, grid_spec=pltpu.PrefetchScalarGridSp...]
    add x4 -> x0, other arithmetic: 3.46 us -> none  [the longest x1 0.91 us: per_device(): right4 = right4 + power(wide * (Z_RING - 1 - source)) * got[0]]
    unnamed x66 -> x40, local copies, waits for them, and re-layouts: 6.23 us -> 3.13 us
    sub x1 -> x0, other arithmetic: 2.77 us -> none  [per_device(): pressure_source[:, :half] - sign * pressure_source[:, half:]]
    another operation x4 -> x0, other arithmetic: 1.94 us -> none  [the longest x1 0.67 us: per_device(): first = move(jnp.stack([into_low, into_high, right4, left4]), other_half)]
    mul x2 -> x0, other arithmetic: 1.77 us -> none  [the longest x1 0.96 us: per_device(): into_low = gain * (into_low + per_rho * low_sum + hop * high_sum)]
  transfers between devices with their start and end apart: 21 -> 22, of which waited for: 7 -> 5; matrix products, arithmetic and copies ran while one was open for 3% -> 0% of each run, Pallas kernels for 26% -> 34%
where the time goes in v1:
time: 87.7 us; the launch traced here: 87.4 us
  Pallas kernels  46.5 us (53%)
  starting transfers between devices  31.8 us (36%)
  waiting for transfers between devices  5.07 us (6%)
  local copies, waits for them, and re-layouts  3.22 us (4%)
  between operations  0.94 us (1%)
    pallas_call x12, Pallas kernels, run(): pl.pallas_call(body, out_shape=outs, grid_spec=pltpu.PrefetchScalarGridSp...  46.5 us
    ppermute x22, starting transfers between devices, move(): return lax.ppermute(value, ('grp', 'pen'), pairs)  31.8 us
    ppermute x22, waiting for transfers between devices, move(): return lax.ppermute(value, ('grp', 'pen'), pairs)  5.07 us
    unnamed x40, local copies, waits for them, and re-layouts  3.13 us
  transfers between devices with their start and end apart: 22, of which 5 were waited for; matrix products, arithmetic and copies ran while one was open for 0% of the time, Pallas kernels for 34%

profile of v1, /device:TPU:1, one launch (start us, length us, event | category | flops | bytes accessed | tf_op | source)
XLA Modules:
  0.0 87.4 jit_solution(1751668797064719808)
XLA Ops:
  0.6 0.0 copy-start
  0.6 0.0 copy-start.2
  0.7 0.1 stack.29.s_ref
  0.8 1.7 %copy-done.3 = f32[4,1024,128]{2,1,0:T(8,128)S(1)} copy-done((f32[4,1024,128]{2,1,0:T(8,128)S(1)}, f32[4,1024,128]{2,1,0:T(8,128)}, u32[]{:S(2)}) %copy-start.3) | copy-done | bytes 2097176
  2.5 0.7 shard_map.185
  3.3 0.0 copy-start.8
  3.3 0.0 copy-start.9
  3.3 0.0 copy-start.12
  3.3 0.0 copy-start.14
  3.3 0.0 copy-start.15
  3.3 1.5 %collective-permute-start = (f32[4,512,128]{2,1,0:T(8,128)S(1)}, f32[4,512,128]{2,1,0:T(8,128)S(1)}, u32[]{:S(2)}, u32[]{:S(2)}) collective-permute-start(f32[4,512,128]{2,1,0:T(8,128)S(1)} %shard_map.185), channel_id=1, source_target_pairs={{0,32},{1,33},{2,34},{3,35},{4,36},{5,37},{6,38},{7,39},{8,40},{9,... | collective-permute-start | bytes 3145736 | tf_op jit(solution)/shard_map/ppermute | solution.py:587
  4.8 2.1 %shard_map.186.held = f32[4,128,512]{2,1,0:T(8,128)S(1)} custom-call(s32[8]{0:T(128)S(1)} %stack.29.s_ref, f32[4,1024,128]{2,1,0:T(8,128)S(1)} %copy-done.3, bf16[256,256]{1,0:T(8,128)(2,1)S(1)} %copy-done.11, bf16[256,256]{1,0:T(8,128)(2,1)S(1)} %copy-done.10, bf16[2,512,512]{2,1,0:T(8,128)(2,1)S(1)} %copy-done.2, bf16[2,512,512]{2,1,0:T(8,128)(2,1)S(1)} %copy-done), custom_call_target="tpu_custom_call" | custom-call | flops 1006632960 | bytes 7864320 | tf_op jit(solution)/shard_map/pallas_call | solution.py:110
  6.9 0.0 copy-start.4
  6.9 0.0 copy-start.16
  6.9 0.2 collective-permute-done.arrived
  7.1 5.4 %shard_map.187 = (f32[8,128,512]{2,1,0:T(8,128)}, f32[2,16,512]{2,1,0:T(8,128)S(1)}, f32[128,512]{1,0:T(8,128)S(1)}, f32[128,512]{1,0:T(8,128)S(1)}) custom-call(s32[8]{0:T(128)S(1)} %stack.29.s_ref, f32[4,512,128]{2,1,0:T(8,128)S(1)} %collective-permute-done.arrived, f32[4,128,512]{2,1,0:T(8,128)S(1)} %shard_map.186.held, bf16[256,256]{1,0:T(8,128)(2,1)S(1)} %copy-done.11, ...), custom_call_target="tpu_custom_call" | custom-call | flops 1006632960 | bytes 9836544 | tf_op jit(solution)/shard_map/pallas_call | solution.py:110
  12.5 3.9 %collective-permute-start.4 = (f32[2,16,512]{2,1,0:T(8,128)S(1)}, f32[2,16,512]{2,1,0:T(8,128)S(1)}, u32[]{:S(2)}, u32[]{:S(2)}) collective-permute-start(f32[2,16,512]{2,1,0:T(8,128)S(1)} %get-tuple-element.22.after.edges), channel_id=1, source_target_pairs={{0,3},{1,0},{2,1},{3,2},{4,7},{5,4},{6,5},{7,6},{8,11},{9,8},{10,9... | collective-permute-start | bytes 196616 | tf_op jit(solution)/shard_map/ppermute | solution.py:587
  16.4 0.0 collective-permute-start.3
  16.4 0.7 collective-permute-start.2
  17.1 2.9 %collective-permute-start.1 = (f32[128,512]{1,0:T(8,128)S(1)}, f32[128,512]{1,0:T(8,128)S(1)}, u32[]{:S(2)}, u32[]{:S(2)}) collective-permute-start(f32[128,512]{1,0:T(8,128)S(1)} %get-tuple-element.21), channel_id=1, source_target_pairs={{0,64},{1,65},{2,66},{3,67},{4,68},{5,69},{6,70},{7,71},{8,72},{9,... | collective-permute-start | bytes 786440 | tf_op jit(solution)/shard_map/ppermute | solution.py:587
  20.0 4.4 %shard_map.188 = (f32[16,256,128]{2,1,0:T(8,128)S(1)}, f32[64,256]{1,0:T(8,128)S(1)}, f32[2,32,128]{2,1,0:T(8,128)S(1)}) custom-call(s32[8]{0:T(128)S(1)} %stack.29.s_ref, f32[2,16,512]{2,1,0:T(8,128)S(1)} %get-tuple-element.22.after.edges, f32[16,256,128]{2,1,0:T(8,128)S(1)} %copy-done.4, s32[16,256,128]{2,1,0:T(8,128)} %phase.1, f32[2]{0:T(128)S(1)} %copy-done.16), custom_call_target="tpu_custom_call" | custom-call | flops 1000000000 | bytes 6455304 | tf_op jit(solution)/shard_map/pallas_call | solution.py:110
  24.4 0.0 copy-start.17
  24.4 1.3 %copy-done.17 = f32[16,256,128]{2,1,0:T(8,128)} copy-done((f32[16,256,128]{2,1,0:T(8,128)}, f32[16,256,128]{2,1,0:T(8,128)S(1)}, u32[]{:S(2)}) %copy-start.17) | copy-done | bytes 2097176
  25.7 4.3 %collective-permute-start.6 = (f32[64,256]{1,0:T(8,128)S(1)}, f32[64,256]{1,0:T(8,128)S(1)}, u32[]{:S(2)}, u32[]{:S(2)}) collective-permute-start(f32[64,256]{1,0:T(8,128)S(1)} %get-tuple-element.26.packs), channel_id=1, source_target_pairs={{0,31},{1,0},{2,1},{3,2},{4,3},{5,4},{6,5},{7,6},{8,7},{9,8},{10,9... | collective-permute-start | bytes 196616 | tf_op jit(solution)/shard_map/ppermute | solution.py:587
  30.0 0.0 collective-permute-done.4.got3
  30.0 0.0 collective-permute-start.5
  30.0 0.0 collective-permute-done.3.got2
  30.0 1.6 %collective-permute-start.8 = (f32[32,128]{1,0:T(8,128)S(1)}, f32[32,128]{1,0:T(8,128)S(1)}, u32[]{:S(2)}, u32[]{:S(2)}) collective-permute-start(f32[32,128]{1,0:T(8,128)S(1)} %get-tuple-element.40), channel_id=1, source_target_pairs={{0,96},{1,97},{2,98},{3,99},{4,100},{5,101},{6,102},{7,103},{8,104... | collective-permute-start | bytes 49160 | tf_op jit(solution)/shard_map/ppermute | solution.py:587
  31.6 0.0 collective-permute-done.2.got1
  31.6 1.8 %collective-permute-start.7 = (f32[32,128]{1,0:T(8,128)S(1)}, f32[32,128]{1,0:T(8,128)S(1)}, u32[]{:S(2)}, u32[]{:S(2)}) collective-permute-start(f32[32,128]{1,0:T(8,128)S(1)} %get-tuple-element.41), channel_id=1, source_target_pairs={{0,32},{1,33},{2,34},{3,35},{4,36},{5,37},{6,38},{7,39},{8,40},{9,... | collective-permute-start | bytes 49160 | tf_op jit(solution)/shard_map/ppermute | solution.py:587
  33.3 0.0 collective-permute-done.1.wall_there.carried
  33.3 0.6 shard_map.189
  34.0 0.1 collective-permute-start.11
  34.1 0.7 collective-permute-done.8.from_down
  34.7 0.6 collective-permute-start.10
  35.3 0.0 collective-permute-done.7.from_up
  35.3 0.0 collective-permute-done.6.from_right
  35.3 2.0 %collective-permute-done.5.from_left = f32[64,256]{1,0:T(8,128)S(1)} collective-permute-done((f32[64,256]{1,0:T(8,128)S(1)}, f32[64,256]{1,0:T(8,128)S(1)}, u32[]{:S(2)}, u32[]{:S(2)}) %collective-permute-start.5) | collective-permute-done | bytes 65568 | tf_op jit(solution)/shard_map/ppermute | solution.py:587
  37.4 8.4 %shard_map.190 = (f32[16,256,128]{2,1,0:T(8,128)S(1)}, f32[32,256]{1,0:T(8,128)S(1)}, f32[2,16,128]{2,1,0:T(8,128)S(1)}) custom-call(s32[8]{0:T(128)S(1)} %stack.29.s_ref, f32[2,16,512]{2,1,0:T(8,128)S(1)} %get-tuple-element.24.after, f32[16,256,128]{2,1,0:T(8,128)S(1)} %copy-done.4, f32[16,256,128]{2,1,0:T(8,128)} %copy-done.17, f32[256,128]{1,0:T(8,128)S(1)} %copy-done.19, ...), custom_call_target="tpu_custom_call" | custom-call | flops 3000000000 | bytes 6766592 | tf_op jit(solution)/shard_map/pallas_call | solution.py:110
  45.8 4.8 %collective-permute-start.13 = (f32[32,256]{1,0:T(8,128)S(1)}, f32[32,256]{1,0:T(8,128)S(1)}, u32[]{:S(2)}, u32[]{:S(2)}) collective-permute-start(f32[32,256]{1,0:T(8,128)S(1)} %get-tuple-element.31.base_packs), channel_id=1, source_target_pairs={{0,31},{1,0},{2,1},{3,2},{4,3},{5,4},{6,5},{7,6},{8,7},{9,8},{10,9... | collective-permute-start | bytes 98312 | tf_op jit(solution)/shard_map/ppermute | solution.py:587
  50.5 0.0 collective-permute-start.12
  50.5 0.9 %collective-permute-start.9 = (f32[4,16,512]{2,1,0:T(8,128)S(1)}, f32[4,16,512]{2,1,0:T(8,128)S(1)}, u32[]{:S(2)}, u32[]{:S(2)}) collective-permute-start(f32[4,16,512]{2,1,0:T(8,128)S(1)} %get-tuple-element.28.four), channel_id=1, source_target_pairs={{0,64},{1,65},{2,66},{3,67},{4,68},{5,69},{6,70},{7,71},{8,72},{9,... | collective-permute-start | bytes 393224 | tf_op jit(solution)/shard_map/ppermute | solution.py:587
  51.4 0.0 collective-permute-done.11.beside2
  51.4 2.0 %collective-permute-start.15 = (f32[16,128]{1,0:T(8,128)S(1)}, f32[16,128]{1,0:T(8,128)S(1)}, u32[]{:S(2)}, u32[]{:S(2)}) collective-permute-start(f32[16,128]{1,0:T(8,128)S(1)} %get-tuple-element.42), channel_id=1, source_target_pairs={{0,96},{1,97},{2,98},{3,99},{4,100},{5,101},{6,102},{7,103},{8,104... | collective-permute-start | bytes 24584 | tf_op jit(solution)/shard_map/ppermute | solution.py:587
  53.4 1.3 %collective-permute-start.14 = (f32[16,128]{1,0:T(8,128)S(1)}, f32[16,128]{1,0:T(8,128)S(1)}, u32[]{:S(2)}, u32[]{:S(2)}) collective-permute-start(f32[16,128]{1,0:T(8,128)S(1)} %get-tuple-element.43), channel_id=1, source_target_pairs={{0,32},{1,33},{2,34},{3,35},{4,36},{5,37},{6,38},{7,39},{8,40},{9,... | collective-permute-start | bytes 24584 | tf_op jit(solution)/shard_map/ppermute | solution.py:587
  54.7 1.9 %collective-permute-done.9.there = f32[4,16,512]{2,1,0:T(8,128)S(1)} collective-permute-done((f32[4,16,512]{2,1,0:T(8,128)S(1)}, f32[4,16,512]{2,1,0:T(8,128)S(1)}, u32[]{:S(2)}, u32[]{:S(2)}) %collective-permute-start.9) | collective-permute-done | bytes 131104 | tf_op jit(solution)/shard_map/ppermute | solution.py:587
  56.7 0.1 collective-permute-start.16
  56.8 0.6 shard_map.191
  57.4 0.2 collective-permute-done.15.base_down
  57.6 0.1 collective-permute-start.19
  57.7 0.0 collective-permute-start.18
  57.7 1.6 %collective-permute-start.17 = (f32[2,16,512]{2,1,0:T(8,128)S(1)}, f32[2,16,512]{2,1,0:T(8,128)S(1)}, u32[]{:S(2)}, u32[]{:S(2)}) collective-permute-start(f32[2,16,512]{2,1,0:T(8,128)S(1)} %get-tuple-element.29.after.run8), channel_id=1, source_target_pairs={{0,8},{1,9},{2,10},{3,11},{4,12},{5,13},{6,14},{7,15},{8,16},{9,17... | collective-permute-start | bytes 196616 | tf_op jit(solution)/shard_map/ppermute | solution.py:587
  59.3 0.0 collective-permute-done.12.base_left
  59.3 0.0 copy-start.13
  59.3 8.1 %shard_map.192 = (f32[16,256,128]{2,1,0:T(8,128)}, f32[5,256,128]{2,1,0:T(8,128)S(1)}) custom-call(s32[8]{0:T(128)S(1)} %stack.29.s_ref, f32[2,16,512]{2,1,0:T(8,128)S(1)} %get-tuple-element.29.after.run8, f32[16,256,128]{2,1,0:T(8,128)S(1)} %get-tuple-element.30.base, f32[16,256,128]{2,1,0:T(8,128)S(1)} %copy-done.18, f32[16,256,128]{2,1,0:T(8,128)} %temp.5, ...), custom_call_target="tpu_custom_call" | custom-call | flops 3000000000 | bytes 9584640 | tf_op jit(solution)/shard_map/pallas_call | solution.py:110
  67.5 0.0 collective-permute-done.18.got2
  67.5 0.0 collective-permute-done.17.got1
  67.5 0.0 copy-start.1
  67.5 8.1 %shard_map.193 = (f32[512,256]{1,0:T(8,128)S(1)}, f32[4,512,128]{2,1,0:T(8,128)S(1)}, f32[4,128,512]{2,1,0:T(8,128)S(1)}) custom-call(s32[8]{0:T(128)S(1)} %stack.29.s_ref, f32[5,256,128]{2,1,0:T(8,128)S(1)} %get-tuple-element.32.after.weights, f32[8,128,512]{2,1,0:T(8,128)} %get-tuple-element.33.planes, ...), custom_call_target="tpu_custom_call" | custom-call | flops 1006632960 | bytes 11278336 | tf_op jit(solution)/shard_map/pallas_call | solution.py:110
  75.7 3.7 %collective-permute-start.20 = (f32[4,512,128]{2,1,0:T(8,128)S(1)}, f32[4,512,128]{2,1,0:T(8,128)S(1)}, u32[]{:S(2)}, u32[]{:S(2)}) collective-permute-start(f32[4,512,128]{2,1,0:T(8,128)S(1)} %get-tuple-element.37), channel_id=1, source_target_pairs={{0,32},{1,33},{2,34},{3,35},{4,36},{5,37},{6,38},{7,39},{8,40},{9,... | collective-permute-start | bytes 3145736 | tf_op jit(solution)/shard_map/ppermute | solution.py:587
  79.4 0.1 collective-permute-start.21
  79.5 3.1 %shard_map.194.mine = f32[4,512,128]{2,1,0:T(8,128)S(1)} custom-call(s32[8]{0:T(128)S(1)} %stack.29.s_ref, f32[4,128,512]{2,1,0:T(8,128)S(1)} %get-tuple-element.36.keep, bf16[2,512,512]{2,1,0:T(8,128)(2,1)S(1)} %copy-done.2, bf16[2,512,512]{2,1,0:T(8,128)(2,1)S(1)} %copy-done.1, bf16[256,256]{1,0:T(8,128)(2,1)S(1)} %copy-done.7, bf16[256,256]{1,0:T(8,128)(2,1)S(1)} %copy-done.6), custom_call_target="tpu_custom_call" | custom-call | flops 1006632960 | bytes 6815744 | tf_op jit(solution)/shard_map/pallas_call | solution.py:110
  82.6 2.4 %shard_map.196 = f32[16,256,128]{2,1,0:T(8,128)} custom-call(s32[8]{0:T(128)S(1)} %stack.29.s_ref, f32[512,256]{1,0:T(8,128)S(1)} %get-tuple-element.38.ours, f32[512,256]{1,0:T(8,128)S(1)} %collective-permute-done.21.theirs, f32[5,256,128]{2,1,0:T(8,128)S(1)} %get-tuple-element.32.after.weights, ...), custom_call_target="tpu_custom_call", output_to_operand_aliasing={{}: (4, {})} | custom-call | bytes 5898240 | tf_op jit(solution)/shard_map/pallas_call | solution.py:110
  85.0 2.4 %shard_map.195 = f32[4,1024,128]{2,1,0:T(8,128)} custom-call(s32[8]{0:T(128)S(1)} %stack.29.s_ref, f32[4,512,128]{2,1,0:T(8,128)S(1)} %shard_map.194.mine, f32[4,512,128]{2,1,0:T(8,128)S(1)} %collective-permute-done.20.came), custom_call_target="tpu_custom_call" | custom-call | bytes 4194304 | tf_op jit(solution)/shard_map/pallas_call | solution.py:110
  (35 shorter events, 0.1 us)
Async XLA Ops:
  0.6 4.2 %copy-start = (bf16[2,512,512]{2,1,0:T(8,128)(2,1)S(1)}, bf16[2,512,512]{2,1,0:T(8,128)(2,1)}, u32[]{:S(2)}) copy-start(bf16[2,512,512]{2,1,0:T(8,128)(2,1)} %constant.94.clone.span_low) | copy-start | bytes 3145732
  0.6 4.2 %copy-start.2 = (bf16[2,512,512]{2,1,0:T(8,128)(2,1)S(1)}, bf16[2,512,512]{2,1,0:T(8,128)(2,1)}, u32[]{:S(2)}) copy-start(bf16[2,512,512]{2,1,0:T(8,128)(2,1)} %constant.93.clone.span_high) | copy-start | bytes 3145732
  0.8 1.7 %copy-start.3 = (f32[4,1024,128]{2,1,0:T(8,128)S(1)}, f32[4,1024,128]{2,1,0:T(8,128)}, u32[]{:S(2)}) copy-start(f32[4,1024,128]{2,1,0:T(8,128)} %source.3) | copy-start | bytes 6291460
  2.5 2.3 %copy-start.10 = (bf16[256,256]{1,0:T(8,128)(2,1)S(1)}, bf16[256,256]{1,0:T(8,128)(2,1)}, u32[]{:S(2)}) copy-start(bf16[256,256]{1,0:T(8,128)(2,1)} %constant.96.clone.into_low) | copy-start | bytes 393220
  2.5 2.3 %copy-start.11 = (bf16[256,256]{1,0:T(8,128)(2,1)S(1)}, bf16[256,256]{1,0:T(8,128)(2,1)}, u32[]{:S(2)}) copy-start(bf16[256,256]{1,0:T(8,128)(2,1)} %constant.95.clone.into_high) | copy-start | bytes 393220
  3.3 3.9 %copy-start.8 = (f32[128,256]{1,0:T(8,128)S(1)}, f32[128,256]{1,0:T(8,128)}, u32[]{:S(2)}) copy-start(f32[128,256]{1,0:T(8,128)} %constant.101.clone.edge) | copy-start | bytes 393220
  3.3 3.8 %copy-start.9 = (f32[128,256]{1,0:T(8,128)S(1)}, f32[128,256]{1,0:T(8,128)}, u32[]{:S(2)}) copy-start(f32[128,256]{1,0:T(8,128)} %constant.100.clone.sigma) | copy-start | bytes 393220
  3.3 3.8 %copy-start.12 = (f32[2,16,512]{2,1,0:T(8,128)S(1)}, f32[2,16,512]{2,1,0:T(8,128)}, u32[]{:S(2)}) copy-start(f32[2,16,512]{2,1,0:T(8,128)} %constant.105.clone.far) | copy-start | bytes 196612
  3.3 3.8 %copy-start.14 = (f32[2,16,16]{2,1,0:T(8,128)S(1)}, f32[2,16,16]{2,1,0:T(8,128)}, u32[]{:S(2)}) copy-start(f32[2,16,16]{2,1,0:T(8,128)} %constant.103.clone.basis_t) | copy-start | bytes 6148
  3.3 3.8 %copy-start.15 = (f32[2,1,512]{2,1,0:T(1,128)S(1)}, f32[2,1,512]{2,1,0:T(1,128)}, u32[]{:S(2)}) copy-start(f32[2,1,512]{2,1,0:T(1,128)} %constant.99.clone.lam) | copy-start | bytes 12292
  3.3 3.8 %collective-permute-start = (f32[4,512,128]{2,1,0:T(8,128)S(1)}, f32[4,512,128]{2,1,0:T(8,128)S(1)}, u32[]{:S(2)}, u32[]{:S(2)}) collective-permute-start(f32[4,512,128]{2,1,0:T(8,128)S(1)} %shard_map.185), channel_id=1, source_target_pairs={{0,32},{1,33},{2,34},{3,35},{4,36},{5,37},{6,38},{7,39},{8,40},{9,... | collective-permute-start | bytes 3145736 | tf_op jit(solution)/shard_map/ppermute | solution.py:587
  6.9 13.1 %copy-start.4 = (f32[16,256,128]{2,1,0:T(8,128)S(1)}, f32[16,256,128]{2,1,0:T(8,128)}, u32[]{:S(2)}) copy-start(f32[16,256,128]{2,1,0:T(8,128)} %temp.5) | copy-start | bytes 6291460
  6.9 13.0 %copy-start.16 = (f32[2]{0:T(128)S(1)}, f32[2]{0:T(128)}, u32[]{:S(2)}) copy-start(f32[2]{0:T(128)} %conductivity.1) | copy-start | bytes 28
  12.5 17.5 %collective-permute-start.4 = (f32[2,16,512]{2,1,0:T(8,128)S(1)}, f32[2,16,512]{2,1,0:T(8,128)S(1)}, u32[]{:S(2)}, u32[]{:S(2)}) collective-permute-start(f32[2,16,512]{2,1,0:T(8,128)S(1)} %get-tuple-element.22.after.edges), channel_id=1, source_target_pairs={{0,3},{1,0},{2,1},{3,2},{4,7},{5,4},{6,5},{7,6},{8,11},{9,8},{10,9... | collective-permute-start | bytes 196616 | tf_op jit(solution)/shard_map/ppermute | solution.py:587
  16.4 13.6 %collective-permute-start.3 = (f32[2,16,512]{2,1,0:T(8,128)S(1)}, f32[2,16,512]{2,1,0:T(8,128)S(1)}, u32[]{:S(2)}, u32[]{:S(2)}) collective-permute-start(f32[2,16,512]{2,1,0:T(8,128)S(1)} %get-tuple-element.22.after.edges), channel_id=1, source_target_pairs={{0,2},{1,3},{2,0},{3,1},{4,6},{5,7},{6,4},{7,5},{8,10},{9,11},{10,... | collective-permute-start | bytes 196616 | tf_op jit(solution)/shard_map/ppermute | solution.py:587
  16.4 15.2 %collective-permute-start.2 = (f32[2,16,512]{2,1,0:T(8,128)S(1)}, f32[2,16,512]{2,1,0:T(8,128)S(1)}, u32[]{:S(2)}, u32[]{:S(2)}) collective-permute-start(f32[2,16,512]{2,1,0:T(8,128)S(1)} %get-tuple-element.22.after.edges), channel_id=1, source_target_pairs={{0,1},{1,2},{2,3},{3,0},{4,5},{5,6},{6,7},{7,4},{8,9},{9,10},{10,1... | collective-permute-start | bytes 196616 | tf_op jit(solution)/shard_map/ppermute | solution.py:587
  17.1 16.3 %copy-start.5 = (f32[2,16,512]{2,1,0:T(8,128)S(1)}, f32[2,16,512]{2,1,0:T(8,128)}, u32[]{:S(2)}) copy-start(f32[2,16,512]{2,1,0:T(8,128)} %constant.104.clone.log_rho) | copy-start | bytes 196612
  17.1 20.3 %copy-start.19 = (f32[256,128]{1,0:T(8,128)S(1)}, f32[256,128]{1,0:T(8,128)}, u32[]{:S(2)}) copy-start(f32[256,128]{1,0:T(8,128)} %gas.3) | copy-start | bytes 393220
  17.1 16.3 %collective-permute-start.1 = (f32[128,512]{1,0:T(8,128)S(1)}, f32[128,512]{1,0:T(8,128)S(1)}, u32[]{:S(2)}, u32[]{:S(2)}) collective-permute-start(f32[128,512]{1,0:T(8,128)S(1)} %get-tuple-element.21), channel_id=1, source_target_pairs={{0,64},{1,65},{2,66},{3,67},{4,68},{5,69},{6,70},{7,71},{8,72},{9,... | collective-permute-start | bytes 786440 | tf_op jit(solution)/shard_map/ppermute | solution.py:587
  24.4 1.3 %copy-start.17 = (f32[16,256,128]{2,1,0:T(8,128)}, f32[16,256,128]{2,1,0:T(8,128)S(1)}, u32[]{:S(2)}) copy-start(f32[16,256,128]{2,1,0:T(8,128)S(1)} %get-tuple-element.25.cond) | copy-start | bytes 6291460
  25.7 9.6 %collective-permute-start.6 = (f32[64,256]{1,0:T(8,128)S(1)}, f32[64,256]{1,0:T(8,128)S(1)}, u32[]{:S(2)}, u32[]{:S(2)}) collective-permute-start(f32[64,256]{1,0:T(8,128)S(1)} %get-tuple-element.26.packs), channel_id=1, source_target_pairs={{0,31},{1,0},{2,1},{3,2},{4,3},{5,4},{6,5},{7,6},{8,7},{9,8},{10,9... | collective-permute-start | bytes 196616 | tf_op jit(solution)/shard_map/ppermute | solution.py:587
  30.0 7.4 %collective-permute-start.5 = (f32[64,256]{1,0:T(8,128)S(1)}, f32[64,256]{1,0:T(8,128)S(1)}, u32[]{:S(2)}, u32[]{:S(2)}) collective-permute-start(f32[64,256]{1,0:T(8,128)S(1)} %get-tuple-element.26.packs), channel_id=1, source_target_pairs={{0,1},{1,2},{2,3},{3,4},{4,5},{5,6},{6,7},{7,8},{8,9},{9,10},{10,1... | collective-permute-start | bytes 196616 | tf_op jit(solution)/shard_map/ppermute | solution.py:587
  30.0 4.7 %collective-permute-start.8 = (f32[32,128]{1,0:T(8,128)S(1)}, f32[32,128]{1,0:T(8,128)S(1)}, u32[]{:S(2)}, u32[]{:S(2)}) collective-permute-start(f32[32,128]{1,0:T(8,128)S(1)} %get-tuple-element.40), channel_id=1, source_target_pairs={{0,96},{1,97},{2,98},{3,99},{4,100},{5,101},{6,102},{7,103},{8,104... | collective-permute-start | bytes 49160 | tf_op jit(solution)/shard_map/ppermute | solution.py:587
  31.6 3.7 %collective-permute-start.7 = (f32[32,128]{1,0:T(8,128)S(1)}, f32[32,128]{1,0:T(8,128)S(1)}, u32[]{:S(2)}, u32[]{:S(2)}) collective-permute-start(f32[32,128]{1,0:T(8,128)S(1)} %get-tuple-element.41), channel_id=1, source_target_pairs={{0,32},{1,33},{2,34},{3,35},{4,36},{5,37},{6,38},{7,39},{8,40},{9,... | collective-permute-start | bytes 49160 | tf_op jit(solution)/shard_map/ppermute | solution.py:587
  34.0 17.5 %collective-permute-start.11 = (f32[2,16,512]{2,1,0:T(8,128)S(1)}, f32[2,16,512]{2,1,0:T(8,128)S(1)}, u32[]{:S(2)}, u32[]{:S(2)}) collective-permute-start(f32[2,16,512]{2,1,0:T(8,128)S(1)} %get-tuple-element.24.after), channel_id=1, source_target_pairs={{0,68},{1,69},{2,70},{3,71},{4,64},{5,65},{6,66},{7,67},{8,76},{9,... | collective-permute-start | bytes 196616 | tf_op jit(solution)/shard_map/ppermute | solution.py:587
  34.7 18.7 %collective-permute-start.10 = (f32[2,16,512]{2,1,0:T(8,128)S(1)}, f32[2,16,512]{2,1,0:T(8,128)S(1)}, u32[]{:S(2)}, u32[]{:S(2)}) collective-permute-start(f32[2,16,512]{2,1,0:T(8,128)S(1)} %get-tuple-element.24.after), channel_id=1, source_target_pairs={{0,4},{1,5},{2,6},{3,7},{4,0},{5,1},{6,2},{7,3},{8,12},{9,13},{10,... | collective-permute-start | bytes 196616 | tf_op jit(solution)/shard_map/ppermute | solution.py:587
  37.4 21.9 %copy-start.18 = (f32[16,256,128]{2,1,0:T(8,128)S(1)}, f32[16,256,128]{2,1,0:T(8,128)}, u32[]{:S(2)}) copy-start(f32[16,256,128]{2,1,0:T(8,128)} %copy-done.17) | copy-start | bytes 6291460
  45.8 11.9 %collective-permute-start.13 = (f32[32,256]{1,0:T(8,128)S(1)}, f32[32,256]{1,0:T(8,128)S(1)}, u32[]{:S(2)}, u32[]{:S(2)}) collective-permute-start(f32[32,256]{1,0:T(8,128)S(1)} %get-tuple-element.31.base_packs), channel_id=1, source_target_pairs={{0,31},{1,0},{2,1},{3,2},{4,3},{5,4},{6,5},{7,6},{8,7},{9,8},{10,9... | collective-permute-start | bytes 98312 | tf_op jit(solution)/shard_map/ppermute | solution.py:587
  50.5 8.8 %collective-permute-start.12 = (f32[32,256]{1,0:T(8,128)S(1)}, f32[32,256]{1,0:T(8,128)S(1)}, u32[]{:S(2)}, u32[]{:S(2)}) collective-permute-start(f32[32,256]{1,0:T(8,128)S(1)} %get-tuple-element.31.base_packs), channel_id=1, source_target_pairs={{0,1},{1,2},{2,3},{3,4},{4,5},{5,6},{6,7},{7,8},{8,9},{9,10},{10,1... | collective-permute-start | bytes 98312 | tf_op jit(solution)/shard_map/ppermute | solution.py:587
  50.5 6.1 %collective-permute-start.9 = (f32[4,16,512]{2,1,0:T(8,128)S(1)}, f32[4,16,512]{2,1,0:T(8,128)S(1)}, u32[]{:S(2)}, u32[]{:S(2)}) collective-permute-start(f32[4,16,512]{2,1,0:T(8,128)S(1)} %get-tuple-element.28.four), channel_id=1, source_target_pairs={{0,64},{1,65},{2,66},{3,67},{4,68},{5,69},{6,70},{7,71},{8,72},{9,... | collective-permute-start | bytes 393224 | tf_op jit(solution)/shard_map/ppermute | solution.py:587
  51.4 6.1 %collective-permute-start.15 = (f32[16,128]{1,0:T(8,128)S(1)}, f32[16,128]{1,0:T(8,128)S(1)}, u32[]{:S(2)}, u32[]{:S(2)}) collective-permute-start(f32[16,128]{1,0:T(8,128)S(1)} %get-tuple-element.42), channel_id=1, source_target_pairs={{0,96},{1,97},{2,98},{3,99},{4,100},{5,101},{6,102},{7,103},{8,104... | collective-permute-start | bytes 24584 | tf_op jit(solution)/shard_map/ppermute | solution.py:587
  53.4 4.3 %collective-permute-start.14 = (f32[16,128]{1,0:T(8,128)S(1)}, f32[16,128]{1,0:T(8,128)S(1)}, u32[]{:S(2)}, u32[]{:S(2)}) collective-permute-start(f32[16,128]{1,0:T(8,128)S(1)} %get-tuple-element.43), channel_id=1, source_target_pairs={{0,32},{1,33},{2,34},{3,35},{4,36},{5,37},{6,38},{7,39},{8,40},{9,... | collective-permute-start | bytes 24584 | tf_op jit(solution)/shard_map/ppermute | solution.py:587
  56.7 10.8 %collective-permute-start.16 = (f32[128,512]{1,0:T(8,128)S(1)}, f32[128,512]{1,0:T(8,128)S(1)}, u32[]{:S(2)}, u32[]{:S(2)}) collective-permute-start(f32[128,512]{1,0:T(8,128)S(1)} %get-tuple-element.34), channel_id=1, source_target_pairs={{0,64},{1,65},{2,66},{3,67},{4,68},{5,69},{6,70},{7,71},{8,72},{9,... | collective-permute-start | bytes 786440 | tf_op jit(solution)/shard_map/ppermute | solution.py:587
  57.6 9.9 %collective-permute-start.19 = (f32[2,16,512]{2,1,0:T(8,128)S(1)}, f32[2,16,512]{2,1,0:T(8,128)S(1)}, u32[]{:S(2)}, u32[]{:S(2)}) collective-permute-start(f32[2,16,512]{2,1,0:T(8,128)S(1)} %get-tuple-element.29.after.run8), channel_id=1, source_target_pairs={{0,24},{1,25},{2,26},{3,27},{4,28},{5,29},{6,30},{7,31},{8,0},{9,1... | collective-permute-start | bytes 196616 | tf_op jit(solution)/shard_map/ppermute | solution.py:587
  57.7 9.8 %collective-permute-start.18 = (f32[2,16,512]{2,1,0:T(8,128)S(1)}, f32[2,16,512]{2,1,0:T(8,128)S(1)}, u32[]{:S(2)}, u32[]{:S(2)}) collective-permute-start(f32[2,16,512]{2,1,0:T(8,128)S(1)} %get-tuple-element.29.after.run8), channel_id=1, source_target_pairs={{0,16},{1,17},{2,18},{3,19},{4,20},{5,21},{6,22},{7,23},{8,24},{9,... | collective-permute-start | bytes 196616 | tf_op jit(solution)/shard_map/ppermute | solution.py:587
  57.7 9.8 %collective-permute-start.17 = (f32[2,16,512]{2,1,0:T(8,128)S(1)}, f32[2,16,512]{2,1,0:T(8,128)S(1)}, u32[]{:S(2)}, u32[]{:S(2)}) collective-permute-start(f32[2,16,512]{2,1,0:T(8,128)S(1)} %get-tuple-element.29.after.run8), channel_id=1, source_target_pairs={{0,8},{1,9},{2,10},{3,11},{4,12},{5,13},{6,14},{7,15},{8,16},{9,17... | collective-permute-start | bytes 196616 | tf_op jit(solution)/shard_map/ppermute | solution.py:587
  59.3 8.2 %copy-start.6 = (bf16[256,256]{1,0:T(8,128)(2,1)S(1)}, bf16[256,256]{1,0:T(8,128)(2,1)}, u32[]{:S(2)}) copy-start(bf16[256,256]{1,0:T(8,128)(2,1)} %constant.98.clone.back_low) | copy-start | bytes 393220
  59.3 8.2 %copy-start.7 = (bf16[256,256]{1,0:T(8,128)(2,1)S(1)}, bf16[256,256]{1,0:T(8,128)(2,1)}, u32[]{:S(2)}) copy-start(bf16[256,256]{1,0:T(8,128)(2,1)} %constant.97.clone.back_high) | copy-start | bytes 393220
  59.3 8.2 %copy-start.13 = (f32[2,16,16]{2,1,0:T(8,128)S(1)}, f32[2,16,16]{2,1,0:T(8,128)}, u32[]{:S(2)}) copy-start(f32[2,16,16]{2,1,0:T(8,128)} %constant.102.clone.basis) | copy-start | bytes 6148
  67.5 11.9 %copy-start.1 = (bf16[2,512,512]{2,1,0:T(8,128)(2,1)S(1)}, bf16[2,512,512]{2,1,0:T(8,128)(2,1)}, u32[]{:S(2)}) copy-start(bf16[2,512,512]{2,1,0:T(8,128)(2,1)} %constant.94.clone.span_low) | copy-start | bytes 3145732
  75.7 9.4 %collective-permute-start.20 = (f32[4,512,128]{2,1,0:T(8,128)S(1)}, f32[4,512,128]{2,1,0:T(8,128)S(1)}, u32[]{:S(2)}, u32[]{:S(2)}) collective-permute-start(f32[4,512,128]{2,1,0:T(8,128)S(1)} %get-tuple-element.37), channel_id=1, source_target_pairs={{0,32},{1,33},{2,34},{3,35},{4,36},{5,37},{6,38},{7,39},{8,40},{9,... | collective-permute-start | bytes 3145736 | tf_op jit(solution)/shard_map/ppermute | solution.py:587
  79.4 3.2 %collective-permute-start.21 = (f32[512,256]{1,0:T(8,128)S(1)}, f32[512,256]{1,0:T(8,128)S(1)}, u32[]{:S(2)}, u32[]{:S(2)}) collective-permute-start(f32[512,256]{1,0:T(8,128)S(1)} %get-tuple-element.38.ours), channel_id=1, source_target_pairs={{0,32},{1,33},{2,34},{3,35},{4,36},{5,37},{6,38},{7,39},{8,40},{9,... | collective-permute-start | bytes 1572872 | tf_op jit(solution)/shard_map/ppermute | solution.py:587

commit v2 on v1

v2 whole, which is shorter than its diff:
```python
import functools
import math

import jax
import jax.numpy as jnp
import numpy as np
from jax import lax
from jax.experimental import pallas as pl
from jax.experimental.pallas import tpu as pltpu
from jax.sharding import PartitionSpec as P

HIGHEST = lax.Precision.HIGHEST
HEAT_TRANSFER = 1.0
PRESSURE_WORK = 0.5
STEP_RATE = 0.12
Z_RING, Y_PAIR, X_RING = 4, 2, 4
VMEM_LIMIT = 18 * 1024 * 1024
BLOCK_LIMIT = 16 * 1024 * 1024
LANES = 512
CHUNK = 32
COST_SCALE = 0.1


def halves(value):
    high = np.asarray(value, np.float32).astype(jnp.bfloat16)
    low = (np.asarray(value, np.float64) - high.astype(np.float64)).astype(jnp.bfloat16)
    return high, low


def make_tables(span_len, width, depth):
    half = span_len // 2
    waves = np.stack([2 * np.arange(half), 2 * np.arange(half) + 1]).astype(np.float64)
    rows = np.arange(half)
    angle = 2 * np.pi * ((rows[None, :, None] * waves[:, None, :]) % span_len) / span_len
    span = np.cos(angle) + np.sin(angle)
    lam = -4 * np.sin(np.pi * waves / span_len) ** 2
    order = np.concatenate([np.arange(0, width, 2), np.arange(1, width, 2)]) + 1.0
    cells = np.arange(width) + 1.0
    sine = np.sqrt(2 / (width + 1)) * np.sin(np.pi * cells[:, None] * order[None, :] / (width + 1))
    sigma = -4 * np.sin(np.pi * order / (2 * (width + 1))) ** 2
    modes = np.arange(depth)
    theta = np.pi * (2 * modes + 1) / (2 * depth + 1)
    basis = np.cos(theta[None, :] * (np.arange(depth)[:, None] + 0.5)) / np.sqrt((2 * depth + 1) / 4)
    mu = -4 * np.sin(theta / 2) ** 2
    stretch = -(mu[None, :, None] + lam[:, None, :])
    log_rho = -2 * np.arcsinh(np.sqrt(stretch) / 2)
    down = np.arange(depth // 2)
    up = depth - 1 - down
    ordered = np.stack([basis[np.concatenate([down, up])], basis[np.concatenate([up, down])]])
    pair = np.kron(np.eye(2), sine)
    f32 = lambda v: np.asarray(v, np.float32)
    lanes = min(LANES, half)
    return {
        "span": halves(span),
        "span_t": halves(np.swapaxes(span, 1, 2)),
        "into": halves(pair / span_len),
        "back": halves(pair.T),
        "lam": f32(lam)[:, None, :],
        "sigma": f32(np.repeat(sigma[:, None], lanes, 1)),
        "edge": f32(np.repeat(sine[0][:, None], lanes, 1)),
        "basis": f32(ordered),
        "basis_t": f32(np.swapaxes(ordered, 1, 2)),
        "log_rho": f32(log_rho),
        "far": f32(np.exp(log_rho * (width + 1))),
    }


def product(first, second):
    return jnp.dot(first, second, preferred_element_type=jnp.float32)


def split(value):
    high = value.astype(jnp.bfloat16)
    return high, (value - high.astype(jnp.float32)).astype(jnp.bfloat16)


def times(value, high, low):
    value_high, value_low = split(value)
    return product(value_high, high) + (product(value_high, low) + product(value_low, high))


def times_turned(high, low, value):
    value_high, value_low = split(value)
    turned = lambda a, b: lax.dot_general(
        a, b, (((1,), (1,)), ((), ())), preferred_element_type=jnp.float32
    )
    return turned(high, value_high) + (turned(low, value_high) + turned(high, value_low))


ORDER = pl.BlockSpec(memory_space=pl.ANY)
SCALARS = pl.BlockSpec(memory_space=pltpu.SMEM)
FAST = pl.BlockSpec(memory_space=pltpu.VMEM)


def plane_of(array):
    rest = array.shape[1:]
    return pl.BlockSpec((1,) + rest, lambda i, s: (i,) + (0,) * len(rest))


def cost(time_us):
    return pl.CostEstimate(flops=1, bytes_accessed=int(time_us * 3.69e6 * COST_SCALE), transcendentals=0)


def run(body, time_us, scalars, ordered, arrays, outs, scratch=(), small=(), out_specs=None, aliases=None):
    outs = [jax.ShapeDtypeStruct(shape, jnp.float32) for shape in outs]
    skip = len(ordered)
    count = len(small)
    kinds = [FAST if spec is None else spec for spec in (a[1] if type(a) is tuple else None for a in arrays)]
    arrays = [a[0] if type(a) is tuple else a for a in arrays]
    specs = [SCALARS] + [SCALARS] * count + [ORDER] * skip + kinds

    def inner(s_ref, *refs):
        body(s_ref, *refs[:count], *refs[count + skip :])

    return pl.pallas_call(
        inner,
        out_shape=outs,
        in_specs=specs,
        out_specs=out_specs or [FAST] * len(outs),
        scratch_shapes=list(scratch),
        input_output_aliases=aliases or {},
        compiler_params=pltpu.CompilerParams(vmem_limit_bytes=VMEM_LIMIT),
        cost_estimate=cost(time_us),
    )(scalars, *small, *ordered, *arrays)


def run_blocks(body, time_us, scalars, arrays, specs, outs, out_specs, steps):
    return pl.pallas_call(
        body,
        out_shape=[jax.ShapeDtypeStruct(out, jnp.float32) for out in outs],
        grid_spec=pltpu.PrefetchScalarGridSpec(
            num_scalar_prefetch=1, grid=(steps,), in_specs=specs, out_specs=out_specs
        ),
        compiler_params=pltpu.CompilerParams(vmem_limit_bytes=BLOCK_LIMIT),
        cost_estimate=cost(time_us),
    )(scalars, *arrays)


def fold_body(s_ref, after, source, away, kept):
    half = source.shape[1] // 2
    sign = (1 - 2 * s_ref[0]).astype(jnp.float32)
    upper = source[:, :half]
    lower = sign * source[:, half:]
    away[...] = upper - lower
    kept[...] = upper + lower


def spectral(planes, into_high, into_low, span_high, span_low):
    turned = []
    for pair in range(0, len(planes), 2):
        cells = jnp.concatenate(planes[pair : pair + 2], axis=1)
        turned.append(times(cells, into_high, into_low).T)
    return times(jnp.concatenate(turned, axis=0), span_high, span_low)


def held_body(s_ref, kept, into_high, into_low, span_high, span_low, out):
    out[...] = spectral(
        [kept[z] for z in range(kept.shape[0])], into_high[...], into_low[...],
        span_high[s_ref[0]], span_low[s_ref[0]],
    ).reshape(out.shape)


def continuants(centre, first, count):
    values = [jnp.ones_like(centre), centre + first]
    for _ in range(1, count):
        values.append(centre * values[-1] - values[-2])
    return values


def pivot_body(s_ref, lam, sigma, out):
    own = (out.shape[0] - 2) // 3
    width = out.shape[1]
    low = s_ref[1].astype(jnp.float32)

    def tile(group, nothing):
        rows = pl.ds(pl.multiple_of(group * 8, 8), 8)
        centre = lam[s_ref[0]] + sigma[rows] - 2.0
        mine = continuants(centre, 1.0 - low, own)
        other = continuants(centre, low, own)
        for i in range(own):
            out[i, rows] = mine[i + 1]
            out[own + i, rows] = other[i + 1]
            out[2 * own + i, rows] = 1.0 / mine[i + 1]
        out[3 * own, rows] = 1.0 / (mine[own] * other[own] - mine[own - 1] * other[own - 1])
        out[3 * own + 1, rows] = 1.0 / other[own]
        return nothing

    lax.fori_loop(0, width // 8, tile, 0)


def arrived_body(
    s_ref, arrived, held, into_high, into_low, span_high, span_low, pivots, edge, basis_t, far,
    planes, edges, carried, opening, sums,
):
    count = held.shape[0]
    own = 2 * count
    width, half = held.shape[1:]
    planes[:count] = held[...]
    planes[count:] = spectral(
        [arrived[z] for z in range(count)], into_high[...], into_low[...],
        span_high[s_ref[0]], span_low[s_ref[0]],
    ).reshape(held.shape)
    sums[...] = jnp.zeros_like(sums)
    code = s_ref[2]
    side = width // 16

    def tile(group, nothing):
        rows = pl.ds(pl.multiple_of(group * 8, 8), 8)
        parity = group // side
        carry = planes[code, rows]
        carries = [carry]
        for i in range(1, own):
            carry = pivots[i - 1, rows] * planes[jnp.bitwise_xor(i, code), rows] - carry
            carries.append(carry)
        carried[rows] = carry
        shared = carry * pivots[3 * own, rows]
        scale = edge[rows]
        value = shared * pivots[2 * own - 1, rows]
        sums[parity, own - 1] += scale * value
        for i in range(own - 2, -1, -1):
            step = value if i == 0 else pivots[i - 1, rows] * value
            value = (carries[i] - step) * pivots[2 * own + i, rows]
            sums[parity, i] += scale * value
        opening[rows] = value + pivots[2 * own - 2, rows] * shared * pivots[3 * own - 1, rows]
        shared = scale * shared
        for i in range(own):
            term = shared if i == 0 else pivots[own + i - 1, rows] * shared
            sums[parity, own + i] += term if (own - i) % 2 == 0 else -term
        return nothing

    lax.fori_loop(0, width // 8, tile, 0)
    total = jnp.sum(sums[...], axis=2)
    modal = lambda v: jnp.dot(
        basis_t[s_ref[1]], v, precision=HIGHEST, preferred_element_type=jnp.float32
    )
    even = modal(total[0])
    odd = modal(total[1])
    edge_low = even + odd
    edge_high = even - odd
    edges[0] = edge_high + far[s_ref[0]] * edge_low
    edges[1] = edge_low + far[s_ref[0]] * edge_high


def powers(s_ref, log_rho):
    rate = log_rho[s_ref[0]]
    return lambda n: jnp.exp(rate * n)


def scalar(value):
    return value.astype(jnp.float32)


def z_body(s_ref, edges, got1, got2, got3, log_rho, carried, four, two, passed, *, width):
    passed[...] = carried[...]
    power = powers(s_ref, log_rho)
    zi = s_ref[5]
    wide = float(width)
    right, left = edges[0], edges[1]
    low_sum = jnp.zeros_like(right)
    high_sum = jnp.zeros_like(right)
    right4 = power(wide * scalar(Z_RING - 1 - zi)) * right
    left4 = power(wide * scalar(zi)) * left
    for d, got in ((1, got1), (2, got2), (3, got3)):
        before = scalar(zi >= d)
        source = jnp.where(zi >= d, zi - d, zi - d + Z_RING)
        low_sum = low_sum + before * power(wide * (d - 1)) * got[0]
        high_sum = high_sum + (1.0 - before) * power(wide * (Z_RING - 1 - d)) * got[1]
        right4 = right4 + power(wide * scalar(Z_RING - 1 - source)) * got[0]
        left4 = left4 + power(wide * scalar(source)) * got[1]
    hop = power(wide)
    per_rho = power(-1.0)
    four[0] = per_rho * low_sum + left + hop * high_sum
    four[1] = per_rho * high_sum + right + hop * low_sum
    four[2] = right4
    four[3] = left4
    two[0] = right4
    two[1] = left4


def y_body(s_ref, four, there, beside1, beside2, log_rho, opening, run8, part, passed, *, width):
    passed[...] = opening[...]
    power = powers(s_ref, log_rho)
    zi = s_ref[5]
    wide = float(width)
    behind = scalar(s_ref[6])
    other0 = beside1[0] + beside2[0]
    other1 = beside1[1] + beside2[1]
    right4 = four[2] + there[2]
    left4 = four[3] + there[3]
    low_sum = behind * power(wide * scalar(zi)) * other0
    high_sum = (1.0 - behind) * power(wide * scalar(Z_RING - 1 - zi)) * other1
    run4 = power(wide * Z_RING)
    is_behind = s_ref[6] == 1
    run8[0] = jnp.where(is_behind, run4 * other0 + right4, run4 * right4 + other0)
    run8[1] = jnp.where(is_behind, other1 + run4 * left4, left4 + run4 * other1)
    hop = power(wide)
    per_rho = power(-1.0)
    part[0] = four[0] + there[0] + per_rho * low_sum + hop * high_sum
    part[1] = four[1] + there[1] + per_rho * high_sum + hop * low_sum


def x_sums(s_ref, run8, part, gots, log_rho, width):
    power = powers(s_ref, log_rho)
    wide = float(width)
    block = Z_RING * Y_PAIR
    right_sum = power(wide * block * (X_RING - 1)) * run8[0]
    left_sum = power(wide * block * (X_RING - 1)) * run8[1]
    for d, got in enumerate(gots, 1):
        right_sum = right_sum + power(wide * block * (d - 1)) * got[0]
        left_sum = left_sum + power(wide * block * (X_RING - 1 - d)) * got[1]
    periodic = 1.0 / (1.0 - power(wide * block * X_RING))
    low_sum = power(wide * scalar(s_ref[7])) * right_sum * periodic
    high_sum = power(wide * scalar(block - 1 - s_ref[7])) * left_sum * periodic
    rho = power(1.0)
    per_rho = power(-1.0)
    hop = power(wide)
    gain = rho / (1.0 - rho * rho)
    into_low = gain * (part[0] + per_rho * low_sum + hop * high_sum)
    into_high = gain * (part[1] + per_rho * high_sum + hop * low_sum)
    return into_low, into_high


def to_cells(values, span_t_high, span_t_low, back_high, back_low):
    lines = times(values, span_t_high, span_t_low)
    size = back_high.shape[0]
    return [
        times(lines[at : at + size].T, back_high, back_low) for at in range(0, lines.shape[0], size)
    ]


def solve_body(
    s_ref, planes, carried, opening, run8, part, got1, got2, got3, log_rho, pivots,
    span_t_high, span_t_low, back_high, back_low, edge, basis,
    wall, away, keep, solved, both, first,
):
    own, width, half = planes.shape
    count = own // 2
    is_low = s_ref[1] == 1
    code = s_ref[2]
    depthwise = lambda v: jnp.dot(
        basis[s_ref[1]], v, precision=HIGHEST, preferred_element_type=jnp.float32
    )
    into_low, into_high = x_sums(s_ref, run8, part, (got1, got2, got3), log_rho, width)
    gain_low = depthwise(into_low)
    gain_high = depthwise(into_high)
    both[0] = gain_low + gain_high
    both[1] = gain_low - gain_high
    first[width:] = jnp.zeros_like(first[width:])
    first[width : width + 1] = jnp.where(is_low, gain_low[own : own + 1], gain_low[:1])
    first[width + 1 : width + 2] = jnp.where(is_low, gain_high[own : own + 1], gain_high[:1])
    side = width // 16

    def tile(group, nothing):
        rows = pl.ds(pl.multiple_of(group * 8, 8), 8)
        parity = group // side
        scale = edge[rows]
        rhs = lambda i: scale * both[parity, i : i + 1]
        mine = lambda i: pivots[i - 1, rows]
        other = lambda i: pivots[own + i - 1, rows]
        carry = planes[code, rows] - rhs(0)
        carries = [carry]
        for i in range(1, own):
            carry = mine(i) * (planes[jnp.bitwise_xor(i, code), rows] - rhs(i)) - carry
            carries.append(carry)
        right = rhs(own)
        total = -right
        direct = -mine(own - 1) * right
        for i in range(1, own):
            right = rhs(own + i)
            total = -other(i) * right - total
            term = right if i == own - 1 else mine(own - 1 - i) * right
            direct = direct - term if i % 2 == 0 else direct + term
        total = total + carried[rows]
        value = (carry * other(own) - mine(own - 1) * total) * pivots[3 * own, rows]
        far_first = opening[rows] + (direct + value) * pivots[3 * own + 1, rows]
        solved[jnp.bitwise_xor(own - 1, code), rows] = value
        for i in range(own - 2, -1, -1):
            step = value if i == 0 else mine(i) * value
            value = (carries[i] - step) * pivots[2 * own + i, rows]
            solved[jnp.bitwise_xor(i, code), rows] = value
        first[rows] = jnp.where(is_low, far_first, value)
        return nothing

    lax.fori_loop(0, width // 8, tile, 0)
    table_high = span_t_high[s_ref[0]]
    table_low = span_t_low[s_ref[0]]
    line = times(first[...], table_high, table_low).T
    main = times(line[:, :width], back_high[:width, :width], back_low[:width, :width])
    wall[...] = jnp.concatenate([main, line[:, width:]], axis=1)
    values = solved[count:].reshape(count * width, half)
    for k, cells in enumerate(to_cells(values, table_high, table_low, back_high[...], back_low[...])):
        away[2 * k] = cells[:, :width]
        away[2 * k + 1] = cells[:, width:]
    keep[...] = solved[:count]


def cells_body(s_ref, keep, span_t_high, span_t_low, back_high, back_low, mine):
    count, width, half = keep.shape
    values = keep[...].reshape(count * width, half)
    pairs = to_cells(
        values, span_t_high[s_ref[0]], span_t_low[s_ref[0]], back_high[...], back_low[...]
    )
    for k, cells in enumerate(pairs):
        mine[2 * k] = cells[:, :width]
        mine[2 * k + 1] = cells[:, width:]


def join_body(s_ref, mine, came, out, held, sems):
    half = mine.shape[1]
    sign = (1 - 2 * s_ref[0]).astype(jnp.float32)
    copies = []
    for z in range(mine.shape[0]):
        ours = mine[z]
        theirs = came[z]
        held[z, :half] = ours + theirs
        held[z, half:] = sign * (ours - theirs)
        copy = pltpu.make_async_copy(held.at[z], out.at[z], sems.at[z])
        copy.start()
        copies.append(copy)
    for copy in copies:
        copy.wait()


def edge_body(s_ref, conductivity, temp, phase, gas, cond, packs, along, packed):
    depth, rows, width = temp.shape
    lane = lax.broadcasted_iota(jnp.int32, (CHUNK, width), 1)
    cold, warm = conductivity[0], conductivity[1]
    packed[...] = jnp.zeros_like(packed)

    def plane(z, nothing):
        for start in range(0, rows, CHUNK):
            at = slice(start, start + CHUNK)
            kept = packed[at]
            value = jnp.where(phase[z, at] == 1, warm, cold)
            cond[z, at] = value
            for k, part in enumerate((temp[z, at], value)):
                spot = 4 * (k * depth + z)
                chosen_lane = (lane >= spot) & (lane < spot + 4)
                kept = jnp.where(chosen_lane, pltpu.roll(part, spot + 2, 1), kept)
                line = 4 * depth * k + z
                if start == 0:
                    along[pl.ds(line + 2 * depth, 1)] = part[:1]
                    along[pl.ds(line + 3 * depth, 1)] = part[1:2]
                if start + CHUNK == rows:
                    along[pl.ds(line, 1)] = part[CHUNK - 2 : CHUNK - 1]
                    along[pl.ds(line + depth, 1)] = part[CHUNK - 1 :]
            packed[at] = kept
        return nothing

    lax.fori_loop(0, depth, plane, 0)
    last = 8 * depth
    turned = packed[...].T
    turned_gas = pltpu.roll(gas[...], 2, 1).T[:8]
    for h, at in pieces(rows):
        packs[h, :last] = turned[:, at]
        packs[h, last:] = turned_gas[:, at]
    along[last : last + 8] = jnp.concatenate(
        [gas[rows - 2 :], gas[:2], jnp.zeros((4, width), jnp.float32)], axis=0
    )


def pieces(length):
    return [(h, slice(h * 128, h * 128 + 128)) for h in range(length // 128)]


def column(ref, depth, kind, k):
    at = pl.ds(4 * depth * kind + k, depth, stride=4)
    return jnp.concatenate([ref[h, at] for h in range(ref.shape[0])], axis=1)


def flat(ref, row):
    return jnp.concatenate([ref[h, row : row + 1] for h in range(ref.shape[0])], axis=1)


def interleave(ref, odd, even):
    depth, length = odd.shape
    for h, at in pieces(length):
        ref[h, pl.ds(1, depth, stride=2)] = odd[:, at]
        ref[h, pl.ds(0, depth, stride=2)] = even[:, at]


def side_columns(s_ref, near, far, depth, kind, k, left):
    even = s_ref[8] == 0
    a, b = (far, near) if left else (near, far)
    return jnp.where(even, column(a, depth, kind, k), column(b, depth, kind, k))


def pass_body(s_ref, value, out):
    out[...] = value[...]


def corner_body(s_ref, along, near_x, far_x, out):
    depth = (along.shape[0] - 8) // 8
    width = along.shape[1]
    out[: along.shape[0]] = along[...]
    lane = lax.broadcasted_iota(jnp.int32, (depth, width), 1)
    block = jnp.zeros((depth, width), jnp.float32)
    rows = near_x.shape[0] * near_x.shape[2]
    spot = 0
    for y in (rows - 1, 0):
        for kind in range(2):
            for k, left in ((1, True), (2, False)):
                value = side_columns(s_ref, near_x, far_x, depth, kind, k, left)
                block = jnp.where(lane == spot, value[:, y : y + 1], block)
                spot += 1
    out[along.shape[0] :] = block


def settle(s_ref, lines, near, far):
    even = s_ref[0] == 0
    lines[0] = jnp.where(even, far[...], near[...])
    lines[1] = jnp.where(even, near[...], far[...])


def to_columns(packed, values):
    for h, at in pieces(packed.shape[1]):
        packed[: values.shape[1], at] = values[h]
    return packed[...].T


def rim(temp, cond, outer, inner, low, high, gas):
    depth, length = temp.shape
    row = lax.broadcasted_iota(jnp.int32, (depth, length), 0)
    lane = lax.broadcasted_iota(jnp.int32, (depth, length), 1)

    def around(value, at_low, at_high):
        return (
            jnp.where(lane == 0, at_low, pltpu.roll(value, 1, 1)),
            jnp.where(lane == length - 1, at_high, pltpu.roll(value, length - 1, 1)),
            jnp.where(row == 0, value, pltpu.roll(value, 1, 0)),
            jnp.where(row == depth - 1, value, pltpu.roll(value, depth - 1, 0)),
        )

    temps = (outer[0], inner[0]) + around(temp, low[0], high[0])
    conds = (outer[1], inner[1]) + around(cond, low[1], high[1])
    total = jnp.zeros_like(temp)
    for side_temp, side_cond in zip(temps, conds):
        total = total + (cond + side_cond) * (side_temp - temp)
    surface = jnp.where(row == 0, (STEP_RATE * HEAT_TRANSFER) * (gas - temp), 0.0)
    return temp + (0.5 * STEP_RATE) * total + surface


def step_planes(temp, cond, up, down, cond_up, cond_down, inflow, emit):
    depth, rows, width = temp.shape
    lane = lax.broadcasted_iota(jnp.int32, (CHUNK, width), 1)
    end = width - 1

    def shifted(ref, z, start, above, below):
        if start == 0:
            upper = jnp.concatenate([above[pl.ds(z, 1)], ref[z, : CHUNK - 1]], axis=0)
        else:
            upper = ref[z, start - 1 : start + CHUNK - 1]
        if start + CHUNK == rows:
            lower = jnp.concatenate([ref[z, start + 1 :], below[pl.ds(z, 1)]], axis=0)
        else:
            lower = ref[z, start + 1 : start + CHUNK + 1]
        return upper, lower

    def plane(z, first):
        before = jnp.maximum(z - 1, 0)
        after = jnp.minimum(z + 1, depth - 1)
        for start in range(0, rows, CHUNK):
            at = slice(start, start + CHUNK)
            here = temp[z, at]
            own = cond[z, at]
            pairs = []
            total = None
            sides = list(zip(shifted(temp, z, start, up, down), shifted(cond, z, start, cond_up, cond_down)))
            sides += [(temp[before, at], cond[before, at]), (temp[after, at], cond[after, at])]
            for side_temp, side_cond in sides:
                pair = own + side_cond
                pairs.append(pair)
                term = pair * (side_temp - here)
                total = term if total is None else total + term
            pair = own + pltpu.roll(own, end, 1)
            pairs.append(pair)
            flow = jnp.where(lane == end, 0.0, pair * (pltpu.roll(here, end, 1) - here))
            total = total + (flow - pltpu.roll(flow, 1, 1))
            spot = width - (2 * z + 1)
            entering = pltpu.roll(inflow[at], spot, 1)
            total = total + jnp.where((lane == 0) | (lane == end), entering, 0.0)
            emit(z, start, first, here + (0.5 * STEP_RATE) * total, pairs)

    plane(0, True)

    def later(z, nothing):
        plane(z, False)
        return nothing

    lax.fori_loop(1, depth, later, 0)


def first_body(
    s_ref, temp, cond, gas, packs, along, near_x, far_x, near_y, far_y,
    out, base_flow, face, base_lines, cond_lines, packed, flow, inflow, lines,
):
    depth, rows, width = temp.shape
    end = width - 1
    settle(s_ref, lines, near_y, far_y)
    last = 8 * depth
    own = lambda k: tuple(column(packs, depth, kind, k) for kind in range(2))
    left = lambda k: tuple(side_columns(s_ref, near_x, far_x, depth, kind, k, True) for kind in range(2))
    right = lambda k: tuple(side_columns(s_ref, near_x, far_x, depth, kind, k, False) for kind in range(2))
    line = lambda ref, k: tuple(
        ref[4 * depth * kind + depth * k : 4 * depth * kind + depth * (k + 1)] for kind in range(2)
    )
    above = lambda k: line(lines.at[0], k)
    below = lambda k: line(lines.at[1], k)
    corner = lambda which, spot: tuple(
        lines[which, last + 8 :][:, at : at + 1] for at in (spot, spot + 2)
    )
    even = s_ref[8] == 0
    gas_left = jnp.where(even, flat(far_x, last + 1), flat(near_x, last + 1))
    gas_right = jnp.where(even, flat(near_x, last + 2), flat(far_x, last + 2))
    at_lane = lambda pair, lane: tuple(v[:, lane : lane + 1] for v in pair)
    up_line, down_line = above(1), below(2)
    out_left = rim(*left(1), left(0), own(2), corner(0, 0), corner(1, 4), gas_left)
    out_right = rim(*right(2), right(3), own(1), corner(0, 1), corner(1, 5), gas_right)
    in_left = rim(
        *own(2), left(1), own(3), at_lane(up_line, 0), at_lane(down_line, 0), flat(packs, last + 2)
    )
    in_right = rim(
        *own(1), right(2), own(0), at_lane(up_line, end), at_lane(down_line, end),
        flat(packs, last + 1),
    )
    base_lines[0] = rim(
        *up_line, above(0), line(along, 2), corner(0, 0), corner(0, 1), lines[0, last + 1 : last + 2]
    )
    base_lines[1] = rim(
        *down_line, below(3), line(along, 1), corner(1, 4), corner(1, 5), lines[1, last + 2 : last + 3]
    )
    cond_lines[0] = up_line[1]
    cond_lines[1] = down_line[1]
    left_pair = own(2)[1] + left(1)[1]
    right_pair = own(1)[1] + right(2)[1]
    interleave(face, left_pair, right_pair)
    interleave(flow, left_pair * (left(1)[0] - own(2)[0]), right_pair * (right(2)[0] - own(1)[0]))
    interleave(base_flow, left_pair * (out_left - in_left), right_pair * (out_right - in_right))
    packed[...] = jnp.zeros_like(packed)
    inflow[...] = to_columns(packed, flow)

    def emit(z, start, first, value, pairs):
        at = slice(start, start + CHUNK)
        if first:
            value = value + (STEP_RATE * HEAT_TRANSFER) * (gas[at] - temp[0, at])
        out[z, at] = value

    span = lambda which, kind, k: lines.at[
        which, 4 * depth * kind + depth * k : 4 * depth * kind + depth * (k + 1)
    ]
    step_planes(
        temp, cond, span(0, 0, 1), span(1, 0, 2), span(0, 1, 1), span(1, 1, 2), inflow, emit
    )


def second_body(
    s_ref, base, cond, temp, gas, base_flow, face_rows, base_lines, cond_lines,
    out, top, weights, held, sems, packed, inflow, face,
):
    depth, rows, width = base.shape
    lane = lax.broadcasted_iota(jnp.int32, (CHUNK, width), 1)
    end = width - 1
    packed[...] = jnp.zeros_like(packed)
    inflow[...] = to_columns(packed, base_flow)
    face[...] = to_columns(packed, face_rows)

    def emit(z, start, first, value, pairs):
        at = slice(start, start + CHUNK)
        if first:
            value = value + (STEP_RATE * HEAT_TRANSFER) * (gas[at] - temp[0, at])
            edge = pltpu.roll(face[at], end, 1)
            across = pairs[4]
            left = jnp.where(lane == 0, edge, pltpu.roll(across, 1, 1))
            right = jnp.where(lane == end, edge, across)
            for k, pair in enumerate((pairs[0], pairs[1], left, right, pairs[3])):
                weights[k, at] = (0.5 * STEP_RATE) * pair
        held[z, at] = value
        if not first and start + CHUNK == rows:

            @pl.when(z >= 2)
            def _():
                pltpu.make_async_copy(held.at[z], out.at[z], sems.at[z]).start()

    step_planes(
        base, cond, base_lines.at[0], base_lines.at[1], cond_lines.at[0], cond_lines.at[1],
        inflow, emit,
    )
    top[...] = held[:2]
    for z in range(2, depth):
        pltpu.make_async_copy(held.at[z], out.at[z], sems.at[z]).wait()


def faces(value, row, lane, up, down, left, right):
    rows, width = value.shape
    return (
        jnp.where(row == 0, up, pltpu.roll(value, 1, 0)),
        jnp.where(row == rows - 1, down, pltpu.roll(value, rows - 1, 0)),
        jnp.where(lane == 0, left, pltpu.roll(value, 1, 1)),
        jnp.where(lane == width - 1, right, pltpu.roll(value, width - 1, 1)),
    )


def wall_body(s_ref, ours, theirs, weights, base, filled, out, held, sem):
    half = ours.shape[0]
    rows, width = weights.shape[1:]
    sign = (1 - 2 * s_ref[0]).astype(jnp.float32)
    bottom = (1 - 2 * s_ref[3]).astype(jnp.float32)
    second = s_ref[4] == 1
    factor = STEP_RATE * HEAT_TRANSFER * PRESSURE_WORK

    def lines(start, count, minus):
        our_sign = jnp.where(s_ref[0] == 0, 1.0, minus) * factor
        their_sign = jnp.where(s_ref[0] == 0, minus, 1.0) * factor
        at = pl.ds(start, count)
        return our_sign * ours[at] + their_sign * theirs[at]

    begin = pl.multiple_of(s_ref[4] * rows, rows)
    middle = lines(begin, rows, bottom)
    above = lines(jnp.where(second, rows - 1, half - 1), 1, jnp.where(second, bottom, -bottom))
    below = lines(jnp.where(second, 0, rows), 1, jnp.where(second, -bottom, bottom))
    share = middle[:, :width]
    row = lax.broadcasted_iota(jnp.int32, (rows, width), 0)
    lane = lax.broadcasted_iota(jnp.int32, (rows, width), 1)
    around = faces(
        share, row, lane, above[:, :width], below[:, :width],
        middle[:, width : width + 1], middle[:, width + 1 : width + 2],
    )
    added = 2.0 * share
    for k in range(4):
        added = added + weights[k] * (around[k] - share)
    down = weights[4] * share
    held[0] = base[0] + added - down
    held[1] = base[1] + down
    copy = pltpu.make_async_copy(held, out.at[:2], sem)
    copy.start()
    copy.wait()


def mover(groups, pencils):
    def move(value, target):
        pairs = []
        for g in range(groups):
            for p in range(pencils):
                to = target(g, p)
                pairs.append((g * pencils + p, to[0] * pencils + to[1]))
        return lax.ppermute(value, ("grp", "pen"), pairs)

    return move


def per_device(pressure_source, solid_temp, gas_wall_temp, phase_map, phase_conductivity):
    groups = lax.axis_size("grp")
    pencils = lax.axis_size("pen")
    group_idx = lax.axis_index("grp")
    pencil_idx = lax.axis_index("pen")
    depth_loc, span_len, width = pressure_source.shape
    depth = depth_loc * groups
    half = span_len // 2
    own = depth // 2
    core = group_idx % 2
    low = group_idx // 2
    zi = pencil_idx % Z_RING
    yl = pencil_idx // Z_RING % Y_PAIR
    place = pencil_idx % (Z_RING * Y_PAIR)
    move = mover(groups, pencils)
    tab = make_tables(span_len, width, depth)
    const = {k: tuple(map(jnp.asarray, v)) if isinstance(v, tuple) else jnp.asarray(v) for k, v in tab.items()}
    code = jnp.where(low == 0, core * 4, 7 - 4 * core)
    scalars = jnp.stack([core, low, code, low, core, zi, yl, place, pencil_idx % 2]).astype(jnp.int32)
    span = list(const["span"])
    into = list(const["into"])
    back = list(const["back"])
    span_t = list(const["span_t"])
    tile_rows = span_len // groups
    flip = lambda mask: lambda g, p: (g ^ mask, p)
    near_pair = lambda g, p: (g, p ^ 1)
    far_pair = lambda g, p: (g, (p + 1 if p % 2 else p - 1) % pencils)

    other_core = lambda g, p: (g ^ 1, p)
    other_half = lambda g, p: (g ^ 2, p)
    halves_of = tile_rows // 128
    column_scratch = pltpu.VMEM((tile_rows, width), jnp.float32)
    row_scratch = pltpu.VMEM((width, tile_rows), jnp.float32)
    (pivots,) = run(
        pivot_body, 1.2, scalars, [], [const["lam"], const["sigma"]], [(3 * own + 2, width, half)]
    )
    cond, packs, along = run(
        edge_body, 2.8, scalars, [pivots], [solid_temp, phase_map, gas_wall_temp],
        [(depth, tile_rows, width), (halves_of, 8 * depth + 8, 128), (8 * depth + 8, width)],
        scratch=[column_scratch], small=[phase_conductivity],
    )
    near_x = [move(packs, near_pair), move(packs, far_pair)]
    folded = jax.ShapeDtypeStruct((depth_loc, half, width), jnp.float32)
    away, kept = run_blocks(
        fold_body, 0.8, scalars, [along, pressure_source], [ORDER, plane_of(pressure_source)],
        [folded.shape, folded.shape], [plane_of(folded), plane_of(folded)], depth_loc,
    )
    arrived = move(away, other_core)
    (held,) = run(
        held_body, 2.1, scalars, [], [kept, *into, *span], [(depth_loc, width, half)]
    )
    (lines,) = run(
        corner_body, 0.6, scalars, [held], [along, *near_x], [(9 * depth + 8, width)]
    )
    near_y = [move(lines, flip(1)), move(lines, flip(3))]
    planes, edges, carried, opening = run(
        arrived_body, 3.4, scalars, [lines],
        [arrived, held, *into, *span, pivots, const["edge"], const["basis_t"], const["far"]],
        [(own, width, half), (2, depth, half), (width, half), (width, half)],
        scratch=[pltpu.VMEM((2, depth, 8, half), jnp.float32)],
    )
    z_got = [
        move(edges, lambda g, p, d=d: (g, p // Z_RING * Z_RING + (p + d) % Z_RING))
        for d in range(1, Z_RING)
    ]
    log_rho = const["log_rho"]
    pair_shape = edges.shape
    four, two, carried = run(
        functools.partial(z_body, width=width), 0.6, scalars, near_y,
        [edges, *z_got, log_rho, carried], [(4,) + pair_shape[1:], pair_shape, carried.shape],
    )
    carried_there = move(carried, other_half)
    there = move(four, other_half)
    beside1 = move(two, lambda g, p: (g, p ^ Z_RING))
    beside2 = move(two, lambda g, p: (g ^ 2, p ^ Z_RING))
    base, base_flow, face, base_lines, cond_lines = run(
        first_body, 6.6, scalars, [two],
        [solid_temp, cond, gas_wall_temp, packs, along, *near_x, *near_y],
        [(depth, tile_rows, width), (halves_of, 2 * depth, 128), (halves_of, 2 * depth, 128),
         (2, depth, width), (2, depth, width)],
        scratch=[
            row_scratch, pltpu.VMEM((halves_of, 2 * depth, 128), jnp.float32), column_scratch,
            pltpu.VMEM((2, 9 * depth + 8, width), jnp.float32),
        ],
    )
    run8, part, opening = run(
        functools.partial(y_body, width=width), 0.6, scalars, [base, carried_there],
        [four, there, beside1, beside2, log_rho, opening], [pair_shape, pair_shape, opening.shape],
    )
    block = Z_RING * Y_PAIR
    opening_there = move(opening, other_half)
    x_got = [move(run8, lambda g, p, d=d: (g, (p + block * d) % pencils)) for d in range(1, X_RING)]
    final, top, weights = run(
        second_body, 6.5, scalars, [run8],
        [base, cond, solid_temp, gas_wall_temp, base_flow, face, base_lines, cond_lines],
        [solid_temp.shape, (2, tile_rows, width), (5, tile_rows, width)],
        scratch=[
            pltpu.VMEM((depth, tile_rows, width), jnp.float32), pltpu.SemaphoreType.DMA((depth,)),
            row_scratch, column_scratch, column_scratch,
        ],
        out_specs=[ORDER, FAST, FAST],
    )
    wall, away, keep = run(
        solve_body, 6.9, scalars, [weights],
        [planes, carried_there, opening_there, run8, part, *x_got, log_rho, pivots, *span_t, *back,
         const["edge"], const["basis"]],
        [(half, 2 * width), (depth_loc, half, width), (depth_loc, width, half)],
        scratch=[
            pltpu.VMEM((own, width, half), jnp.float32),
            pltpu.VMEM((2, depth, half), jnp.float32),
            pltpu.VMEM((2 * width, half), jnp.float32),
        ],
    )
    wall_came = move(wall, other_core)
    came = move(away, other_core)
    (mine,) = run(cells_body, 2.2, scalars, [], [keep, *span_t, *back], [(depth_loc, half, width)])
    (pressure,) = run(
        join_body, 1.9, scalars, [], [mine, came], [pressure_source.shape], out_specs=[ORDER],
        scratch=[
            pltpu.VMEM(pressure_source.shape, jnp.float32), pltpu.SemaphoreType.DMA((depth_loc,))
        ],
    )
    (final,) = run(
        wall_body, 1.5, scalars, [], [wall, wall_came, weights, top, (final, ORDER)], [final.shape],
        scratch=[pltpu.VMEM(top.shape, jnp.float32), pltpu.SemaphoreType.DMA],
        out_specs=[ORDER], aliases={5: 0},
    )
    return (pressure, final)


def solution(mesh):
    in_specs = (
        P("grp", None, "pen"),
        P(None, "grp", "pen"),
        P("grp", "pen"),
        P(None, "grp", "pen"),
        P(),
    )
    out_specs = (P("grp", None, "pen"), P(None, "grp", "pen"))
    return jax.shard_map(
        per_device, mesh=mesh, in_specs=in_specs, out_specs=out_specs, check_vma=False
    )
```

time: 87.7 us -> 75.6 us (0.86)
  Pallas kernels: 46.5 us -> 34.5 us
  starting transfers between devices: 31.8 us -> 23.3 us
  waiting for transfers between devices: 5.07 us -> 13.4 us
    pallas_call x12 -> x14, Pallas kernels: 46.5 us -> 34.5 us  [the longest x13 33.7 us: run(): pl.pallas_call(inner, out_shape=outs, in_specs=specs, out_specs=out_specs...]
    ppermute x22 -> x18, starting transfers between devices: 31.8 us -> 23.3 us  [move(): return lax.ppermute(value, ('grp', 'pen'), pairs)]
    ppermute x22 -> x18, waiting for transfers between devices: 5.07 us -> 13.4 us  [move(): return lax.ppermute(value, ('grp', 'pen'), pairs)]
  transfers between devices with their start and end apart: 22 -> 18, of which waited for: 5 -> 7; matrix products, arithmetic and copies ran while one was open for 0% -> 0% of each run, Pallas kernels for 34% -> 29%
where the time goes in v2:
time: 75.6 us; the launch traced here: 75.1 us
  Pallas kernels  34.5 us (46%)
  starting transfers between devices  23.3 us (31%)
  waiting for transfers between devices  13.4 us (18%)
  local copies, waits for them, and re-layouts  2.86 us (4%)
  between operations  1.02 us (1%)
    pallas_call x13, Pallas kernels, run(): pl.pallas_call(inner, out_shape=outs, in_specs=specs, out_specs=out_specs...  33.7 us
    ppermute x18, starting transfers between devices, move(): return lax.ppermute(value, ('grp', 'pen'), pairs)  23.3 us
    ppermute x18, waiting for transfers between devices, move(): return lax.ppermute(value, ('grp', 'pen'), pairs)  13.4 us
    unnamed x40, local copies, waits for them, and re-layouts  2.77 us
  transfers between devices with their start and end apart: 18, of which 7 were waited for; matrix products, arithmetic and copies ran while one was open for 0% of the time, Pallas kernels for 29%

profile of v2, /device:TPU:1, one launch (start us, length us, event | category | flops | bytes accessed | tf_op | source)
XLA Modules:
  0.0 75.1 jit_solution(6461163058230912079)
XLA Ops:
  0.7 0.1 stack.33.s_ref
  0.8 1.0 %copy-done.14 = f32[128,512]{1,0:T(8,128)S(1)} copy-done((f32[128,512]{1,0:T(8,128)S(1)}, f32[128,512]{1,0:T(8,128)}, u32[]{:S(2)}) %copy-start.14) | copy-done | bytes 262168
  1.7 0.7 copy-done.18
  2.4 1.2 %shard_map.203.refs_1_.refs_7_.refs_10_ = f32[26,128,512]{2,1,0:T(8,128)S(1)} custom-call(s32[9]{0:T(128)S(1)} %stack.33.s_ref, f32[2,1,512]{2,1,0:T(1,128)S(1)} %copy-done.18, f32[128,512]{1,0:T(8,128)S(1)} %copy-done.14), custom_call_target="tpu_custom_call" | custom-call | flops 1 | bytes 442800 | tf_op jit(solution)/shard_map/pallas_call | solution.py:115
  3.6 0.4 copy-done
  4.0 0.6 copy-done.6
  4.7 0.0 copy-start.13
  4.7 2.8 %shard_map.204 = (f32[16,256,128]{2,1,0:T(8,128)S(1)}, f32[2,136,128]{2,1,0:T(8,128)S(1)}, f32[136,128]{1,0:T(8,128)S(1)}) custom-call(s32[9]{0:T(128)S(1)} %stack.33.s_ref, f32[2]{0:T(128)S(1)} %copy-done.19, f32[26,128,512]{2,1,0:T(8,128)S(1)} %shard_map.203.refs_1_.refs_7_.refs_10_, f32[16,256,128]{2,1,0:T(8,128)S(1)} %copy-done, ...), custom_call_target="tpu_custom_call" | custom-call | flops 1 | bytes 1033200 | tf_op jit(solution)/shard_map/pallas_call | solution.py:115
  7.5 0.0 copy-start.3
  7.5 0.0 copy-start.4
  7.6 0.0 copy-done.5
  7.6 0.8 %shard_map.205 = (f32[4,512,128]{2,1,0:T(8,128)S(1)}, f32[4,512,128]{2,1,0:T(8,128)S(1)}) custom-call(s32[9]{0:T(128)S(1)} %stack.33.s_ref, f32[136,128]{1,0:T(8,128)S(1)} %get-tuple-element.28.after.refs_1_.refs_5_, f32[4,1024,128]{2,1,0:T(8,128)S(1)} %copy-done.5), custom_call_target="tpu_custom_call" | custom-call | flops 1 | bytes 295200 | tf_op jit(solution)/shard_map/pallas_call | solution.py:128
  8.4 1.5 %collective-permute-start.4 = (f32[4,512,128]{2,1,0:T(8,128)S(1)}, f32[4,512,128]{2,1,0:T(8,128)S(1)}, u32[]{:S(2)}, u32[]{:S(2)}) collective-permute-start(f32[4,512,128]{2,1,0:T(8,128)S(1)} %get-tuple-element.31), channel_id=1, source_target_pairs={{0,32},{1,33},{2,34},{3,35},{4,36},{5,37},{6,38},{7,39},{8,40},{9,... | collective-permute-start | bytes 3145736 | tf_op jit(solution)/shard_map/ppermute | solution.py:746
  9.9 7.1 %collective-permute-start.1 = (f32[2,136,128]{2,1,0:T(8,128)S(1)}, f32[2,136,128]{2,1,0:T(8,128)S(1)}, u32[]{:S(2)}, u32[]{:S(2)}) collective-permute-start(f32[2,136,128]{2,1,0:T(8,128)S(1)} %get-tuple-element.30.refs_4_), channel_id=1, source_target_pairs={{0,31},{1,2},{2,1},{3,4},{4,3},{5,6},{6,5},{7,8},{8,7},{9,10},{10,... | collective-permute-start | bytes 417800 | tf_op jit(solution)/shard_map/ppermute | solution.py:746
  16.9 0.0 collective-permute-start
  17.0 0.0 copy-start.8
  17.0 0.0 copy-start.15
  17.0 0.0 copy-start.17
  17.0 2.1 %shard_map.206.refs_0_.refs_2_ = f32[4,128,512]{2,1,0:T(8,128)S(1)} custom-call(s32[9]{0:T(128)S(1)} %stack.33.s_ref, f32[4,512,128]{2,1,0:T(8,128)S(1)} %get-tuple-element.29.refs_0_, bf16[256,256]{1,0:T(8,128)(2,1)S(1)} %copy-done.13, bf16[256,256]{1,0:T(8,128)(2,1)S(1)} %copy-done.12, bf16[2,512,512]{2,1,0:T(8,128)(2,1)S(1)} %copy-done.4, ...), custom_call_target="tpu_custom_call" | custom-call | flops 1 | bytes 774900 | tf_op jit(solution)/shard_map/pallas_call | solution.py:115
  19.1 1.8 %collective-permute-done.1.refs_3_.refs_7_ = f32[2,136,128]{2,1,0:T(8,128)S(1)} collective-permute-done((f32[2,136,128]{2,1,0:T(8,128)S(1)}, f32[2,136,128]{2,1,0:T(8,128)S(1)}, u32[]{:S(2)}, u32[]{:S(2)}) %collective-permute-start.1) | collective-permute-done | bytes 139296 | tf_op jit(solution)/shard_map/ppermute | solution.py:746
  20.9 1.0 %collective-permute-done.refs_2_.refs_6_ = f32[2,136,128]{2,1,0:T(8,128)S(1)} collective-permute-done((f32[2,136,128]{2,1,0:T(8,128)S(1)}, f32[2,136,128]{2,1,0:T(8,128)S(1)}, u32[]{:S(2)}, u32[]{:S(2)}) %collective-permute-start) | collective-permute-done | bytes 139296 | tf_op jit(solution)/shard_map/ppermute | solution.py:746
  21.8 0.6 shard_map.207.refs_0_
  22.4 0.0 copy-start.9
  22.5 3.8 %collective-permute-start.3 = (f32[152,128]{1,0:T(8,128)S(1)}, f32[152,128]{1,0:T(8,128)S(1)}, u32[]{:S(2)}, u32[]{:S(2)}) collective-permute-start(f32[152,128]{1,0:T(8,128)S(1)} %shard_map.207.refs_0_), channel_id=1, source_target_pairs={{0,96},{1,97},{2,98},{3,99},{4,100},{5,101},{6,102},{7,103},{8,104... | collective-permute-start | bytes 233480 | tf_op jit(solution)/shard_map/ppermute | solution.py:746
  26.2 0.0 collective-permute-start.2
  26.2 0.0 collective-permute-done.4.refs_1_
  26.3 3.5 %shard_map.208 = (f32[8,128,512]{2,1,0:T(8,128)S(1)}, f32[2,16,512]{2,1,0:T(8,128)S(1)}, f32[128,512]{1,0:T(8,128)S(1)}, f32[128,512]{1,0:T(8,128)S(1)}) custom-call(s32[9]{0:T(128)S(1)} %stack.33.s_ref, f32[152,128]{1,0:T(8,128)S(1)} %shard_map.207.refs_0_, f32[4,512,128]{2,1,0:T(8,128)S(1)} %collective-permute-done.4.refs_1_, ...), custom_call_target="tpu_custom_call" | custom-call | flops 1 | bytes 1254600 | tf_op jit(solution)/shard_map/pallas_call | solution.py:115
  29.7 0.1 collective-permute-start.7
  29.8 1.8 %collective-permute-start.6 = (f32[2,16,512]{2,1,0:T(8,128)S(1)}, f32[2,16,512]{2,1,0:T(8,128)S(1)}, u32[]{:S(2)}, u32[]{:S(2)}) collective-permute-start(f32[2,16,512]{2,1,0:T(8,128)S(1)} %get-tuple-element.32.refs_2_), channel_id=1, source_target_pairs={{0,2},{1,3},{2,0},{3,1},{4,6},{5,7},{6,4},{7,5},{8,10},{9,11},{10,... | collective-permute-start | bytes 196616 | tf_op jit(solution)/shard_map/ppermute | solution.py:746
  31.6 0.0 collective-permute-start.5
  31.6 0.0 collective-permute-done.3.refs_1_.refs_9_
  31.6 0.0 collective-permute-done.2.refs_0_.refs_8_
  31.6 1.3 %collective-permute-done.7.refs_5_ = f32[2,16,512]{2,1,0:T(8,128)S(1)} collective-permute-done((f32[2,16,512]{2,1,0:T(8,128)S(1)}, f32[2,16,512]{2,1,0:T(8,128)S(1)}, u32[]{:S(2)}, u32[]{:S(2)}) %collective-permute-start.7) | collective-permute-done | bytes 65568 | tf_op jit(solution)/shard_map/ppermute | solution.py:746
  32.9 1.6 %collective-permute-done.6.refs_4_ = f32[2,16,512]{2,1,0:T(8,128)S(1)} collective-permute-done((f32[2,16,512]{2,1,0:T(8,128)S(1)}, f32[2,16,512]{2,1,0:T(8,128)S(1)}, u32[]{:S(2)}, u32[]{:S(2)}) %collective-permute-start.6) | collective-permute-done | bytes 65568 | tf_op jit(solution)/shard_map/ppermute | solution.py:746
  34.5 1.7 %collective-permute-done.5.refs_3_ = f32[2,16,512]{2,1,0:T(8,128)S(1)} collective-permute-done((f32[2,16,512]{2,1,0:T(8,128)S(1)}, f32[2,16,512]{2,1,0:T(8,128)S(1)}, u32[]{:S(2)}, u32[]{:S(2)}) %collective-permute-start.5) | collective-permute-done | bytes 65568 | tf_op jit(solution)/shard_map/ppermute | solution.py:746
  36.2 0.6 shard_map.209
  36.8 0.4 collective-permute-start.8
  37.3 2.6 %collective-permute-start.9 = (f32[4,16,512]{2,1,0:T(8,128)S(1)}, f32[4,16,512]{2,1,0:T(8,128)S(1)}, u32[]{:S(2)}, u32[]{:S(2)}) collective-permute-start(f32[4,16,512]{2,1,0:T(8,128)S(1)} %get-tuple-element.38.refs_2_), channel_id=1, source_target_pairs={{0,64},{1,65},{2,66},{3,67},{4,68},{5,69},{6,70},{7,71},{8,72},{9,... | collective-permute-start | bytes 393224 | tf_op jit(solution)/shard_map/ppermute | solution.py:746
  39.9 0.0 collective-permute-start.11
  39.9 0.0 collective-permute-start.10
  39.9 5.6 %shard_map.210 = (f32[16,256,128]{2,1,0:T(8,128)S(1)}, f32[2,32,128]{2,1,0:T(8,128)S(1)}, f32[2,32,128]{2,1,0:T(8,128)S(1)}, f32[2,16,128]{2,1,0:T(8,128)S(1)}, f32[2,16,128]{2,1,0:T(8,128)S(1)}) custom-call(s32[9]{0:T(128)S(1)} %stack.33.s_ref, f32[2,16,512]{2,1,0:T(8,128)S(1)} %get-tuple-element.34.refs_0_, f32[16,256,128]{2,1,0:T(8,128)S(1)} %copy-done, ...), custom_call_target="tpu_custom_call" | custom-call | flops 1 | bytes 2435400 | tf_op jit(solution)/shard_map/pallas_call | solution.py:115
  45.5 5.3 %collective-permute-done.11.refs_5_ = f32[2,16,512]{2,1,0:T(8,128)S(1)} collective-permute-done((f32[2,16,512]{2,1,0:T(8,128)S(1)}, f32[2,16,512]{2,1,0:T(8,128)S(1)}, u32[]{:S(2)}, u32[]{:S(2)}) %collective-permute-start.11) | collective-permute-done | bytes 65568 | tf_op jit(solution)/shard_map/ppermute | solution.py:746
  50.9 0.0 collective-permute-done.10.refs_4_
  50.9 0.0 collective-permute-done.9.refs_3_
  50.9 0.0 collective-permute-done.8.refs_1_.refs_2_
  50.9 0.6 shard_map.211
  51.5 0.4 collective-permute-start.12
  51.9 2.4 %collective-permute-start.15 = (f32[2,16,512]{2,1,0:T(8,128)S(1)}, f32[2,16,512]{2,1,0:T(8,128)S(1)}, u32[]{:S(2)}, u32[]{:S(2)}) collective-permute-start(f32[2,16,512]{2,1,0:T(8,128)S(1)} %get-tuple-element.40.refs_0_.refs_4_), channel_id=1, source_target_pairs={{0,24},{1,25},{2,26},{3,27},{4,28},{5,29},{6,30},{7,31},{8,0},{9,1... | collective-permute-start | bytes 196616 | tf_op jit(solution)/shard_map/ppermute | solution.py:746
  54.3 0.0 collective-permute-start.14
  54.3 0.6 collective-permute-start.13
  54.9 0.0 copy-start.16
  54.9 6.5 %shard_map.212 = (f32[16,256,128]{2,1,0:T(8,128)}, f32[2,256,128]{2,1,0:T(8,128)S(1)}, f32[5,256,128]{2,1,0:T(8,128)S(1)}) custom-call(s32[9]{0:T(128)S(1)} %stack.33.s_ref, f32[2,16,512]{2,1,0:T(8,128)S(1)} %get-tuple-element.40.refs_0_.refs_4_, f32[16,256,128]{2,1,0:T(8,128)S(1)} %get-tuple-element.36.refs_0_.refs_1_, ...), custom_call_target="tpu_custom_call" | custom-call | flops 1 | bytes 2398500 | tf_op jit(solution)/shard_map/pallas_call | solution.py:115
  61.4 0.0 collective-permute-done.15.refs_8_
  61.4 0.0 collective-permute-done.14.refs_7_
  61.4 0.0 collective-permute-done.13.refs_6_
  61.4 0.0 collective-permute-done.12.refs_3_
  61.5 4.5 %shard_map.213 = (f32[512,256]{1,0:T(8,128)S(1)}, f32[4,512,128]{2,1,0:T(8,128)S(1)}, f32[4,128,512]{2,1,0:T(8,128)S(1)}) custom-call(s32[9]{0:T(128)S(1)} %stack.33.s_ref, f32[5,256,128]{2,1,0:T(8,128)S(1)} %get-tuple-element.45.refs_0_.refs_2_, f32[8,128,512]{2,1,0:T(8,128)S(1)} %get-tuple-element.46.refs_1_, ...), custom_call_target="tpu_custom_call" | custom-call | flops 1 | bytes 2546100 | tf_op jit(solution)/shard_map/pallas_call | solution.py:115
  66.0 2.6 %collective-permute-start.16 = (f32[4,512,128]{2,1,0:T(8,128)S(1)}, f32[4,512,128]{2,1,0:T(8,128)S(1)}, u32[]{:S(2)}, u32[]{:S(2)}) collective-permute-start(f32[4,512,128]{2,1,0:T(8,128)S(1)} %get-tuple-element.50), channel_id=1, source_target_pairs={{0,32},{1,33},{2,34},{3,35},{4,36},{5,37},{6,38},{7,39},{8,40},{9,... | collective-permute-start | bytes 3145736 | tf_op jit(solution)/shard_map/ppermute | solution.py:746
  68.6 0.1 collective-permute-start.17
  68.7 2.2 %shard_map.214.refs_0_ = f32[4,512,128]{2,1,0:T(8,128)S(1)} custom-call(s32[9]{0:T(128)S(1)} %stack.33.s_ref, f32[4,128,512]{2,1,0:T(8,128)S(1)} %get-tuple-element.49.refs_0_, bf16[2,512,512]{2,1,0:T(8,128)(2,1)S(1)} %copy-done.2, bf16[2,512,512]{2,1,0:T(8,128)(2,1)S(1)} %copy-done.1, bf16[256,256]{1,0:T(8,128)(2,1)S(1)} %copy-done.11, ...), custom_call_target="tpu_custom_call" | custom-call | flops 1 | bytes 811800 | tf_op jit(solution)/shard_map/pallas_call | solution.py:115
  70.9 0.7 collective-permute-done.17.refs_1_
  71.7 1.5 %shard_map.216 = f32[16,256,128]{2,1,0:T(8,128)} custom-call(s32[9]{0:T(128)S(1)} %stack.33.s_ref, f32[512,256]{1,0:T(8,128)S(1)} %get-tuple-element.51.refs_0_, f32[512,256]{1,0:T(8,128)S(1)} %collective-permute-done.17.refs_1_, f32[5,256,128]{2,1,0:T(8,128)S(1)} %get-tuple-element.45.refs_0_.refs_2_, ...), custom_call_target="tpu_custom_call", output_to_operand_aliasing={{}: (5, {})} | custom-call | flops 1 | bytes 553500 | tf_op jit(solution)/shard_map/pallas_call | solution.py:115
  73.2 0.0 collective-permute-done.16.refs_1_
  73.2 1.9 %shard_map.215 = f32[4,1024,128]{2,1,0:T(8,128)} custom-call(s32[9]{0:T(128)S(1)} %stack.33.s_ref, f32[4,512,128]{2,1,0:T(8,128)S(1)} %shard_map.214.refs_0_, f32[4,512,128]{2,1,0:T(8,128)S(1)} %collective-permute-done.16.refs_1_), custom_call_target="tpu_custom_call" | custom-call | flops 1 | bytes 701100 | tf_op jit(solution)/shard_map/pallas_call | solution.py:115
  (27 shorter events, 0.1 us)
Async XLA Ops:
  0.8 1.0 %copy-start.14 = (f32[128,512]{1,0:T(8,128)S(1)}, f32[128,512]{1,0:T(8,128)}, u32[]{:S(2)}) copy-start(f32[128,512]{1,0:T(8,128)} %constant.110.clone.refs_1_) | copy-start | bytes 786436
  1.7 0.7 copy-start.18
  2.4 1.6 %copy-start = (f32[16,256,128]{2,1,0:T(8,128)S(1)}, f32[16,256,128]{2,1,0:T(8,128)}, u32[]{:S(2)}) copy-start(f32[16,256,128]{2,1,0:T(8,128)} %refs_3_.8) | copy-start | bytes 6291460
  2.4 2.2 %copy-start.6 = (s32[16,256,128]{2,1,0:T(8,128)S(1)}, s32[16,256,128]{2,1,0:T(8,128)}, u32[]{:S(2)}) copy-start(s32[16,256,128]{2,1,0:T(8,128)} %refs_3_.6) | copy-start | bytes 6291460
  2.4 2.2 %copy-start.7 = (f32[256,128]{1,0:T(8,128)S(1)}, f32[256,128]{1,0:T(8,128)}, u32[]{:S(2)}) copy-start(f32[256,128]{1,0:T(8,128)} %refs_4_.6) | copy-start | bytes 393220
  2.4 2.2 %copy-start.19 = (f32[2]{0:T(128)S(1)}, f32[2]{0:T(128)}, u32[]{:S(2)}) copy-start(f32[2]{0:T(128)} %refs_0_.2) | copy-start | bytes 28
  4.7 2.9 %copy-start.5 = (f32[4,1024,128]{2,1,0:T(8,128)S(1)}, f32[4,1024,128]{2,1,0:T(8,128)}, u32[]{:S(2)}) copy-start(f32[4,1024,128]{2,1,0:T(8,128)} %source.1) | copy-start | bytes 6291460
  4.7 12.3 %copy-start.12 = (bf16[256,256]{1,0:T(8,128)(2,1)S(1)}, bf16[256,256]{1,0:T(8,128)(2,1)}, u32[]{:S(2)}) copy-start(bf16[256,256]{1,0:T(8,128)(2,1)} %constant.106.clone.refs_2_.refs_4_) | copy-start | bytes 393220
  4.7 12.3 %copy-start.13 = (bf16[256,256]{1,0:T(8,128)(2,1)S(1)}, bf16[256,256]{1,0:T(8,128)(2,1)}, u32[]{:S(2)}) copy-start(bf16[256,256]{1,0:T(8,128)(2,1)} %constant.105.clone.refs_1_.refs_3_) | copy-start | bytes 393220
  7.5 9.4 %copy-start.3 = (bf16[2,512,512]{2,1,0:T(8,128)(2,1)S(1)}, bf16[2,512,512]{2,1,0:T(8,128)(2,1)}, u32[]{:S(2)}) copy-start(bf16[2,512,512]{2,1,0:T(8,128)(2,1)} %constant.102.clone.refs_4_.refs_6_) | copy-start | bytes 3145732
  7.5 9.4 %copy-start.4 = (bf16[2,512,512]{2,1,0:T(8,128)(2,1)S(1)}, bf16[2,512,512]{2,1,0:T(8,128)(2,1)}, u32[]{:S(2)}) copy-start(bf16[2,512,512]{2,1,0:T(8,128)(2,1)} %constant.101.clone.refs_3_.refs_5_) | copy-start | bytes 3145732
  8.4 17.9 %collective-permute-start.4 = (f32[4,512,128]{2,1,0:T(8,128)S(1)}, f32[4,512,128]{2,1,0:T(8,128)S(1)}, u32[]{:S(2)}, u32[]{:S(2)}) collective-permute-start(f32[4,512,128]{2,1,0:T(8,128)S(1)} %get-tuple-element.31), channel_id=1, source_target_pairs={{0,32},{1,33},{2,34},{3,35},{4,36},{5,37},{6,38},{7,39},{8,40},{9,... | collective-permute-start | bytes 3145736 | tf_op jit(solution)/shard_map/ppermute | solution.py:746
  9.9 11.0 %collective-permute-start.1 = (f32[2,136,128]{2,1,0:T(8,128)S(1)}, f32[2,136,128]{2,1,0:T(8,128)S(1)}, u32[]{:S(2)}, u32[]{:S(2)}) collective-permute-start(f32[2,136,128]{2,1,0:T(8,128)S(1)} %get-tuple-element.30.refs_4_), channel_id=1, source_target_pairs={{0,31},{1,2},{2,1},{3,4},{4,3},{5,6},{6,5},{7,8},{8,7},{9,10},{10,... | collective-permute-start | bytes 417800 | tf_op jit(solution)/shard_map/ppermute | solution.py:746
  16.9 4.9 %collective-permute-start = (f32[2,136,128]{2,1,0:T(8,128)S(1)}, f32[2,136,128]{2,1,0:T(8,128)S(1)}, u32[]{:S(2)}, u32[]{:S(2)}) collective-permute-start(f32[2,136,128]{2,1,0:T(8,128)S(1)} %get-tuple-element.30.refs_4_), channel_id=1, source_target_pairs={{0,1},{1,0},{2,3},{3,2},{4,5},{5,4},{6,7},{7,6},{8,9},{9,8},{10,11... | collective-permute-start | bytes 417800 | tf_op jit(solution)/shard_map/ppermute | solution.py:746
  17.0 9.3 %copy-start.8 = (f32[128,512]{1,0:T(8,128)S(1)}, f32[128,512]{1,0:T(8,128)}, u32[]{:S(2)}) copy-start(f32[128,512]{1,0:T(8,128)} %constant.111.clone.refs_8_.refs_15_) | copy-start | bytes 786436
  17.0 9.3 %copy-start.15 = (f32[2,16,512]{2,1,0:T(8,128)S(1)}, f32[2,16,512]{2,1,0:T(8,128)}, u32[]{:S(2)}) copy-start(f32[2,16,512]{2,1,0:T(8,128)} %constant.115.clone.refs_10_) | copy-start | bytes 196612
  17.0 9.3 %copy-start.17 = (f32[2,16,16]{2,1,0:T(8,128)S(1)}, f32[2,16,16]{2,1,0:T(8,128)}, u32[]{:S(2)}) copy-start(f32[2,16,16]{2,1,0:T(8,128)} %constant.113.clone.refs_9_) | copy-start | bytes 6148
  22.4 13.7 %copy-start.9 = (f32[2,16,512]{2,1,0:T(8,128)S(1)}, f32[2,16,512]{2,1,0:T(8,128)}, u32[]{:S(2)}) copy-start(f32[2,16,512]{2,1,0:T(8,128)} %constant.114.clone.refs_6_.refs_9_) | copy-start | bytes 196612
  22.5 9.1 %collective-permute-start.3 = (f32[152,128]{1,0:T(8,128)S(1)}, f32[152,128]{1,0:T(8,128)S(1)}, u32[]{:S(2)}, u32[]{:S(2)}) collective-permute-start(f32[152,128]{1,0:T(8,128)S(1)} %shard_map.207.refs_0_), channel_id=1, source_target_pairs={{0,96},{1,97},{2,98},{3,99},{4,100},{5,101},{6,102},{7,103},{8,104... | collective-permute-start | bytes 233480 | tf_op jit(solution)/shard_map/ppermute | solution.py:746
  26.2 5.4 %collective-permute-start.2 = (f32[152,128]{1,0:T(8,128)S(1)}, f32[152,128]{1,0:T(8,128)S(1)}, u32[]{:S(2)}, u32[]{:S(2)}) collective-permute-start(f32[152,128]{1,0:T(8,128)S(1)} %shard_map.207.refs_0_), channel_id=1, source_target_pairs={{0,32},{1,33},{2,34},{3,35},{4,36},{5,37},{6,38},{7,39},{8,40},{9,... | collective-permute-start | bytes 233480 | tf_op jit(solution)/shard_map/ppermute | solution.py:746
  29.7 3.2 %collective-permute-start.7 = (f32[2,16,512]{2,1,0:T(8,128)S(1)}, f32[2,16,512]{2,1,0:T(8,128)S(1)}, u32[]{:S(2)}, u32[]{:S(2)}) collective-permute-start(f32[2,16,512]{2,1,0:T(8,128)S(1)} %get-tuple-element.32.refs_2_), channel_id=1, source_target_pairs={{0,3},{1,0},{2,1},{3,2},{4,7},{5,4},{6,5},{7,6},{8,11},{9,8},{10,9... | collective-permute-start | bytes 196616 | tf_op jit(solution)/shard_map/ppermute | solution.py:746
  29.8 4.7 %collective-permute-start.6 = (f32[2,16,512]{2,1,0:T(8,128)S(1)}, f32[2,16,512]{2,1,0:T(8,128)S(1)}, u32[]{:S(2)}, u32[]{:S(2)}) collective-permute-start(f32[2,16,512]{2,1,0:T(8,128)S(1)} %get-tuple-element.32.refs_2_), channel_id=1, source_target_pairs={{0,2},{1,3},{2,0},{3,1},{4,6},{5,7},{6,4},{7,5},{8,10},{9,11},{10,... | collective-permute-start | bytes 196616 | tf_op jit(solution)/shard_map/ppermute | solution.py:746
  31.6 4.6 %collective-permute-start.5 = (f32[2,16,512]{2,1,0:T(8,128)S(1)}, f32[2,16,512]{2,1,0:T(8,128)S(1)}, u32[]{:S(2)}, u32[]{:S(2)}) collective-permute-start(f32[2,16,512]{2,1,0:T(8,128)S(1)} %get-tuple-element.32.refs_2_), channel_id=1, source_target_pairs={{0,1},{1,2},{2,3},{3,0},{4,5},{5,6},{6,7},{7,4},{8,9},{9,10},{10,1... | collective-permute-start | bytes 196616 | tf_op jit(solution)/shard_map/ppermute | solution.py:746
  36.8 14.0 %collective-permute-start.8 = (f32[128,512]{1,0:T(8,128)S(1)}, f32[128,512]{1,0:T(8,128)S(1)}, u32[]{:S(2)}, u32[]{:S(2)}) collective-permute-start(f32[128,512]{1,0:T(8,128)S(1)} %get-tuple-element.37), channel_id=1, source_target_pairs={{0,64},{1,65},{2,66},{3,67},{4,68},{5,69},{6,70},{7,71},{8,72},{9,... | collective-permute-start | bytes 786440 | tf_op jit(solution)/shard_map/ppermute | solution.py:746
  37.3 13.6 %collective-permute-start.9 = (f32[4,16,512]{2,1,0:T(8,128)S(1)}, f32[4,16,512]{2,1,0:T(8,128)S(1)}, u32[]{:S(2)}, u32[]{:S(2)}) collective-permute-start(f32[4,16,512]{2,1,0:T(8,128)S(1)} %get-tuple-element.38.refs_2_), channel_id=1, source_target_pairs={{0,64},{1,65},{2,66},{3,67},{4,68},{5,69},{6,70},{7,71},{8,72},{9,... | collective-permute-start | bytes 393224 | tf_op jit(solution)/shard_map/ppermute | solution.py:746
  39.9 11.0 %collective-permute-start.11 = (f32[2,16,512]{2,1,0:T(8,128)S(1)}, f32[2,16,512]{2,1,0:T(8,128)S(1)}, u32[]{:S(2)}, u32[]{:S(2)}) collective-permute-start(f32[2,16,512]{2,1,0:T(8,128)S(1)} %get-tuple-element.34.refs_0_), channel_id=1, source_target_pairs={{0,68},{1,69},{2,70},{3,71},{4,64},{5,65},{6,66},{7,67},{8,76},{9,... | collective-permute-start | bytes 196616 | tf_op jit(solution)/shard_map/ppermute | solution.py:746
  39.9 11.0 %collective-permute-start.10 = (f32[2,16,512]{2,1,0:T(8,128)S(1)}, f32[2,16,512]{2,1,0:T(8,128)S(1)}, u32[]{:S(2)}, u32[]{:S(2)}) collective-permute-start(f32[2,16,512]{2,1,0:T(8,128)S(1)} %get-tuple-element.34.refs_0_), channel_id=1, source_target_pairs={{0,4},{1,5},{2,6},{3,7},{4,0},{5,1},{6,2},{7,3},{8,12},{9,13},{10,... | collective-permute-start | bytes 196616 | tf_op jit(solution)/shard_map/ppermute | solution.py:746
  51.5 9.9 %collective-permute-start.12 = (f32[128,512]{1,0:T(8,128)S(1)}, f32[128,512]{1,0:T(8,128)S(1)}, u32[]{:S(2)}, u32[]{:S(2)}) collective-permute-start(f32[128,512]{1,0:T(8,128)S(1)} %get-tuple-element.47), channel_id=1, source_target_pairs={{0,64},{1,65},{2,66},{3,67},{4,68},{5,69},{6,70},{7,71},{8,72},{9,... | collective-permute-start | bytes 786440 | tf_op jit(solution)/shard_map/ppermute | solution.py:746
  51.9 9.5 %collective-permute-start.15 = (f32[2,16,512]{2,1,0:T(8,128)S(1)}, f32[2,16,512]{2,1,0:T(8,128)S(1)}, u32[]{:S(2)}, u32[]{:S(2)}) collective-permute-start(f32[2,16,512]{2,1,0:T(8,128)S(1)} %get-tuple-element.40.refs_0_.refs_4_), channel_id=1, source_target_pairs={{0,24},{1,25},{2,26},{3,27},{4,28},{5,29},{6,30},{7,31},{8,0},{9,1... | collective-permute-start | bytes 196616 | tf_op jit(solution)/shard_map/ppermute | solution.py:746
  54.3 7.1 %collective-permute-start.14 = (f32[2,16,512]{2,1,0:T(8,128)S(1)}, f32[2,16,512]{2,1,0:T(8,128)S(1)}, u32[]{:S(2)}, u32[]{:S(2)}) collective-permute-start(f32[2,16,512]{2,1,0:T(8,128)S(1)} %get-tuple-element.40.refs_0_.refs_4_), channel_id=1, source_target_pairs={{0,16},{1,17},{2,18},{3,19},{4,20},{5,21},{6,22},{7,23},{8,24},{9,... | collective-permute-start | bytes 196616 | tf_op jit(solution)/shard_map/ppermute | solution.py:746
  54.3 7.1 %collective-permute-start.13 = (f32[2,16,512]{2,1,0:T(8,128)S(1)}, f32[2,16,512]{2,1,0:T(8,128)S(1)}, u32[]{:S(2)}, u32[]{:S(2)}) collective-permute-start(f32[2,16,512]{2,1,0:T(8,128)S(1)} %get-tuple-element.40.refs_0_.refs_4_), channel_id=1, source_target_pairs={{0,8},{1,9},{2,10},{3,11},{4,12},{5,13},{6,14},{7,15},{8,16},{9,17... | collective-permute-start | bytes 196616 | tf_op jit(solution)/shard_map/ppermute | solution.py:746
  54.8 6.6 %copy-start.1 = (bf16[2,512,512]{2,1,0:T(8,128)(2,1)S(1)}, bf16[2,512,512]{2,1,0:T(8,128)(2,1)}, u32[]{:S(2)}) copy-start(bf16[2,512,512]{2,1,0:T(8,128)(2,1)} %constant.104.clone.refs_12_.refs_2_) | copy-start | bytes 3145732
  54.8 6.6 %copy-start.2 = (bf16[2,512,512]{2,1,0:T(8,128)(2,1)S(1)}, bf16[2,512,512]{2,1,0:T(8,128)(2,1)}, u32[]{:S(2)}) copy-start(bf16[2,512,512]{2,1,0:T(8,128)(2,1)} %constant.103.clone.refs_11_.refs_1_) | copy-start | bytes 3145732
  54.9 6.6 %copy-start.10 = (bf16[256,256]{1,0:T(8,128)(2,1)S(1)}, bf16[256,256]{1,0:T(8,128)(2,1)}, u32[]{:S(2)}) copy-start(bf16[256,256]{1,0:T(8,128)(2,1)} %constant.108.clone.refs_14_.refs_4_) | copy-start | bytes 393220
  54.9 6.6 %copy-start.11 = (bf16[256,256]{1,0:T(8,128)(2,1)S(1)}, bf16[256,256]{1,0:T(8,128)(2,1)}, u32[]{:S(2)}) copy-start(bf16[256,256]{1,0:T(8,128)(2,1)} %constant.107.clone.refs_13_.refs_3_) | copy-start | bytes 393220
  54.9 6.6 %copy-start.16 = (f32[2,16,16]{2,1,0:T(8,128)S(1)}, f32[2,16,16]{2,1,0:T(8,128)}, u32[]{:S(2)}) copy-start(f32[2,16,16]{2,1,0:T(8,128)} %constant.112.clone.refs_16_) | copy-start | bytes 6148
  66.0 7.2 %collective-permute-start.16 = (f32[4,512,128]{2,1,0:T(8,128)S(1)}, f32[4,512,128]{2,1,0:T(8,128)S(1)}, u32[]{:S(2)}, u32[]{:S(2)}) collective-permute-start(f32[4,512,128]{2,1,0:T(8,128)S(1)} %get-tuple-element.50), channel_id=1, source_target_pairs={{0,32},{1,33},{2,34},{3,35},{4,36},{5,37},{6,38},{7,39},{8,40},{9,... | collective-permute-start | bytes 3145736 | tf_op jit(solution)/shard_map/ppermute | solution.py:746
  68.6 3.0 %collective-permute-start.17 = (f32[512,256]{1,0:T(8,128)S(1)}, f32[512,256]{1,0:T(8,128)S(1)}, u32[]{:S(2)}, u32[]{:S(2)}) collective-permute-start(f32[512,256]{1,0:T(8,128)S(1)} %get-tuple-element.51.refs_0_), channel_id=1, source_target_pairs={{0,32},{1,33},{2,34},{3,35},{4,36},{5,37},{6,38},{7,39},{8,40},{9,... | collective-permute-start | bytes 1572872 | tf_op jit(solution)/shard_map/ppermute | solution.py:746

commit v3 on v2

--- a/solution.py
+++ b/solution.py
@@ -189,8 +189,8 @@
 
 
 def arrived_body(
-    s_ref, arrived, held, into_high, into_low, span_high, span_low, pivots, edge, basis_t, far,
-    planes, edges, carried, opening, sums,
+    s_ref, arrived, held, into_high, into_low, span_high, span_low, pivots, edge, basis_t, far, packs,
+    planes, edges, carried, opening, mixed, sums,
 ):
     count = held.shape[0]
     own = 2 * count
@@ -237,8 +237,16 @@
     odd = modal(total[1])
     edge_low = even + odd
     edge_high = even - odd
-    edges[0] = edge_high + far[s_ref[0]] * edge_low
-    edges[1] = edge_low + far[s_ref[0]] * edge_high
+    right = edge_high + far[s_ref[0]] * edge_low
+    left = edge_low + far[s_ref[0]] * edge_high
+    edges[0] = right
+    edges[1] = left
+    at = 0
+    for value in (right, left):
+        for _, lanes in pieces(half):
+            mixed[at : at + value.shape[0]] = value[:, lanes]
+            at += value.shape[0]
+    mixed[at:] = packs[...]
 
 
 def powers(s_ref, log_rho):
@@ -250,8 +258,7 @@
     return value.astype(jnp.float32)
 
 
-def z_body(s_ref, edges, got1, got2, got3, log_rho, carried, four, two, passed, *, width):
-    passed[...] = carried[...]
+def z_body(s_ref, edges, mixed, got2, got3, log_rho, four, two, *, width):
     power = powers(s_ref, log_rho)
     zi = s_ref[5]
     wide = float(width)
@@ -260,13 +267,27 @@
     high_sum = jnp.zeros_like(right)
     right4 = power(wide * scalar(Z_RING - 1 - zi)) * right
     left4 = power(wide * scalar(zi)) * left
-    for d, got in ((1, got1), (2, got2), (3, got3)):
-        before = scalar(zi >= d)
-        source = jnp.where(zi >= d, zi - d, zi - d + Z_RING)
-        low_sum = low_sum + before * power(wide * (d - 1)) * got[0]
-        high_sum = high_sum + (1.0 - before) * power(wide * (Z_RING - 1 - d)) * got[1]
-        right4 = right4 + power(wide * scalar(Z_RING - 1 - source)) * got[0]
-        left4 = left4 + power(wide * scalar(source)) * got[1]
+    size = right.shape[0]
+    lanes = mixed.shape[1]
+    pieces_of = right.shape[1] // lanes
+    first_right, first_left = (
+        jnp.concatenate(
+            [mixed[(k * pieces_of + c) * size : (k * pieces_of + c + 1) * size] for c in range(pieces_of)],
+            axis=1,
+        )
+        for k in range(2)
+    )
+    for d, got_right, got_left in (
+        (1, first_right, first_left), (2, got2[0], got2[1]), (3, got3[0], got3[1])
+    ):
+        source = jnp.bitwise_xor(zi, d)
+        before = scalar(source < zi)
+        gap = jnp.maximum(zi - source, source - zi) - 1
+        step = power(wide * scalar(gap))
+        low_sum = low_sum + before * step * got_right
+        high_sum = high_sum + (1.0 - before) * step * got_left
+        right4 = right4 + power(wide * scalar(Z_RING - 1 - source)) * got_right
+        left4 = left4 + power(wide * scalar(source)) * got_left
     hop = power(wide)
     per_rho = power(-1.0)
     four[0] = per_rho * low_sum + left + hop * high_sum
@@ -405,7 +426,7 @@
         mine[2 * k + 1] = cells[:, width:]
 
 
-def join_body(s_ref, mine, came, out, held, sems):
+def join_planes(s_ref, mine, came, out, held, sems):
     half = mine.shape[1]
     sign = (1 - 2 * s_ref[0]).astype(jnp.float32)
     copies = []
@@ -417,8 +438,7 @@
         copy = pltpu.make_async_copy(held.at[z], out.at[z], sems.at[z])
         copy.start()
         copies.append(copy)
-    for copy in copies:
-        copy.wait()
+    return copies
 
 
 def edge_body(s_ref, conductivity, temp, phase, gas, cond, packs, along, packed):
@@ -452,8 +472,9 @@
     turned = packed[...].T
     turned_gas = pltpu.roll(gas[...], 2, 1).T[:8]
     for h, at in pieces(rows):
-        packs[h, :last] = turned[:, at]
-        packs[h, last:] = turned_gas[:, at]
+        base = h * (last + 8)
+        packs[base : base + last] = turned[:, at]
+        packs[base + last : base + last + 8] = turned_gas[:, at]
     along[last : last + 8] = jnp.concatenate(
         [gas[rows - 2 :], gas[:2], jnp.zeros((4, width), jnp.float32)], axis=0
     )
@@ -463,13 +484,22 @@
     return [(h, slice(h * 128, h * 128 + 128)) for h in range(length // 128)]
 
 
-def column(ref, depth, kind, k):
-    at = pl.ds(4 * depth * kind + k, depth, stride=4)
-    return jnp.concatenate([ref[h, at] for h in range(ref.shape[0])], axis=1)
-
-
-def flat(ref, row):
-    return jnp.concatenate([ref[h, row : row + 1] for h in range(ref.shape[0])], axis=1)
+def column(source, depth, kind, k):
+    ref, base, size = source
+    at = lambda h: pl.ds(base + h * size + 4 * depth * kind + k, depth, stride=4)
+    return jnp.concatenate([ref[at(h)] for h in range((ref.shape[0] - base) // size)], axis=1)
+
+
+def flat(source, row):
+    ref, base, size = source
+    at = lambda h: base + h * size + row
+    count = (ref.shape[0] - base) // size
+    return jnp.concatenate([ref[at(h) : at(h) + 1] for h in range(count)], axis=1)
+
+
+def sources(packs, mixed, far_x, depth):
+    size = 8 * depth + 8
+    return (packs, 0, size), (mixed, mixed.shape[0] - packs.shape[0], size), (far_x, 0, size)
 
 
 def interleave(ref, odd, even):
@@ -485,17 +515,14 @@
     return jnp.where(even, column(a, depth, kind, k), column(b, depth, kind, k))
 
 
-def pass_body(s_ref, value, out):
-    out[...] = value[...]
-
-
-def corner_body(s_ref, along, near_x, far_x, out):
+def corner_body(s_ref, along, packs, mixed, far, out):
     depth = (along.shape[0] - 8) // 8
     width = along.shape[1]
+    _, near_x, far_x = sources(packs, mixed, far, depth)
     out[: along.shape[0]] = along[...]
     lane = lax.broadcasted_iota(jnp.int32, (depth, width), 1)
     block = jnp.zeros((depth, width), jnp.float32)
-    rows = near_x.shape[0] * near_x.shape[2]
+    rows = packs.shape[0] // (8 * depth + 8) * 128
     spot = 0
     for y in (rows - 1, 0):
         for kind in range(2):
@@ -540,7 +567,13 @@
     return temp + (0.5 * STEP_RATE) * total + surface
 
 
-def step_planes(temp, cond, up, down, cond_up, cond_down, inflow, emit):
+def entering(inflow, z, at, lane):
+    width = lane.shape[1]
+    moved = pltpu.roll(inflow[at], width - (2 * z + 1), 1)
+    return jnp.where((lane == 0) | (lane == width - 1), moved, 0.0)
+
+
+def step_planes(temp, cond, up, down, cond_up, cond_down, inflow, emit, starts):
     depth, rows, width = temp.shape
     lane = lax.broadcasted_iota(jnp.int32, (CHUNK, width), 1)
     end = width - 1
@@ -559,7 +592,7 @@
     def plane(z, first):
         before = jnp.maximum(z - 1, 0)
         after = jnp.minimum(z + 1, depth - 1)
-        for start in range(0, rows, CHUNK):
+        for start in starts:
             at = slice(start, start + CHUNK)
             here = temp[z, at]
             own = cond[z, at]
@@ -576,9 +609,8 @@
             pairs.append(pair)
             flow = jnp.where(lane == end, 0.0, pair * (pltpu.roll(here, end, 1) - here))
             total = total + (flow - pltpu.roll(flow, 1, 1))
-            spot = width - (2 * z + 1)
-            entering = pltpu.roll(inflow[at], spot, 1)
-            total = total + jnp.where((lane == 0) | (lane == end), entering, 0.0)
+            if inflow is not None:
+                total = total + entering(inflow, z, at, lane)
             emit(z, start, first, here + (0.5 * STEP_RATE) * total, pairs)
 
     plane(0, True)
@@ -590,79 +622,97 @@
     lax.fori_loop(1, depth, later, 0)
 
 
-def first_body(
-    s_ref, temp, cond, gas, packs, along, near_x, far_x, near_y, far_y,
-    out, base_flow, face, base_lines, cond_lines, packed, flow, inflow, lines,
-):
-    depth, rows, width = temp.shape
-    end = width - 1
-    settle(s_ref, lines, near_y, far_y)
-    last = 8 * depth
-    own = lambda k: tuple(column(packs, depth, kind, k) for kind in range(2))
-    left = lambda k: tuple(side_columns(s_ref, near_x, far_x, depth, kind, k, True) for kind in range(2))
-    right = lambda k: tuple(side_columns(s_ref, near_x, far_x, depth, kind, k, False) for kind in range(2))
-    line = lambda ref, k: tuple(
-        ref[4 * depth * kind + depth * k : 4 * depth * kind + depth * (k + 1)] for kind in range(2)
-    )
-    above = lambda k: line(lines.at[0], k)
-    below = lambda k: line(lines.at[1], k)
-    corner = lambda which, spot: tuple(
-        lines[which, last + 8 :][:, at : at + 1] for at in (spot, spot + 2)
-    )
-    even = s_ref[8] == 0
-    gas_left = jnp.where(even, flat(far_x, last + 1), flat(near_x, last + 1))
-    gas_right = jnp.where(even, flat(near_x, last + 2), flat(far_x, last + 2))
-    at_lane = lambda pair, lane: tuple(v[:, lane : lane + 1] for v in pair)
-    up_line, down_line = above(1), below(2)
-    out_left = rim(*left(1), left(0), own(2), corner(0, 0), corner(1, 4), gas_left)
-    out_right = rim(*right(2), right(3), own(1), corner(0, 1), corner(1, 5), gas_right)
-    in_left = rim(
-        *own(2), left(1), own(3), at_lane(up_line, 0), at_lane(down_line, 0), flat(packs, last + 2)
-    )
-    in_right = rim(
-        *own(1), right(2), own(0), at_lane(up_line, end), at_lane(down_line, end),
-        flat(packs, last + 1),
-    )
-    base_lines[0] = rim(
-        *up_line, above(0), line(along, 2), corner(0, 0), corner(0, 1), lines[0, last + 1 : last + 2]
-    )
-    base_lines[1] = rim(
-        *down_line, below(3), line(along, 1), corner(1, 4), corner(1, 5), lines[1, last + 2 : last + 3]
-    )
-    cond_lines[0] = up_line[1]
-    cond_lines[1] = down_line[1]
-    left_pair = own(2)[1] + left(1)[1]
-    right_pair = own(1)[1] + right(2)[1]
-    interleave(face, left_pair, right_pair)
-    interleave(flow, left_pair * (left(1)[0] - own(2)[0]), right_pair * (right(2)[0] - own(1)[0]))
-    interleave(base_flow, left_pair * (out_left - in_left), right_pair * (out_right - in_right))
-    packed[...] = jnp.zeros_like(packed)
-    inflow[...] = to_columns(packed, flow)
-
+def inflow_rows(s_ref, packs, near_x, far_x, flow, depth):
+    own = lambda kind, k: column(packs, depth, kind, k)
+    side = lambda kind, k, left: side_columns(s_ref, near_x, far_x, depth, kind, k, left)
+    left_pair = own(1, 2) + side(1, 1, True)
+    right_pair = own(1, 1) + side(1, 2, False)
+    interleave(
+        flow,
+        left_pair * (side(0, 1, True) - own(0, 2)),
+        right_pair * (side(0, 2, False) - own(0, 1)),
+    )
+    return left_pair, right_pair
+
+
+def base_emit(temp, gas, out):
     def emit(z, start, first, value, pairs):
         at = slice(start, start + CHUNK)
         if first:
             value = value + (STEP_RATE * HEAT_TRANSFER) * (gas[at] - temp[0, at])
         out[z, at] = value
 
-    span = lambda which, kind, k: lines.at[
-        which, 4 * depth * kind + depth * k : 4 * depth * kind + depth * (k + 1)
-    ]
+    return emit
+
+
+def inner_body(s_ref, temp, cond, gas, out):
+    rows = temp.shape[1]
     step_planes(
-        temp, cond, span(0, 0, 1), span(1, 0, 2), span(0, 1, 1), span(1, 1, 2), inflow, emit
-    )
-
-
-def second_body(
-    s_ref, base, cond, temp, gas, base_flow, face_rows, base_lines, cond_lines,
-    out, top, weights, held, sems, packed, inflow, face,
-):
-    depth, rows, width = base.shape
+        temp, cond, None, None, None, None, None, base_emit(temp, gas, out),
+        range(CHUNK, rows - CHUNK, CHUNK),
+    )
+
+
+def tile_rims(mine, near_x, far_x, along, lines, depth, width, side):
+    last = 8 * depth
+    own = lambda k: tuple(column(mine, depth, kind, k) for kind in range(2))
+    left = lambda k: tuple(side(depth, kind, k, True) for kind in range(2))
+    right = lambda k: tuple(side(depth, kind, k, False) for kind in range(2))
+    zero = jnp.zeros((depth, 1), jnp.float32)
+    if lines is None:
+        corner = lambda which, spot: (zero, zero)
+        at_lane = lambda pair, lane: (zero, zero)
+        up_line = down_line = None
+    else:
+        line = lambda ref, k: tuple(
+            ref[4 * depth * kind + depth * k : 4 * depth * kind + depth * (k + 1)] for kind in range(2)
+        )
+        corner = lambda which, spot: tuple(
+            lines[which, last + 8 :][:, at : at + 1] for at in (spot, spot + 2)
+        )
+        at_lane = lambda pair, lane: tuple(v[:, lane : lane + 1] for v in pair)
+        up_line, down_line = line(lines.at[0], 1), line(lines.at[1], 2)
+    gas_left, gas_right = side.gas
+    out_left = rim(*left(1), left(0), own(2), corner(0, 0), corner(1, 4), gas_left)
+    out_right = rim(*right(2), right(3), own(1), corner(0, 1), corner(1, 5), gas_right)
+    in_left = rim(
+        *own(2), left(1), own(3), at_lane(up_line, 0), at_lane(down_line, 0), flat(mine, last + 2)
+    )
+    in_right = rim(
+        *own(1), right(2), own(0), at_lane(up_line, width - 1), at_lane(down_line, width - 1),
+        flat(mine, last + 1),
+    )
+    if lines is None:
+        return out_left - in_left, out_right - in_right, None, None
+    upper = rim(
+        *up_line, line(lines.at[0], 0), line(along, 2), corner(0, 0), corner(0, 1),
+        lines[0, last + 1 : last + 2],
+    )
+    lower = rim(
+        *down_line, line(lines.at[1], 3), line(along, 1), corner(1, 4), corner(1, 5),
+        lines[1, last + 2 : last + 3],
+    )
+    return out_left - in_left, out_right - in_right, upper, lower
+
+
+class Sides:
+    def __init__(self, s_ref, near_x, far_x, depth):
+        self.s_ref, self.near_x, self.far_x = s_ref, near_x, far_x
+        last = 8 * depth
+        even = s_ref[8] == 0
+        self.gas = (
+            jnp.where(even, flat(far_x, last + 1), flat(near_x, last + 1)),
+            jnp.where(even, flat(near_x, last + 2), flat(far_x, last + 2)),
+        )
+
+    def __call__(self, depth, kind, k, left):
+        return side_columns(self.s_ref, self.near_x, self.far_x, depth, kind, k, left)
+
+
+def final_emit(temp, gas, face, held, weights, done):
+    rows, width = held.shape[1:]
     lane = lax.broadcasted_iota(jnp.int32, (CHUNK, width), 1)
     end = width - 1
-    packed[...] = jnp.zeros_like(packed)
-    inflow[...] = to_columns(packed, base_flow)
-    face[...] = to_columns(packed, face_rows)
 
     def emit(z, start, first, value, pairs):
         at = slice(start, start + CHUNK)
@@ -675,6 +725,70 @@
             for k, pair in enumerate((pairs[0], pairs[1], left, right, pairs[3])):
                 weights[k, at] = (0.5 * STEP_RATE) * pair
         held[z, at] = value
+        done(z, start, first)
+
+    return emit
+
+
+def middle_body(
+    s_ref, base_in, temp, cond, gas, packs, mixed, far, base, held, weights,
+    packed, flow, inflow, face,
+):
+    depth, rows, width = temp.shape
+    lane = lax.broadcasted_iota(jnp.int32, (CHUNK, width), 1)
+    mine, near_x, far_x = sources(packs, mixed, far, depth)
+    left_pair, right_pair = inflow_rows(s_ref, mine, near_x, far_x, flow, depth)
+    packed[...] = jnp.zeros_like(packed)
+    inflow[...] = to_columns(packed, flow)
+
+    def mend(z, nothing):
+        for start in range(CHUNK, rows - CHUNK, CHUNK):
+            at = slice(start, start + CHUNK)
+            base[z, at] = base_in[z, at] + (0.5 * STEP_RATE) * entering(inflow, z, at, lane)
+        return nothing
+
+    lax.fori_loop(0, depth, mend, 0)
+    side = Sides(s_ref, near_x, far_x, depth)
+    left_step, right_step, _, _ = tile_rims(mine, near_x, far_x, None, None, depth, width, side)
+    interleave(flow, left_pair * left_step, right_pair * right_step)
+    inflow[...] = to_columns(packed, flow)
+    interleave(flow, left_pair, right_pair)
+    face[...] = to_columns(packed, flow)
+    step_planes(
+        base, cond, None, None, None, None, inflow,
+        final_emit(temp, gas, face, held, weights, lambda z, start, first: None),
+        range(2 * CHUNK, rows - 2 * CHUNK, CHUNK),
+    )
+
+
+def outer_body(
+    s_ref, base_in, held_in, weights_in, temp, cond, gas, packs, along, mixed, far, near_y, far_y,
+    base, held, weights, out, top, sems, packed, flow, inflow, face, lines, base_lines,
+):
+    depth, rows, width = temp.shape
+    settle(s_ref, lines, near_y, far_y)
+    mine, near_x, far_x = sources(packs, mixed, far, depth)
+    left_pair, right_pair = inflow_rows(s_ref, mine, near_x, far_x, flow, depth)
+    packed[...] = jnp.zeros_like(packed)
+    inflow[...] = to_columns(packed, flow)
+    side = Sides(s_ref, near_x, far_x, depth)
+    left_step, right_step, base_lines[0], base_lines[1] = tile_rims(
+        mine, near_x, far_x, along, lines, depth, width, side
+    )
+    span = lambda which, kind, k: lines.at[
+        which, 4 * depth * kind + depth * k : 4 * depth * kind + depth * (k + 1)
+    ]
+    cond_up, cond_down = span(0, 1, 1), span(1, 1, 2)
+    step_planes(
+        temp, cond, span(0, 0, 1), span(1, 0, 2), cond_up, cond_down, inflow,
+        base_emit(temp, gas, base), (0, rows - CHUNK),
+    )
+    interleave(flow, left_pair * left_step, right_pair * right_step)
+    inflow[...] = to_columns(packed, flow)
+    interleave(flow, left_pair, right_pair)
+    face[...] = to_columns(packed, flow)
+
+    def done(z, start, first):
         if not first and start + CHUNK == rows:
 
             @pl.when(z >= 2)
@@ -682,8 +796,9 @@
                 pltpu.make_async_copy(held.at[z], out.at[z], sems.at[z]).start()
 
     step_planes(
-        base, cond, base_lines.at[0], base_lines.at[1], cond_lines.at[0], cond_lines.at[1],
-        inflow, emit,
+        base, cond, base_lines.at[0], base_lines.at[1], cond_up, cond_down, inflow,
+        final_emit(temp, gas, face, held, weights, done),
+        (0, CHUNK, rows - 2 * CHUNK, rows - CHUNK),
     )
     top[...] = held[:2]
     for z in range(2, depth):
@@ -700,7 +815,9 @@
     )
 
 
-def wall_body(s_ref, ours, theirs, weights, base, filled, out, held, sem):
+def finish_body(
+    s_ref, ours, theirs, weights, base, mine, came, filled, pressure, out, held, sem, joined, sems
+):
     half = ours.shape[0]
     rows, width = weights.shape[1:]
     sign = (1 - 2 * s_ref[0]).astype(jnp.float32)
@@ -733,6 +850,8 @@
     held[1] = base[1] + down
     copy = pltpu.make_async_copy(held, out.at[:2], sem)
     copy.start()
+    for other in join_planes(s_ref, mine, came, pressure, joined, sems):
+        other.wait()
     copy.wait()
 
 
@@ -784,71 +903,76 @@
     (pivots,) = run(
         pivot_body, 1.2, scalars, [], [const["lam"], const["sigma"]], [(3 * own + 2, width, half)]
     )
-    cond, packs, along = run(
-        edge_body, 2.8, scalars, [pivots], [solid_temp, phase_map, gas_wall_temp],
-        [(depth, tile_rows, width), (halves_of, 8 * depth + 8, 128), (8 * depth + 8, width)],
-        scratch=[column_scratch], small=[phase_conductivity],
-    )
-    near_x = [move(packs, near_pair), move(packs, far_pair)]
     folded = jax.ShapeDtypeStruct((depth_loc, half, width), jnp.float32)
     away, kept = run_blocks(
-        fold_body, 0.8, scalars, [along, pressure_source], [ORDER, plane_of(pressure_source)],
+        fold_body, 0.8, scalars, [pivots, pressure_source], [ORDER, plane_of(pressure_source)],
         [folded.shape, folded.shape], [plane_of(folded), plane_of(folded)], depth_loc,
     )
     arrived = move(away, other_core)
     (held,) = run(
         held_body, 2.1, scalars, [], [kept, *into, *span], [(depth_loc, width, half)]
     )
-    (lines,) = run(
-        corner_body, 0.6, scalars, [held], [along, *near_x], [(9 * depth + 8, width)]
-    )
-    near_y = [move(lines, flip(1)), move(lines, flip(3))]
-    planes, edges, carried, opening = run(
-        arrived_body, 3.4, scalars, [lines],
-        [arrived, held, *into, *span, pivots, const["edge"], const["basis_t"], const["far"]],
-        [(own, width, half), (2, depth, half), (width, half), (width, half)],
+    cond, packs, along = run(
+        edge_body, 2.8, scalars, [held], [solid_temp, phase_map, gas_wall_temp],
+        [(depth, tile_rows, width), (halves_of * (8 * depth + 8), 128), (8 * depth + 8, width)],
+        scratch=[column_scratch], small=[phase_conductivity],
+    )
+    planes, edges, carried, opening, mixed = run(
+        arrived_body, 3.4, scalars, [],
+        [arrived, held, *into, *span, pivots, const["edge"], const["basis_t"], const["far"],
+         packs],
+        [(own, width, half), (2, depth, half), (width, half), (width, half),
+         (2 * depth * half // 128 + packs.shape[0], 128)],
         scratch=[pltpu.VMEM((2, depth, 8, half), jnp.float32)],
     )
-    z_got = [
-        move(edges, lambda g, p, d=d: (g, p // Z_RING * Z_RING + (p + d) % Z_RING))
-        for d in range(1, Z_RING)
-    ]
+    mixed = move(mixed, near_pair)
+    z_got = [move(edges, lambda g, p, d=d: (g, p ^ d)) for d in range(2, Z_RING)]
+    far_x = move(packs, far_pair)
+    carried_there = move(carried, other_half)
     log_rho = const["log_rho"]
     pair_shape = edges.shape
-    four, two, carried = run(
-        functools.partial(z_body, width=width), 0.6, scalars, near_y,
-        [edges, *z_got, log_rho, carried], [(4,) + pair_shape[1:], pair_shape, carried.shape],
-    )
-    carried_there = move(carried, other_half)
+    (base,) = run(
+        inner_body, 4.5, scalars, [edges], [solid_temp, cond, gas_wall_temp],
+        [(depth, tile_rows, width)],
+    )
+    four, two = run(
+        functools.partial(z_body, width=width), 0.6, scalars, [far_x, carried_there, base],
+        [edges, mixed, *z_got, log_rho], [(4,) + pair_shape[1:], pair_shape],
+    )
     there = move(four, other_half)
     beside1 = move(two, lambda g, p: (g, p ^ Z_RING))
     beside2 = move(two, lambda g, p: (g ^ 2, p ^ Z_RING))
-    base, base_flow, face, base_lines, cond_lines = run(
-        first_body, 6.6, scalars, [two],
-        [solid_temp, cond, gas_wall_temp, packs, along, *near_x, *near_y],
-        [(depth, tile_rows, width), (halves_of, 2 * depth, 128), (halves_of, 2 * depth, 128),
-         (2, depth, width), (2, depth, width)],
-        scratch=[
-            row_scratch, pltpu.VMEM((halves_of, 2 * depth, 128), jnp.float32), column_scratch,
-            pltpu.VMEM((2, 9 * depth + 8, width), jnp.float32),
-        ],
+    (lines,) = run(
+        corner_body, 0.6, scalars, [two], [along, packs, mixed, far_x], [(9 * depth + 8, width)]
+    )
+    near_y = [move(lines, flip(1)), move(lines, flip(3))]
+    flow_scratch = pltpu.VMEM((halves_of, 2 * depth, 128), jnp.float32)
+    tile = (depth, tile_rows, width)
+    base, begun, weights = run(
+        middle_body, 4.5, scalars, [lines],
+        [base, solid_temp, cond, gas_wall_temp, packs, mixed, far_x],
+        [tile, tile, (5, tile_rows, width)],
+        scratch=[row_scratch, flow_scratch, column_scratch, column_scratch],
+        aliases={2: 0},
     )
     run8, part, opening = run(
-        functools.partial(y_body, width=width), 0.6, scalars, [base, carried_there],
+        functools.partial(y_body, width=width), 0.6, scalars, [base, *near_y],
         [four, there, beside1, beside2, log_rho, opening], [pair_shape, pair_shape, opening.shape],
     )
     block = Z_RING * Y_PAIR
     opening_there = move(opening, other_half)
     x_got = [move(run8, lambda g, p, d=d: (g, (p + block * d) % pencils)) for d in range(1, X_RING)]
-    final, top, weights = run(
-        second_body, 6.5, scalars, [run8],
-        [base, cond, solid_temp, gas_wall_temp, base_flow, face, base_lines, cond_lines],
-        [solid_temp.shape, (2, tile_rows, width), (5, tile_rows, width)],
+    _, _, weights, final, top = run(
+        outer_body, 5.5, scalars, [run8],
+        [base, begun, weights, solid_temp, cond, gas_wall_temp, packs, along, mixed, far_x, *near_y],
+        [tile, tile, (5, tile_rows, width), solid_temp.shape, (2, tile_rows, width)],
         scratch=[
-            pltpu.VMEM((depth, tile_rows, width), jnp.float32), pltpu.SemaphoreType.DMA((depth,)),
-            row_scratch, column_scratch, column_scratch,
+            pltpu.SemaphoreType.DMA((depth,)),
+            row_scratch, flow_scratch, column_scratch, column_scratch,
+            pltpu.VMEM((2, 9 * depth + 8, width), jnp.float32),
+            pltpu.VMEM((2, depth, width), jnp.float32),
         ],
-        out_specs=[ORDER, FAST, FAST],
+        out_specs=[FAST, FAST, FAST, ORDER, FAST], aliases={2: 0, 3: 1, 4: 2},
     )
     wall, away, keep = run(
         solve_body, 6.9, scalars, [weights],
@@ -864,16 +988,14 @@
     wall_came = move(wall, other_core)
     came = move(away, other_core)
     (mine,) = run(cells_body, 2.2, scalars, [], [keep, *span_t, *back], [(depth_loc, half, width)])
-    (pressure,) = run(
-        join_body, 1.9, scalars, [], [mine, came], [pressure_source.shape], out_specs=[ORDER],
+    pressure, final = run(
+        finish_body, 2.5, scalars, [], [wall, wall_came, weights, top, mine, came, (final, ORDER)],
+        [pressure_source.shape, final.shape],
         scratch=[
-            pltpu.VMEM(pressure_source.shape, jnp.float32), pltpu.SemaphoreType.DMA((depth_loc,))
+            pltpu.VMEM(top.shape, jnp.float32), pltpu.SemaphoreType.DMA,
+            pltpu.VMEM(pressure_source.shape, jnp.float32), pltpu.SemaphoreType.DMA((depth_loc,)),
         ],
-    )
-    (final,) = run(
-        wall_body, 1.5, scalars, [], [wall, wall_came, weights, top, (final, ORDER)], [final.shape],
-        scratch=[pltpu.VMEM(top.shape, jnp.float32), pltpu.SemaphoreType.DMA],
-        out_specs=[ORDER], aliases={5: 0},
+        out_specs=[ORDER, ORDER], aliases={7: 1},
     )
     return (pressure, final)
 

time: 75.6 us -> 70 us (0.926)
  waiting for transfers between devices: 13.4 us -> 4.96 us
  Pallas kernels: 34.5 us -> 37.8 us
    ppermute x18 -> x17, waiting for transfers between devices: 13.4 us -> 4.96 us  [move(): return lax.ppermute(value, ('grp', 'pen'), pairs)]
    pallas_call x13, Pallas kernels: 33.7 us -> 37.1 us  [run(): pl.pallas_call(inner, out_shape=outs, in_specs=specs, out_specs=out_specs...]
    ppermute x18 -> x17, starting transfers between devices: 23.3 us -> 23.6 us  [move(): return lax.ppermute(value, ('grp', 'pen'), pairs)]
  transfers between devices with their start and end apart: 18 -> 17, of which waited for: 7 -> 2; matrix products, arithmetic and copies ran while one was open for 0% -> 0% of each run, Pallas kernels for 29% -> 35%
where the time goes in v3:
time: 70 us; the launch traced here: 69.7 us
  Pallas kernels  37.8 us (54%)
  starting transfers between devices  23.6 us (34%)
  waiting for transfers between devices  4.96 us (7%)
  local copies, waits for them, and re-layouts  2.33 us (3%)
  between operations  1.04 us (1%)
    pallas_call x13, Pallas kernels, run(): pl.pallas_call(inner, out_shape=outs, in_specs=specs, out_specs=out_specs...  37.1 us
    ppermute x17, starting transfers between devices, move(): return lax.ppermute(value, ('grp', 'pen'), pairs)  23.6 us
    ppermute x17, waiting for transfers between devices, move(): return lax.ppermute(value, ('grp', 'pen'), pairs)  4.96 us
    unnamed x40, local copies, waits for them, and re-layouts  2.25 us
  transfers between devices with their start and end apart: 17, of which 2 were waited for; matrix products, arithmetic and copies ran while one was open for 0% of the time, Pallas kernels for 35%

profile of v3, /device:TPU:1, one launch (start us, length us, event | category | flops | bytes accessed | tf_op | source)
XLA Modules:
  0.0 69.7 jit_solution(3925162058677730420)
XLA Ops:
  0.7 0.1 stack.33.s_ref
  0.8 1.0 %copy-done.14 = f32[128,512]{1,0:T(8,128)S(1)} copy-done((f32[128,512]{1,0:T(8,128)S(1)}, f32[128,512]{1,0:T(8,128)}, u32[]{:S(2)}) %copy-start.14) | copy-done | bytes 262168
  1.7 0.7 copy-done.18
  2.4 1.2 %shard_map.203.after.refs_6_.refs_10_ = f32[26,128,512]{2,1,0:T(8,128)S(1)} custom-call(s32[9]{0:T(128)S(1)} %stack.33.s_ref, f32[2,1,512]{2,1,0:T(1,128)S(1)} %copy-done.18, f32[128,512]{1,0:T(8,128)S(1)} %copy-done.14), custom_call_target="tpu_custom_call" | custom-call | flops 1 | bytes 442800 | tf_op jit(solution)/shard_map/pallas_call | solution.py:115
  3.6 0.4 copy-done.6
  4.0 0.8 %shard_map.204 = (f32[4,512,128]{2,1,0:T(8,128)S(1)}, f32[4,512,128]{2,1,0:T(8,128)S(1)}) custom-call(s32[9]{0:T(128)S(1)} %stack.33.s_ref, f32[26,128,512]{2,1,0:T(8,128)S(1)} %shard_map.203.after.refs_6_.refs_10_, f32[4,1024,128]{2,1,0:T(8,128)S(1)} %copy-done.6), custom_call_target="tpu_custom_call" | custom-call | flops 1 | bytes 295200 | tf_op jit(solution)/shard_map/pallas_call | solution.py:128
  4.8 1.5 %collective-permute-start.1 = (f32[4,512,128]{2,1,0:T(8,128)S(1)}, f32[4,512,128]{2,1,0:T(8,128)S(1)}, u32[]{:S(2)}, u32[]{:S(2)}) collective-permute-start(f32[4,512,128]{2,1,0:T(8,128)S(1)} %get-tuple-element.28), channel_id=1, source_target_pairs={{0,32},{1,33},{2,34},{3,35},{4,36},{5,37},{6,38},{7,39},{8,40},{9,... | collective-permute-start | bytes 3145736 | tf_op jit(solution)/shard_map/ppermute | solution.py:865
  6.3 0.0 copy-done.3
  6.3 0.0 copy-done.12
  6.3 0.0 copy-start
  6.4 0.0 copy-start.5
  6.4 0.0 copy-start.7
  6.4 0.0 copy-start.19
  6.4 2.1 %shard_map.205.refs_1_ = f32[4,128,512]{2,1,0:T(8,128)S(1)} custom-call(s32[9]{0:T(128)S(1)} %stack.33.s_ref, f32[4,512,128]{2,1,0:T(8,128)S(1)} %get-tuple-element.26.refs_0_, bf16[256,256]{1,0:T(8,128)(2,1)S(1)} %copy-done.13, bf16[256,256]{1,0:T(8,128)(2,1)S(1)} %copy-done.12, bf16[2,512,512]{2,1,0:T(8,128)(2,1)S(1)} %copy-done.4, ...), custom_call_target="tpu_custom_call" | custom-call | flops 1 | bytes 774900 | tf_op jit(solution)/shard_map/pallas_call | solution.py:115
  8.5 0.0 copy-done
  8.5 0.0 copy-done.5
  8.5 0.1 copy-done.7
  8.6 2.8 %shard_map.206 = (f32[16,256,128]{2,1,0:T(8,128)S(1)}, f32[272,128]{1,0:T(8,128)S(1)}, f32[136,128]{1,0:T(8,128)S(1)}) custom-call(s32[9]{0:T(128)S(1)} %stack.33.s_ref, f32[2]{0:T(128)S(1)} %copy-done.19, f32[4,128,512]{2,1,0:T(8,128)S(1)} %shard_map.205.refs_1_, f32[16,256,128]{2,1,0:T(8,128)S(1)} %copy-done, s32[16,256,128]{2,1,0:T(8,128)S(1)} %copy-done.7, ...), custom_call_target="tpu_custom_call" | custom-call | flops 1 | bytes 1033200 | tf_op jit(solution)/shard_map/pallas_call | solution.py:115
  11.5 0.0 collective-permute-done.1.refs_0_
  11.5 0.0 copy-done.8
  11.5 0.0 copy-done.15
  11.5 3.5 %shard_map.207 = (f32[8,128,512]{2,1,0:T(8,128)S(1)}, f32[2,16,512]{2,1,0:T(8,128)S(1)}, f32[128,512]{1,0:T(8,128)S(1)}, f32[128,512]{1,0:T(8,128)S(1)}, f32[400,128]{1,0:T(8,128)S(1)}) custom-call(s32[9]{0:T(128)S(1)} %stack.33.s_ref, f32[4,512,128]{2,1,0:T(8,128)S(1)} %collective-permute-done.1.refs_0_, f32[4,128,512]{2,1,0:T(8,128)S(1)} %shard_map.205.refs_1_, ...), custom_call_target="tpu_custom_call" | custom-call | flops 1 | bytes 1254600 | tf_op jit(solution)/shard_map/pallas_call | solution.py:115
  15.0 3.1 %collective-permute-start.2 = (f32[128,512]{1,0:T(8,128)S(1)}, f32[128,512]{1,0:T(8,128)S(1)}, u32[]{:S(2)}, u32[]{:S(2)}) collective-permute-start(f32[128,512]{1,0:T(8,128)S(1)} %get-tuple-element.29), channel_id=1, source_target_pairs={{0,64},{1,65},{2,66},{3,67},{4,68},{5,69},{6,70},{7,71},{8,72},{9,... | collective-permute-start | bytes 786440 | tf_op jit(solution)/shard_map/ppermute | solution.py:865
  18.1 1.6 %collective-permute-start.3 = (f32[400,128]{1,0:T(8,128)S(1)}, f32[400,128]{1,0:T(8,128)S(1)}, u32[]{:S(2)}, u32[]{:S(2)}) collective-permute-start(f32[400,128]{1,0:T(8,128)S(1)} %get-tuple-element.32), channel_id=1, source_target_pairs={{0,1},{1,0},{2,3},{3,2},{4,5},{5,4},{6,7},{7,6},{8,9},{9,8},{10,11... | collective-permute-start | bytes 614408 | tf_op jit(solution)/shard_map/ppermute | solution.py:865
  19.7 4.6 %collective-permute-start = (f32[272,128]{1,0:T(8,128)S(1)}, f32[272,128]{1,0:T(8,128)S(1)}, u32[]{:S(2)}, u32[]{:S(2)}) collective-permute-start(f32[272,128]{1,0:T(8,128)S(1)} %get-tuple-element.27.refs_10_.refs_2_.refs_5_.refs_7_), channel_id=1, source_target_pairs={{0,31},{1,2},{2,1},{3,4},{4,3},{5,6},{6,5},{7,8},{8,7},{9,10},{10,... | collective-permute-start | bytes 417800 | tf_op jit(solution)/shard_map/ppermute | solution.py:865
  24.3 0.0 collective-permute-start.5
  24.3 0.2 collective-permute-start.4
  24.5 3.7 %shard_map.208.refs_2_.refs_1_ = f32[16,256,128]{2,1,0:T(8,128)S(1)} custom-call(s32[9]{0:T(128)S(1)} %stack.33.s_ref, f32[2,16,512]{2,1,0:T(8,128)S(1)} %get-tuple-element.30.refs_0_.refs_3_, f32[16,256,128]{2,1,0:T(8,128)S(1)} %copy-done, f32[16,256,128]{2,1,0:T(8,128)S(1)} %get-tuple-element.31.refs_2_.refs_3_.refs_5_, f32[256,128]{1,0:T(8,128)S(1)} %copy-done.5), custom_call_target="tpu_custom_call" | custom-call | flops 1 | bytes 1660500 | tf_op jit(solution)/shard_map/pallas_call | solution.py:115
  28.2 0.0 collective-permute-done.refs_0_.refs_4_.refs_7_.refs_10_
  28.2 4.2 %collective-permute-done.5.refs_6_ = f32[2,16,512]{2,1,0:T(8,128)S(1)} collective-permute-done((f32[2,16,512]{2,1,0:T(8,128)S(1)}, f32[2,16,512]{2,1,0:T(8,128)S(1)}, u32[]{:S(2)}, u32[]{:S(2)}) %collective-permute-start.5) | collective-permute-done | bytes 65568 | tf_op jit(solution)/shard_map/ppermute | solution.py:865
  32.4 0.0 collective-permute-done.4.refs_5_
  32.4 0.0 collective-permute-done.3.refs_4_.refs_3_.refs_6_.refs_9_
  32.4 0.0 collective-permute-done.2.refs_1_.refs_2_
  32.4 0.6 shard_map.209
  33.1 0.1 collective-permute-start.8
  33.2 0.6 shard_map.210.refs_0_
  33.8 3.7 %collective-permute-start.7 = (f32[152,128]{1,0:T(8,128)S(1)}, f32[152,128]{1,0:T(8,128)S(1)}, u32[]{:S(2)}, u32[]{:S(2)}) collective-permute-start(f32[152,128]{1,0:T(8,128)S(1)} %shard_map.210.refs_0_), channel_id=1, source_target_pairs={{0,96},{1,97},{2,98},{3,99},{4,100},{5,101},{6,102},{7,103},{8,104... | collective-permute-start | bytes 233480 | tf_op jit(solution)/shard_map/ppermute | solution.py:865
  37.5 0.0 collective-permute-start.6
  37.5 1.0 %collective-permute-start.10 = (f32[2,16,512]{2,1,0:T(8,128)S(1)}, f32[2,16,512]{2,1,0:T(8,128)S(1)}, u32[]{:S(2)}, u32[]{:S(2)}) collective-permute-start(f32[2,16,512]{2,1,0:T(8,128)S(1)} %get-tuple-element.33.refs_0_), channel_id=1, source_target_pairs={{0,68},{1,69},{2,70},{3,71},{4,64},{5,65},{6,66},{7,67},{8,76},{9,... | collective-permute-start | bytes 196616 | tf_op jit(solution)/shard_map/ppermute | solution.py:865
  38.5 0.4 collective-permute-start.9
  38.9 5.6 %shard_map.211 = (f32[16,256,128]{2,1,0:T(8,128)S(1)}, f32[16,256,128]{2,1,0:T(8,128)S(1)}, f32[5,256,128]{2,1,0:T(8,128)S(1)}) custom-call(s32[9]{0:T(128)S(1)} %stack.33.s_ref, f32[152,128]{1,0:T(8,128)S(1)} %shard_map.210.refs_0_, f32[16,256,128]{2,1,0:T(8,128)S(1)} %shard_map.208.refs_2_.refs_1_, ...), custom_call_target="tpu_custom_call", output_to_operand_aliasing={{0}: (2, {})} | custom-call | flops 1 | bytes 1660500 | tf_op jit(solution)/shard_map/pallas_call | solution.py:115
  44.5 0.0 collective-permute-done.10.refs_6_
  44.5 0.0 collective-permute-done.9.refs_5_
  44.5 0.0 collective-permute-done.7.refs_2_.refs_12_
  44.5 0.0 collective-permute-done.6.refs_1_.refs_11_
  44.5 0.0 collective-permute-done.8.refs_4_
  44.5 0.6 shard_map.212
  45.1 2.6 %collective-permute-start.11 = (f32[128,512]{1,0:T(8,128)S(1)}, f32[128,512]{1,0:T(8,128)S(1)}, u32[]{:S(2)}, u32[]{:S(2)}) collective-permute-start(f32[128,512]{1,0:T(8,128)S(1)} %get-tuple-element.43), channel_id=1, source_target_pairs={{0,64},{1,65},{2,66},{3,67},{4,68},{5,69},{6,70},{7,71},{8,72},{9,... | collective-permute-start | bytes 786440 | tf_op jit(solution)/shard_map/ppermute | solution.py:865
  47.7 1.3 %collective-permute-start.14 = (f32[2,16,512]{2,1,0:T(8,128)S(1)}, f32[2,16,512]{2,1,0:T(8,128)S(1)}, u32[]{:S(2)}, u32[]{:S(2)}) collective-permute-start(f32[2,16,512]{2,1,0:T(8,128)S(1)} %get-tuple-element.38.refs_0_.refs_4_), channel_id=1, source_target_pairs={{0,24},{1,25},{2,26},{3,27},{4,28},{5,29},{6,30},{7,31},{8,0},{9,1... | collective-permute-start | bytes 196616 | tf_op jit(solution)/shard_map/ppermute | solution.py:865
  49.0 1.0 %collective-permute-start.13 = (f32[2,16,512]{2,1,0:T(8,128)S(1)}, f32[2,16,512]{2,1,0:T(8,128)S(1)}, u32[]{:S(2)}, u32[]{:S(2)}) collective-permute-start(f32[2,16,512]{2,1,0:T(8,128)S(1)} %get-tuple-element.38.refs_0_.refs_4_), channel_id=1, source_target_pairs={{0,16},{1,17},{2,18},{3,19},{4,20},{5,21},{6,22},{7,23},{8,24},{9,... | collective-permute-start | bytes 196616 | tf_op jit(solution)/shard_map/ppermute | solution.py:865
  50.0 0.5 collective-permute-start.12
  50.5 0.0 copy-start.16
  50.5 7.3 %shard_map.213 = (f32[16,256,128]{2,1,0:T(8,128)S(1)}, f32[16,256,128]{2,1,0:T(8,128)S(1)}, f32[5,256,128]{2,1,0:T(8,128)S(1)}, f32[16,256,128]{2,1,0:T(8,128)}, f32[2,256,128]{2,1,0:T(8,128)S(1)}) custom-call(s32[9]{0:T(128)S(1)} %stack.33.s_ref, ...), custom_call_target="tpu_custom_call", output_to_operand_aliasing={{0}: (2, {}), {1}: (3, {}), {2}: (4, {})} | custom-call | flops 1 | bytes 2029500 | tf_op jit(solution)/shard_map/pallas_call | solution.py:115
  57.8 0.0 collective-permute-done.14.refs_8_
  57.8 0.0 collective-permute-done.13.refs_7_
  57.8 0.0 collective-permute-done.12.refs_6_
  57.8 0.0 collective-permute-done.11.refs_3_
  57.9 4.5 %shard_map.214 = (f32[512,256]{1,0:T(8,128)S(1)}, f32[4,512,128]{2,1,0:T(8,128)S(1)}, f32[4,128,512]{2,1,0:T(8,128)S(1)}) custom-call(s32[9]{0:T(128)S(1)} %stack.33.s_ref, f32[5,256,128]{2,1,0:T(8,128)S(1)} %get-tuple-element.41.refs_0_.refs_2_, f32[8,128,512]{2,1,0:T(8,128)S(1)} %get-tuple-element.42.refs_1_, ...), custom_call_target="tpu_custom_call" | custom-call | flops 1 | bytes 2546100 | tf_op jit(solution)/shard_map/pallas_call | solution.py:115
  62.4 2.0 %collective-permute-start.16 = (f32[4,512,128]{2,1,0:T(8,128)S(1)}, f32[4,512,128]{2,1,0:T(8,128)S(1)}, u32[]{:S(2)}, u32[]{:S(2)}) collective-permute-start(f32[4,512,128]{2,1,0:T(8,128)S(1)} %get-tuple-element.48), channel_id=1, source_target_pairs={{0,32},{1,33},{2,34},{3,35},{4,36},{5,37},{6,38},{7,39},{8,40},{9,... | collective-permute-start | bytes 3145736 | tf_op jit(solution)/shard_map/ppermute | solution.py:865
  64.4 0.1 collective-permute-start.15
  64.5 2.2 %shard_map.215.refs_4_ = f32[4,512,128]{2,1,0:T(8,128)S(1)} custom-call(s32[9]{0:T(128)S(1)} %stack.33.s_ref, f32[4,128,512]{2,1,0:T(8,128)S(1)} %get-tuple-element.47.refs_0_, bf16[2,512,512]{2,1,0:T(8,128)(2,1)S(1)} %copy-done.2, bf16[2,512,512]{2,1,0:T(8,128)(2,1)S(1)} %copy-done.1, bf16[256,256]{1,0:T(8,128)(2,1)S(1)} %copy-done.11, ...), custom_call_target="tpu_custom_call" | custom-call | flops 1 | bytes 811800 | tf_op jit(solution)/shard_map/pallas_call | solution.py:115
  66.8 0.7 %collective-permute-done.15.refs_1_ = f32[512,256]{1,0:T(8,128)S(1)} collective-permute-done((f32[512,256]{1,0:T(8,128)S(1)}, f32[512,256]{1,0:T(8,128)S(1)}, u32[]{:S(2)}, u32[]{:S(2)}) %collective-permute-start.15) | collective-permute-done | bytes 524320 | tf_op jit(solution)/shard_map/ppermute | solution.py:865
  67.5 0.0 collective-permute-done.16.refs_5_
  67.5 2.3 %shard_map.216 = (f32[4,1024,128]{2,1,0:T(8,128)}, f32[16,256,128]{2,1,0:T(8,128)}) custom-call(s32[9]{0:T(128)S(1)} %stack.33.s_ref, f32[512,256]{1,0:T(8,128)S(1)} %get-tuple-element.45.refs_0_, f32[512,256]{1,0:T(8,128)S(1)} %collective-permute-done.15.refs_1_, ...), custom_call_target="tpu_custom_call", output_to_operand_aliasing={{1}: (7, {})} | custom-call | flops 1 | bytes 922500 | tf_op jit(solution)/shard_map/pallas_call | solution.py:115
  (25 shorter events, 0.0 us)
Async XLA Ops:
  0.8 1.0 %copy-start.14 = (f32[128,512]{1,0:T(8,128)S(1)}, f32[128,512]{1,0:T(8,128)}, u32[]{:S(2)}) copy-start(f32[128,512]{1,0:T(8,128)} %constant.110.clone.refs_1_) | copy-start | bytes 786436
  1.7 0.7 copy-start.18
  2.4 1.6 %copy-start.6 = (f32[4,1024,128]{2,1,0:T(8,128)S(1)}, f32[4,1024,128]{2,1,0:T(8,128)}, u32[]{:S(2)}) copy-start(f32[4,1024,128]{2,1,0:T(8,128)} %source.1) | copy-start | bytes 6291460
  4.0 2.3 %copy-start.3 = (bf16[2,512,512]{2,1,0:T(8,128)(2,1)S(1)}, bf16[2,512,512]{2,1,0:T(8,128)(2,1)}, u32[]{:S(2)}) copy-start(bf16[2,512,512]{2,1,0:T(8,128)(2,1)} %constant.102.clone.refs_4_.refs_5_) | copy-start | bytes 3145732
  4.0 2.3 %copy-start.4 = (bf16[2,512,512]{2,1,0:T(8,128)(2,1)S(1)}, bf16[2,512,512]{2,1,0:T(8,128)(2,1)}, u32[]{:S(2)}) copy-start(bf16[2,512,512]{2,1,0:T(8,128)(2,1)} %constant.101.clone.refs_3_.refs_4_) | copy-start | bytes 3145732
  4.0 2.3 %copy-start.12 = (bf16[256,256]{1,0:T(8,128)(2,1)S(1)}, bf16[256,256]{1,0:T(8,128)(2,1)}, u32[]{:S(2)}) copy-start(bf16[256,256]{1,0:T(8,128)(2,1)} %constant.106.clone.refs_2_.refs_3_) | copy-start | bytes 393220
  4.0 2.3 %copy-start.13 = (bf16[256,256]{1,0:T(8,128)(2,1)S(1)}, bf16[256,256]{1,0:T(8,128)(2,1)}, u32[]{:S(2)}) copy-start(bf16[256,256]{1,0:T(8,128)(2,1)} %constant.105.clone.refs_1_.refs_2_) | copy-start | bytes 393220
  4.8 6.7 %collective-permute-start.1 = (f32[4,512,128]{2,1,0:T(8,128)S(1)}, f32[4,512,128]{2,1,0:T(8,128)S(1)}, u32[]{:S(2)}, u32[]{:S(2)}) collective-permute-start(f32[4,512,128]{2,1,0:T(8,128)S(1)} %get-tuple-element.28), channel_id=1, source_target_pairs={{0,32},{1,33},{2,34},{3,35},{4,36},{5,37},{6,38},{7,39},{8,40},{9,... | collective-permute-start | bytes 3145736 | tf_op jit(solution)/shard_map/ppermute | solution.py:865
  6.3 2.1 %copy-start = (f32[16,256,128]{2,1,0:T(8,128)S(1)}, f32[16,256,128]{2,1,0:T(8,128)}, u32[]{:S(2)}) copy-start(f32[16,256,128]{2,1,0:T(8,128)} %refs_4_.8) | copy-start | bytes 6291460
  6.4 2.1 %copy-start.5 = (f32[256,128]{1,0:T(8,128)S(1)}, f32[256,128]{1,0:T(8,128)}, u32[]{:S(2)}) copy-start(f32[256,128]{1,0:T(8,128)} %refs_6_.1) | copy-start | bytes 393220
  6.4 2.2 %copy-start.7 = (s32[16,256,128]{2,1,0:T(8,128)S(1)}, s32[16,256,128]{2,1,0:T(8,128)}, u32[]{:S(2)}) copy-start(s32[16,256,128]{2,1,0:T(8,128)} %refs_3_.5) | copy-start | bytes 6291460
  6.4 2.2 %copy-start.19 = (f32[2]{0:T(128)S(1)}, f32[2]{0:T(128)}, u32[]{:S(2)}) copy-start(f32[2]{0:T(128)} %refs_0_.2) | copy-start | bytes 28
  8.6 2.9 %copy-start.8 = (f32[128,512]{1,0:T(8,128)S(1)}, f32[128,512]{1,0:T(8,128)}, u32[]{:S(2)}) copy-start(f32[128,512]{1,0:T(8,128)} %constant.111.clone.refs_7_.refs_15_) | copy-start | bytes 786436
  8.6 2.9 %copy-start.15 = (f32[2,16,512]{2,1,0:T(8,128)S(1)}, f32[2,16,512]{2,1,0:T(8,128)}, u32[]{:S(2)}) copy-start(f32[2,16,512]{2,1,0:T(8,128)} %constant.115.clone.refs_9_) | copy-start | bytes 196612
  8.6 2.9 %copy-start.17 = (f32[2,16,16]{2,1,0:T(8,128)S(1)}, f32[2,16,16]{2,1,0:T(8,128)}, u32[]{:S(2)}) copy-start(f32[2,16,16]{2,1,0:T(8,128)} %constant.113.clone.refs_8_) | copy-start | bytes 6148
  15.0 17.4 %collective-permute-start.2 = (f32[128,512]{1,0:T(8,128)S(1)}, f32[128,512]{1,0:T(8,128)S(1)}, u32[]{:S(2)}, u32[]{:S(2)}) collective-permute-start(f32[128,512]{1,0:T(8,128)S(1)} %get-tuple-element.29), channel_id=1, source_target_pairs={{0,64},{1,65},{2,66},{3,67},{4,68},{5,69},{6,70},{7,71},{8,72},{9,... | collective-permute-start | bytes 786440 | tf_op jit(solution)/shard_map/ppermute | solution.py:865
  18.1 14.3 %collective-permute-start.3 = (f32[400,128]{1,0:T(8,128)S(1)}, f32[400,128]{1,0:T(8,128)S(1)}, u32[]{:S(2)}, u32[]{:S(2)}) collective-permute-start(f32[400,128]{1,0:T(8,128)S(1)} %get-tuple-element.32), channel_id=1, source_target_pairs={{0,1},{1,0},{2,3},{3,2},{4,5},{5,4},{6,7},{7,6},{8,9},{9,8},{10,11... | collective-permute-start | bytes 614408 | tf_op jit(solution)/shard_map/ppermute | solution.py:865
  19.7 8.5 %collective-permute-start = (f32[272,128]{1,0:T(8,128)S(1)}, f32[272,128]{1,0:T(8,128)S(1)}, u32[]{:S(2)}, u32[]{:S(2)}) collective-permute-start(f32[272,128]{1,0:T(8,128)S(1)} %get-tuple-element.27.refs_10_.refs_2_.refs_5_.refs_7_), channel_id=1, source_target_pairs={{0,31},{1,2},{2,1},{3,4},{4,3},{5,6},{6,5},{7,8},{8,7},{9,10},{10,... | collective-permute-start | bytes 417800 | tf_op jit(solution)/shard_map/ppermute | solution.py:865
  24.3 8.1 %collective-permute-start.5 = (f32[2,16,512]{2,1,0:T(8,128)S(1)}, f32[2,16,512]{2,1,0:T(8,128)S(1)}, u32[]{:S(2)}, u32[]{:S(2)}) collective-permute-start(f32[2,16,512]{2,1,0:T(8,128)S(1)} %get-tuple-element.30.refs_0_.refs_3_), channel_id=1, source_target_pairs={{0,3},{1,2},{2,1},{3,0},{4,7},{5,6},{6,5},{7,4},{8,11},{9,10},{10,... | collective-permute-start | bytes 196616 | tf_op jit(solution)/shard_map/ppermute | solution.py:865
  24.3 8.1 %collective-permute-start.4 = (f32[2,16,512]{2,1,0:T(8,128)S(1)}, f32[2,16,512]{2,1,0:T(8,128)S(1)}, u32[]{:S(2)}, u32[]{:S(2)}) collective-permute-start(f32[2,16,512]{2,1,0:T(8,128)S(1)} %get-tuple-element.30.refs_0_.refs_3_), channel_id=1, source_target_pairs={{0,2},{1,3},{2,0},{3,1},{4,6},{5,7},{6,4},{7,5},{8,10},{9,11},{10,... | collective-permute-start | bytes 196616 | tf_op jit(solution)/shard_map/ppermute | solution.py:865
  24.5 7.9 %copy-start.9 = (f32[2,16,512]{2,1,0:T(8,128)S(1)}, f32[2,16,512]{2,1,0:T(8,128)}, u32[]{:S(2)}) copy-start(f32[2,16,512]{2,1,0:T(8,128)} %constant.114.clone.refs_7_.refs_9_) | copy-start | bytes 196612
  33.1 11.4 %collective-permute-start.8 = (f32[4,16,512]{2,1,0:T(8,128)S(1)}, f32[4,16,512]{2,1,0:T(8,128)S(1)}, u32[]{:S(2)}, u32[]{:S(2)}) collective-permute-start(f32[4,16,512]{2,1,0:T(8,128)S(1)} %get-tuple-element.36.refs_3_), channel_id=1, source_target_pairs={{0,64},{1,65},{2,66},{3,67},{4,68},{5,69},{6,70},{7,71},{8,72},{9,... | collective-permute-start | bytes 393224 | tf_op jit(solution)/shard_map/ppermute | solution.py:865
  33.8 10.7 %collective-permute-start.7 = (f32[152,128]{1,0:T(8,128)S(1)}, f32[152,128]{1,0:T(8,128)S(1)}, u32[]{:S(2)}, u32[]{:S(2)}) collective-permute-start(f32[152,128]{1,0:T(8,128)S(1)} %shard_map.210.refs_0_), channel_id=1, source_target_pairs={{0,96},{1,97},{2,98},{3,99},{4,100},{5,101},{6,102},{7,103},{8,104... | collective-permute-start | bytes 233480 | tf_op jit(solution)/shard_map/ppermute | solution.py:865
  37.5 7.0 %collective-permute-start.6 = (f32[152,128]{1,0:T(8,128)S(1)}, f32[152,128]{1,0:T(8,128)S(1)}, u32[]{:S(2)}, u32[]{:S(2)}) collective-permute-start(f32[152,128]{1,0:T(8,128)S(1)} %shard_map.210.refs_0_), channel_id=1, source_target_pairs={{0,32},{1,33},{2,34},{3,35},{4,36},{5,37},{6,38},{7,39},{8,40},{9,... | collective-permute-start | bytes 233480 | tf_op jit(solution)/shard_map/ppermute | solution.py:865
  37.5 6.9 %collective-permute-start.10 = (f32[2,16,512]{2,1,0:T(8,128)S(1)}, f32[2,16,512]{2,1,0:T(8,128)S(1)}, u32[]{:S(2)}, u32[]{:S(2)}) collective-permute-start(f32[2,16,512]{2,1,0:T(8,128)S(1)} %get-tuple-element.33.refs_0_), channel_id=1, source_target_pairs={{0,68},{1,69},{2,70},{3,71},{4,64},{5,65},{6,66},{7,67},{8,76},{9,... | collective-permute-start | bytes 196616 | tf_op jit(solution)/shard_map/ppermute | solution.py:865
  38.5 6.0 %collective-permute-start.9 = (f32[2,16,512]{2,1,0:T(8,128)S(1)}, f32[2,16,512]{2,1,0:T(8,128)S(1)}, u32[]{:S(2)}, u32[]{:S(2)}) collective-permute-start(f32[2,16,512]{2,1,0:T(8,128)S(1)} %get-tuple-element.33.refs_0_), channel_id=1, source_target_pairs={{0,4},{1,5},{2,6},{3,7},{4,0},{5,1},{6,2},{7,3},{8,12},{9,13},{10,... | collective-permute-start | bytes 196616 | tf_op jit(solution)/shard_map/ppermute | solution.py:865
  45.1 12.7 %collective-permute-start.11 = (f32[128,512]{1,0:T(8,128)S(1)}, f32[128,512]{1,0:T(8,128)S(1)}, u32[]{:S(2)}, u32[]{:S(2)}) collective-permute-start(f32[128,512]{1,0:T(8,128)S(1)} %get-tuple-element.43), channel_id=1, source_target_pairs={{0,64},{1,65},{2,66},{3,67},{4,68},{5,69},{6,70},{7,71},{8,72},{9,... | collective-permute-start | bytes 786440 | tf_op jit(solution)/shard_map/ppermute | solution.py:865
  47.7 10.1 %collective-permute-start.14 = (f32[2,16,512]{2,1,0:T(8,128)S(1)}, f32[2,16,512]{2,1,0:T(8,128)S(1)}, u32[]{:S(2)}, u32[]{:S(2)}) collective-permute-start(f32[2,16,512]{2,1,0:T(8,128)S(1)} %get-tuple-element.38.refs_0_.refs_4_), channel_id=1, source_target_pairs={{0,24},{1,25},{2,26},{3,27},{4,28},{5,29},{6,30},{7,31},{8,0},{9,1... | collective-permute-start | bytes 196616 | tf_op jit(solution)/shard_map/ppermute | solution.py:865
  49.0 8.8 %collective-permute-start.13 = (f32[2,16,512]{2,1,0:T(8,128)S(1)}, f32[2,16,512]{2,1,0:T(8,128)S(1)}, u32[]{:S(2)}, u32[]{:S(2)}) collective-permute-start(f32[2,16,512]{2,1,0:T(8,128)S(1)} %get-tuple-element.38.refs_0_.refs_4_), channel_id=1, source_target_pairs={{0,16},{1,17},{2,18},{3,19},{4,20},{5,21},{6,22},{7,23},{8,24},{9,... | collective-permute-start | bytes 196616 | tf_op jit(solution)/shard_map/ppermute | solution.py:865
  50.0 7.8 %collective-permute-start.12 = (f32[2,16,512]{2,1,0:T(8,128)S(1)}, f32[2,16,512]{2,1,0:T(8,128)S(1)}, u32[]{:S(2)}, u32[]{:S(2)}) collective-permute-start(f32[2,16,512]{2,1,0:T(8,128)S(1)} %get-tuple-element.38.refs_0_.refs_4_), channel_id=1, source_target_pairs={{0,8},{1,9},{2,10},{3,11},{4,12},{5,13},{6,14},{7,15},{8,16},{9,17... | collective-permute-start | bytes 196616 | tf_op jit(solution)/shard_map/ppermute | solution.py:865
  50.4 7.4 %copy-start.1 = (bf16[2,512,512]{2,1,0:T(8,128)(2,1)S(1)}, bf16[2,512,512]{2,1,0:T(8,128)(2,1)}, u32[]{:S(2)}) copy-start(bf16[2,512,512]{2,1,0:T(8,128)(2,1)} %constant.104.clone.refs_12_.refs_2_) | copy-start | bytes 3145732
  50.4 7.4 %copy-start.2 = (bf16[2,512,512]{2,1,0:T(8,128)(2,1)S(1)}, bf16[2,512,512]{2,1,0:T(8,128)(2,1)}, u32[]{:S(2)}) copy-start(bf16[2,512,512]{2,1,0:T(8,128)(2,1)} %constant.103.clone.refs_11_.refs_1_) | copy-start | bytes 3145732
  50.4 7.4 %copy-start.10 = (bf16[256,256]{1,0:T(8,128)(2,1)S(1)}, bf16[256,256]{1,0:T(8,128)(2,1)}, u32[]{:S(2)}) copy-start(bf16[256,256]{1,0:T(8,128)(2,1)} %constant.108.clone.refs_14_.refs_4_) | copy-start | bytes 393220
  50.5 7.4 %copy-start.11 = (bf16[256,256]{1,0:T(8,128)(2,1)S(1)}, bf16[256,256]{1,0:T(8,128)(2,1)}, u32[]{:S(2)}) copy-start(bf16[256,256]{1,0:T(8,128)(2,1)} %constant.107.clone.refs_13_.refs_3_) | copy-start | bytes 393220
  50.5 7.4 %copy-start.16 = (f32[2,16,16]{2,1,0:T(8,128)S(1)}, f32[2,16,16]{2,1,0:T(8,128)}, u32[]{:S(2)}) copy-start(f32[2,16,16]{2,1,0:T(8,128)} %constant.112.clone.refs_16_) | copy-start | bytes 6148
  62.4 5.0 %collective-permute-start.16 = (f32[4,512,128]{2,1,0:T(8,128)S(1)}, f32[4,512,128]{2,1,0:T(8,128)S(1)}, u32[]{:S(2)}, u32[]{:S(2)}) collective-permute-start(f32[4,512,128]{2,1,0:T(8,128)S(1)} %get-tuple-element.48), channel_id=1, source_target_pairs={{0,32},{1,33},{2,34},{3,35},{4,36},{5,37},{6,38},{7,39},{8,40},{9,... | collective-permute-start | bytes 3145736 | tf_op jit(solution)/shard_map/ppermute | solution.py:865
  64.4 3.0 %collective-permute-start.15 = (f32[512,256]{1,0:T(8,128)S(1)}, f32[512,256]{1,0:T(8,128)S(1)}, u32[]{:S(2)}, u32[]{:S(2)}) collective-permute-start(f32[512,256]{1,0:T(8,128)S(1)} %get-tuple-element.45.refs_0_), channel_id=1, source_target_pairs={{0,32},{1,33},{2,34},{3,35},{4,36},{5,37},{6,38},{7,39},{8,40},{9,... | collective-permute-start | bytes 1572872 | tf_op jit(solution)/shard_map/ppermute | solution.py:865

commit v4 on v3

--- a/solution.py
+++ b/solution.py
@@ -16,8 +16,10 @@
 Z_RING, Y_PAIR, X_RING = 4, 2, 4
 VMEM_LIMIT = 18 * 1024 * 1024
 BLOCK_LIMIT = 16 * 1024 * 1024
-LANES = 512
+LANES = 128
 CHUNK = 32
+RIM = 32
+MIDDLE = 64
 COST_SCALE = 0.1
 
 
@@ -160,6 +162,10 @@
     ).reshape(out.shape)
 
 
+def across(value, length):
+    return jnp.concatenate([value] * (length // value.shape[1]), axis=1)
+
+
 def continuants(centre, first, count):
     values = [jnp.ones_like(centre), centre + first]
     for _ in range(1, count):
@@ -174,7 +180,7 @@
 
     def tile(group, nothing):
         rows = pl.ds(pl.multiple_of(group * 8, 8), 8)
-        centre = lam[s_ref[0]] + sigma[rows] - 2.0
+        centre = lam[s_ref[0]] + across(sigma[rows], out.shape[2]) - 2.0
         mine = continuants(centre, 1.0 - low, own)
         other = continuants(centre, low, own)
         for i in range(own):
@@ -214,7 +220,7 @@
             carries.append(carry)
         carried[rows] = carry
         shared = carry * pivots[3 * own, rows]
-        scale = edge[rows]
+        scale = across(edge[rows], half)
         value = shared * pivots[2 * own - 1, rows]
         sums[parity, own - 1] += scale * value
         for i in range(own - 2, -1, -1):
@@ -374,7 +380,7 @@
     def tile(group, nothing):
         rows = pl.ds(pl.multiple_of(group * 8, 8), 8)
         parity = group // side
-        scale = edge[rows]
+        scale = across(edge[rows], half)
         rhs = lambda i: scale * both[parity, i : i + 1]
         mine = lambda i: pivots[i - 1, rows]
         other = lambda i: pivots[own + i - 1, rows]
@@ -573,7 +579,7 @@
     return jnp.where((lane == 0) | (lane == width - 1), moved, 0.0)
 
 
-def step_planes(temp, cond, up, down, cond_up, cond_down, inflow, emit, starts):
+def step_planes(temp, cond, up, down, cond_up, cond_down, inflow, emit, starts, kept=None):
     depth, rows, width = temp.shape
     lane = lax.broadcasted_iota(jnp.int32, (CHUNK, width), 1)
     end = width - 1
@@ -605,7 +611,7 @@
                 pairs.append(pair)
                 term = pair * (side_temp - here)
                 total = term if total is None else total + term
-            pair = own + pltpu.roll(own, end, 1)
+            pair = own + pltpu.roll(own, end, 1) if kept is None else kept[z, at]
             pairs.append(pair)
             flow = jnp.where(lane == end, 0.0, pair * (pltpu.roll(here, end, 1) - here))
             total = total + (flow - pltpu.roll(flow, 1, 1))
@@ -635,21 +641,22 @@
     return left_pair, right_pair
 
 
-def base_emit(temp, gas, out):
+def base_emit(temp, gas, out, kept):
     def emit(z, start, first, value, pairs):
         at = slice(start, start + CHUNK)
         if first:
             value = value + (STEP_RATE * HEAT_TRANSFER) * (gas[at] - temp[0, at])
         out[z, at] = value
+        kept[z, at] = pairs[4]
 
     return emit
 
 
-def inner_body(s_ref, temp, cond, gas, out):
+def inner_body(s_ref, temp, cond, gas, out, kept):
     rows = temp.shape[1]
     step_planes(
-        temp, cond, None, None, None, None, None, base_emit(temp, gas, out),
-        range(CHUNK, rows - CHUNK, CHUNK),
+        temp, cond, None, None, None, None, None, base_emit(temp, gas, out, kept),
+        range(RIM, rows - RIM, CHUNK),
     )
 
 
@@ -731,7 +738,7 @@
 
 
 def middle_body(
-    s_ref, base_in, temp, cond, gas, packs, mixed, far, base, held, weights,
+    s_ref, base_in, temp, cond, kept, gas, packs, mixed, far, base, held, weights,
     packed, flow, inflow, face,
 ):
     depth, rows, width = temp.shape
@@ -742,7 +749,7 @@
     inflow[...] = to_columns(packed, flow)
 
     def mend(z, nothing):
-        for start in range(CHUNK, rows - CHUNK, CHUNK):
+        for start in range(RIM, rows - RIM, CHUNK):
             at = slice(start, start + CHUNK)
             base[z, at] = base_in[z, at] + (0.5 * STEP_RATE) * entering(inflow, z, at, lane)
         return nothing
@@ -757,13 +764,13 @@
     step_planes(
         base, cond, None, None, None, None, inflow,
         final_emit(temp, gas, face, held, weights, lambda z, start, first: None),
-        range(2 * CHUNK, rows - 2 * CHUNK, CHUNK),
+        range(MIDDLE, rows - MIDDLE, CHUNK), kept,
     )
 
 
 def outer_body(
-    s_ref, base_in, held_in, weights_in, temp, cond, gas, packs, along, mixed, far, near_y, far_y,
-    base, held, weights, out, top, sems, packed, flow, inflow, face, lines, base_lines,
+    s_ref, base_in, held_in, weights_in, kept_in, temp, cond, gas, packs, along, mixed, far, near_y, far_y,
+    base, held, weights, kept, out, top, sems, packed, flow, inflow, face, lines, base_lines,
 ):
     depth, rows, width = temp.shape
     settle(s_ref, lines, near_y, far_y)
@@ -781,7 +788,8 @@
     cond_up, cond_down = span(0, 1, 1), span(1, 1, 2)
     step_planes(
         temp, cond, span(0, 0, 1), span(1, 0, 2), cond_up, cond_down, inflow,
-        base_emit(temp, gas, base), (0, rows - CHUNK),
+        base_emit(temp, gas, base, kept),
+        (*range(0, RIM, CHUNK), *range(rows - RIM, rows, CHUNK)),
     )
     interleave(flow, left_pair * left_step, right_pair * right_step)
     inflow[...] = to_columns(packed, flow)
@@ -798,7 +806,7 @@
     step_planes(
         base, cond, base_lines.at[0], base_lines.at[1], cond_up, cond_down, inflow,
         final_emit(temp, gas, face, held, weights, done),
-        (0, CHUNK, rows - 2 * CHUNK, rows - CHUNK),
+        (*range(0, MIDDLE, CHUNK), *range(rows - MIDDLE, rows, CHUNK)), kept,
     )
     top[...] = held[:2]
     for z in range(2, depth):
@@ -931,9 +939,9 @@
     carried_there = move(carried, other_half)
     log_rho = const["log_rho"]
     pair_shape = edges.shape
-    (base,) = run(
+    base, sides = run(
         inner_body, 4.5, scalars, [edges], [solid_temp, cond, gas_wall_temp],
-        [(depth, tile_rows, width)],
+        [(depth, tile_rows, width), (depth, tile_rows, width)],
     )
     four, two = run(
         functools.partial(z_body, width=width), 0.6, scalars, [far_x, carried_there, base],
@@ -950,7 +958,7 @@
     tile = (depth, tile_rows, width)
     base, begun, weights = run(
         middle_body, 4.5, scalars, [lines],
-        [base, solid_temp, cond, gas_wall_temp, packs, mixed, far_x],
+        [base, solid_temp, cond, sides, gas_wall_temp, packs, mixed, far_x],
         [tile, tile, (5, tile_rows, width)],
         scratch=[row_scratch, flow_scratch, column_scratch, column_scratch],
         aliases={2: 0},
@@ -962,17 +970,18 @@
     block = Z_RING * Y_PAIR
     opening_there = move(opening, other_half)
     x_got = [move(run8, lambda g, p, d=d: (g, (p + block * d) % pencils)) for d in range(1, X_RING)]
-    _, _, weights, final, top = run(
+    _, _, weights, _, final, top = run(
         outer_body, 5.5, scalars, [run8],
-        [base, begun, weights, solid_temp, cond, gas_wall_temp, packs, along, mixed, far_x, *near_y],
-        [tile, tile, (5, tile_rows, width), solid_temp.shape, (2, tile_rows, width)],
+        [base, begun, weights, sides, solid_temp, cond, gas_wall_temp, packs, along, mixed, far_x,
+         *near_y],
+        [tile, tile, (5, tile_rows, width), tile, solid_temp.shape, (2, tile_rows, width)],
         scratch=[
             pltpu.SemaphoreType.DMA((depth,)),
             row_scratch, flow_scratch, column_scratch, column_scratch,
             pltpu.VMEM((2, 9 * depth + 8, width), jnp.float32),
             pltpu.VMEM((2, depth, width), jnp.float32),
         ],
-        out_specs=[FAST, FAST, FAST, ORDER, FAST], aliases={2: 0, 3: 1, 4: 2},
+        out_specs=[FAST, FAST, FAST, FAST, ORDER, FAST], aliases={2: 0, 3: 1, 4: 2, 5: 3},
     )
     wall, away, keep = run(
         solve_body, 6.9, scalars, [weights],

time: 70 us -> 69.2 us (0.989)
  transfers between devices with their start and end apart: 17 -> 17, of which waited for: 2 -> 2; matrix products, arithmetic and copies ran while one was open for 0% -> 0% of each run, Pallas kernels for 35% -> 34%
where the time goes in v4:
time: 69.2 us; the launch traced here: 69 us
  Pallas kernels  37.2 us (54%)
  starting transfers between devices  23.5 us (34%)
  waiting for transfers between devices  5.03 us (7%)
  local copies, waits for them, and re-layouts  2.25 us (3%)
  between operations  1.04 us (2%)
    pallas_call x13, Pallas kernels, run(): pl.pallas_call(inner, out_shape=outs, in_specs=specs, out_specs=out_specs...  36.4 us
    ppermute x17, starting transfers between devices, move(): return lax.ppermute(value, ('grp', 'pen'), pairs)  23.5 us
    ppermute x17, waiting for transfers between devices, move(): return lax.ppermute(value, ('grp', 'pen'), pairs)  5.03 us
    unnamed x40, local copies, waits for them, and re-layouts  2.17 us
  transfers between devices with their start and end apart: 17, of which 2 were waited for; matrix products, arithmetic and copies ran while one was open for 0% of the time, Pallas kernels for 34%

profile of v4, /device:TPU:1, one launch (start us, length us, event | category | flops | bytes accessed | tf_op | source)
XLA Modules:
  0.0 69.0 jit_solution(591671128043631154)
XLA Ops:
  0.7 0.1 stack.33.s_ref
  0.8 0.8 %copy-done.15 = f32[128,128]{1,0:T(8,128)S(1)} copy-done((f32[128,128]{1,0:T(8,128)S(1)}, f32[128,128]{1,0:T(8,128)}, u32[]{:S(2)}) %copy-start.15) | copy-done | bytes 65560
  1.6 0.7 copy-done.18
  2.3 1.2 %shard_map.203.after.refs_6_.refs_10_ = f32[26,128,512]{2,1,0:T(8,128)S(1)} custom-call(s32[9]{0:T(128)S(1)} %stack.33.s_ref, f32[2,1,512]{2,1,0:T(1,128)S(1)} %copy-done.18, f32[128,128]{1,0:T(8,128)S(1)} %copy-done.15), custom_call_target="tpu_custom_call" | custom-call | flops 1 | bytes 442800 | tf_op jit(solution)/shard_map/pallas_call | solution.py:117
  3.5 0.4 copy-done.6
  3.9 0.8 %shard_map.204 = (f32[4,512,128]{2,1,0:T(8,128)S(1)}, f32[4,512,128]{2,1,0:T(8,128)S(1)}) custom-call(s32[9]{0:T(128)S(1)} %stack.33.s_ref, f32[26,128,512]{2,1,0:T(8,128)S(1)} %shard_map.203.after.refs_6_.refs_10_, f32[4,1024,128]{2,1,0:T(8,128)S(1)} %copy-done.6), custom_call_target="tpu_custom_call" | custom-call | flops 1 | bytes 295200 | tf_op jit(solution)/shard_map/pallas_call | solution.py:130
  4.7 1.5 %collective-permute-start.1 = (f32[4,512,128]{2,1,0:T(8,128)S(1)}, f32[4,512,128]{2,1,0:T(8,128)S(1)}, u32[]{:S(2)}, u32[]{:S(2)}) collective-permute-start(f32[4,512,128]{2,1,0:T(8,128)S(1)} %get-tuple-element.30), channel_id=1, source_target_pairs={{0,32},{1,33},{2,34},{3,35},{4,36},{5,37},{6,38},{7,39},{8,40},{9,... | collective-permute-start | bytes 3145736 | tf_op jit(solution)/shard_map/ppermute | solution.py:873
  6.2 0.0 copy-done.3
  6.2 0.0 copy-done.4
  6.2 0.0 copy-done.11
  6.2 0.0 copy-done.12
  6.2 0.0 copy-start
  6.2 0.0 copy-start.5
  6.3 0.0 copy-start.7
  6.3 0.0 copy-start.19
  6.3 2.1 %shard_map.205.refs_1_ = f32[4,128,512]{2,1,0:T(8,128)S(1)} custom-call(s32[9]{0:T(128)S(1)} %stack.33.s_ref, f32[4,512,128]{2,1,0:T(8,128)S(1)} %get-tuple-element.28.refs_0_, bf16[256,256]{1,0:T(8,128)(2,1)S(1)} %copy-done.12, bf16[256,256]{1,0:T(8,128)(2,1)S(1)} %copy-done.11, bf16[2,512,512]{2,1,0:T(8,128)(2,1)S(1)} %copy-done.4, ...), custom_call_target="tpu_custom_call" | custom-call | flops 1 | bytes 774900 | tf_op jit(solution)/shard_map/pallas_call | solution.py:117
  8.3 0.0 copy-done
  8.4 0.1 copy-done.7
  8.5 0.0 copy-done.19
  8.5 2.8 %shard_map.206 = (f32[16,256,128]{2,1,0:T(8,128)S(1)}, f32[272,128]{1,0:T(8,128)S(1)}, f32[136,128]{1,0:T(8,128)S(1)}) custom-call(s32[9]{0:T(128)S(1)} %stack.33.s_ref, f32[2]{0:T(128)S(1)} %copy-done.19, f32[4,128,512]{2,1,0:T(8,128)S(1)} %shard_map.205.refs_1_, f32[16,256,128]{2,1,0:T(8,128)S(1)} %copy-done, s32[16,256,128]{2,1,0:T(8,128)S(1)} %copy-done.7, ...), custom_call_target="tpu_custom_call" | custom-call | flops 1 | bytes 1033200 | tf_op jit(solution)/shard_map/pallas_call | solution.py:117
  11.4 0.0 collective-permute-done.1.refs_0_
  11.4 3.5 %shard_map.207 = (f32[8,128,512]{2,1,0:T(8,128)S(1)}, f32[2,16,512]{2,1,0:T(8,128)S(1)}, f32[128,512]{1,0:T(8,128)S(1)}, f32[128,512]{1,0:T(8,128)S(1)}, f32[400,128]{1,0:T(8,128)S(1)}) custom-call(s32[9]{0:T(128)S(1)} %stack.33.s_ref, f32[4,512,128]{2,1,0:T(8,128)S(1)} %collective-permute-done.1.refs_0_, f32[4,128,512]{2,1,0:T(8,128)S(1)} %shard_map.205.refs_1_, ...), custom_call_target="tpu_custom_call" | custom-call | flops 1 | bytes 1254600 | tf_op jit(solution)/shard_map/pallas_call | solution.py:117
  14.9 3.1 %collective-permute-start.2 = (f32[128,512]{1,0:T(8,128)S(1)}, f32[128,512]{1,0:T(8,128)S(1)}, u32[]{:S(2)}, u32[]{:S(2)}) collective-permute-start(f32[128,512]{1,0:T(8,128)S(1)} %get-tuple-element.31), channel_id=1, source_target_pairs={{0,64},{1,65},{2,66},{3,67},{4,68},{5,69},{6,70},{7,71},{8,72},{9,... | collective-permute-start | bytes 786440 | tf_op jit(solution)/shard_map/ppermute | solution.py:873
  17.9 1.7 %collective-permute-start.3 = (f32[400,128]{1,0:T(8,128)S(1)}, f32[400,128]{1,0:T(8,128)S(1)}, u32[]{:S(2)}, u32[]{:S(2)}) collective-permute-start(f32[400,128]{1,0:T(8,128)S(1)} %get-tuple-element.35), channel_id=1, source_target_pairs={{0,1},{1,0},{2,3},{3,2},{4,5},{5,4},{6,7},{7,6},{8,9},{9,8},{10,11... | collective-permute-start | bytes 614408 | tf_op jit(solution)/shard_map/ppermute | solution.py:873
  19.6 4.5 %collective-permute-start = (f32[272,128]{1,0:T(8,128)S(1)}, f32[272,128]{1,0:T(8,128)S(1)}, u32[]{:S(2)}, u32[]{:S(2)}) collective-permute-start(f32[272,128]{1,0:T(8,128)S(1)} %get-tuple-element.29.refs_10_.refs_2_.refs_6_.refs_8_), channel_id=1, source_target_pairs={{0,31},{1,2},{2,1},{3,4},{4,3},{5,6},{6,5},{7,8},{8,7},{9,10},{10,... | collective-permute-start | bytes 417800 | tf_op jit(solution)/shard_map/ppermute | solution.py:873
  24.1 0.0 collective-permute-start.5
  24.1 0.2 collective-permute-start.4
  24.3 3.7 %shard_map.208 = (f32[16,256,128]{2,1,0:T(8,128)S(1)}, f32[16,256,128]{2,1,0:T(8,128)S(1)}) custom-call(s32[9]{0:T(128)S(1)} %stack.33.s_ref, f32[2,16,512]{2,1,0:T(8,128)S(1)} %get-tuple-element.32.refs_0_.refs_3_, f32[16,256,128]{2,1,0:T(8,128)S(1)} %copy-done, f32[16,256,128]{2,1,0:T(8,128)S(1)} %get-tuple-element.33.refs_2_.refs_3_.refs_6_, ...), custom_call_target="tpu_custom_call" | custom-call | flops 1 | bytes 1660500 | tf_op jit(solution)/shard_map/pallas_call | solution.py:117
  28.0 0.0 collective-permute-done.refs_0_.refs_4_.refs_8_.refs_11_
  28.0 4.3 %collective-permute-done.5.refs_6_ = f32[2,16,512]{2,1,0:T(8,128)S(1)} collective-permute-done((f32[2,16,512]{2,1,0:T(8,128)S(1)}, f32[2,16,512]{2,1,0:T(8,128)S(1)}, u32[]{:S(2)}, u32[]{:S(2)}) %collective-permute-start.5) | collective-permute-done | bytes 65568 | tf_op jit(solution)/shard_map/ppermute | solution.py:873
  32.3 0.0 collective-permute-done.4.refs_5_
  32.3 0.0 collective-permute-done.3.refs_4_.refs_3_.refs_7_.refs_10_
  32.3 0.0 collective-permute-done.2.refs_1_.refs_2_
  32.3 0.6 shard_map.209
  33.0 0.1 collective-permute-start.8
  33.1 0.6 shard_map.210.refs_0_
  33.7 3.7 %collective-permute-start.7 = (f32[152,128]{1,0:T(8,128)S(1)}, f32[152,128]{1,0:T(8,128)S(1)}, u32[]{:S(2)}, u32[]{:S(2)}) collective-permute-start(f32[152,128]{1,0:T(8,128)S(1)} %shard_map.210.refs_0_), channel_id=1, source_target_pairs={{0,96},{1,97},{2,98},{3,99},{4,100},{5,101},{6,102},{7,103},{8,104... | collective-permute-start | bytes 233480 | tf_op jit(solution)/shard_map/ppermute | solution.py:873
  37.4 0.0 collective-permute-start.6
  37.4 0.9 %collective-permute-start.10 = (f32[2,16,512]{2,1,0:T(8,128)S(1)}, f32[2,16,512]{2,1,0:T(8,128)S(1)}, u32[]{:S(2)}, u32[]{:S(2)}) collective-permute-start(f32[2,16,512]{2,1,0:T(8,128)S(1)} %get-tuple-element.36.refs_0_), channel_id=1, source_target_pairs={{0,68},{1,69},{2,70},{3,71},{4,64},{5,65},{6,66},{7,67},{8,76},{9,... | collective-permute-start | bytes 196616 | tf_op jit(solution)/shard_map/ppermute | solution.py:873
  38.3 0.4 collective-permute-start.9
  38.7 5.3 %shard_map.211 = (f32[16,256,128]{2,1,0:T(8,128)S(1)}, f32[16,256,128]{2,1,0:T(8,128)S(1)}, f32[5,256,128]{2,1,0:T(8,128)S(1)}) custom-call(s32[9]{0:T(128)S(1)} %stack.33.s_ref, f32[152,128]{1,0:T(8,128)S(1)} %shard_map.210.refs_0_, f32[16,256,128]{2,1,0:T(8,128)S(1)} %get-tuple-element.34.refs_2_.refs_1_, ...), custom_call_target="tpu_custom_call", output_to_operand_aliasing={{0}: (2, {})} | custom-call | flops 1 | bytes 1660500 | tf_op jit(solution)/shard_map/pallas_call | solution.py:117
  44.0 0.0 collective-permute-done.10.refs_6_
  44.0 0.0 collective-permute-done.9.refs_5_
  44.0 0.0 collective-permute-done.7.refs_2_.refs_13_
  44.0 0.0 collective-permute-done.6.refs_1_.refs_12_
  44.0 0.0 collective-permute-done.8.refs_4_
  44.0 0.6 shard_map.212
  44.6 2.6 %collective-permute-start.11 = (f32[128,512]{1,0:T(8,128)S(1)}, f32[128,512]{1,0:T(8,128)S(1)}, u32[]{:S(2)}, u32[]{:S(2)}) collective-permute-start(f32[128,512]{1,0:T(8,128)S(1)} %get-tuple-element.47), channel_id=1, source_target_pairs={{0,64},{1,65},{2,66},{3,67},{4,68},{5,69},{6,70},{7,71},{8,72},{9,... | collective-permute-start | bytes 786440 | tf_op jit(solution)/shard_map/ppermute | solution.py:873
  47.3 1.2 %collective-permute-start.14 = (f32[2,16,512]{2,1,0:T(8,128)S(1)}, f32[2,16,512]{2,1,0:T(8,128)S(1)}, u32[]{:S(2)}, u32[]{:S(2)}) collective-permute-start(f32[2,16,512]{2,1,0:T(8,128)S(1)} %get-tuple-element.42.refs_0_.refs_4_), channel_id=1, source_target_pairs={{0,24},{1,25},{2,26},{3,27},{4,28},{5,29},{6,30},{7,31},{8,0},{9,1... | collective-permute-start | bytes 196616 | tf_op jit(solution)/shard_map/ppermute | solution.py:873
  48.5 1.0 %collective-permute-start.13 = (f32[2,16,512]{2,1,0:T(8,128)S(1)}, f32[2,16,512]{2,1,0:T(8,128)S(1)}, u32[]{:S(2)}, u32[]{:S(2)}) collective-permute-start(f32[2,16,512]{2,1,0:T(8,128)S(1)} %get-tuple-element.42.refs_0_.refs_4_), channel_id=1, source_target_pairs={{0,16},{1,17},{2,18},{3,19},{4,20},{5,21},{6,22},{7,23},{8,24},{9,... | collective-permute-start | bytes 196616 | tf_op jit(solution)/shard_map/ppermute | solution.py:873
  49.5 0.4 collective-permute-start.12
  50.0 0.0 copy-start.16
  50.0 7.0 %shard_map.213 = (f32[16,256,128]{2,1,0:T(8,128)S(1)}, f32[16,256,128]{2,1,0:T(8,128)S(1)}, f32[5,256,128]{2,1,0:T(8,128)S(1)}, f32[16,256,128]{2,1,0:T(8,128)S(...) custom-call(s32[9]{0:T(128)S(1)} %stack.33.s_ref, ...), custom_call_target="tpu_custom_call", output_to_operand_aliasing={{0}: (2, {}), {1}: (3, {}), {2}: (4, {}), {3}: (5, {})} | custom-call | flops 1 | bytes 2029500 | tf_op jit(solution)/shard_map/pallas_call | solution.py:117
  57.0 0.0 collective-permute-done.14.refs_8_
  57.0 0.0 collective-permute-done.13.refs_7_
  57.0 0.0 collective-permute-done.12.refs_6_
  57.0 0.0 collective-permute-done.11.refs_3_
  57.1 4.6 %shard_map.214 = (f32[512,256]{1,0:T(8,128)S(1)}, f32[4,512,128]{2,1,0:T(8,128)S(1)}, f32[4,128,512]{2,1,0:T(8,128)S(1)}) custom-call(s32[9]{0:T(128)S(1)} %stack.33.s_ref, f32[5,256,128]{2,1,0:T(8,128)S(1)} %get-tuple-element.45.refs_0_.refs_2_, f32[8,128,512]{2,1,0:T(8,128)S(1)} %get-tuple-element.46.refs_1_, ...), custom_call_target="tpu_custom_call" | custom-call | flops 1 | bytes 2546100 | tf_op jit(solution)/shard_map/pallas_call | solution.py:117
  61.7 2.0 %collective-permute-start.16 = (f32[4,512,128]{2,1,0:T(8,128)S(1)}, f32[4,512,128]{2,1,0:T(8,128)S(1)}, u32[]{:S(2)}, u32[]{:S(2)}) collective-permute-start(f32[4,512,128]{2,1,0:T(8,128)S(1)} %get-tuple-element.52), channel_id=1, source_target_pairs={{0,32},{1,33},{2,34},{3,35},{4,36},{5,37},{6,38},{7,39},{8,40},{9,... | collective-permute-start | bytes 3145736 | tf_op jit(solution)/shard_map/ppermute | solution.py:873
  63.7 0.1 collective-permute-start.15
  63.7 2.2 %shard_map.215.refs_4_ = f32[4,512,128]{2,1,0:T(8,128)S(1)} custom-call(s32[9]{0:T(128)S(1)} %stack.33.s_ref, f32[4,128,512]{2,1,0:T(8,128)S(1)} %get-tuple-element.51.refs_0_, bf16[2,512,512]{2,1,0:T(8,128)(2,1)S(1)} %copy-done.2, bf16[2,512,512]{2,1,0:T(8,128)(2,1)S(1)} %copy-done.1, bf16[256,256]{1,0:T(8,128)(2,1)S(1)} %copy-done.10, ...), custom_call_target="tpu_custom_call" | custom-call | flops 1 | bytes 811800 | tf_op jit(solution)/shard_map/pallas_call | solution.py:117
  66.0 0.7 %collective-permute-done.15.refs_1_ = f32[512,256]{1,0:T(8,128)S(1)} collective-permute-done((f32[512,256]{1,0:T(8,128)S(1)}, f32[512,256]{1,0:T(8,128)S(1)}, u32[]{:S(2)}, u32[]{:S(2)}) %collective-permute-start.15) | collective-permute-done | bytes 524320 | tf_op jit(solution)/shard_map/ppermute | solution.py:873
  66.7 0.0 collective-permute-done.16.refs_5_
  66.7 2.3 %shard_map.216 = (f32[4,1024,128]{2,1,0:T(8,128)}, f32[16,256,128]{2,1,0:T(8,128)}) custom-call(s32[9]{0:T(128)S(1)} %stack.33.s_ref, f32[512,256]{1,0:T(8,128)S(1)} %get-tuple-element.49.refs_0_, f32[512,256]{1,0:T(8,128)S(1)} %collective-permute-done.15.refs_1_, ...), custom_call_target="tpu_custom_call", output_to_operand_aliasing={{1}: (7, {})} | custom-call | flops 1 | bytes 922500 | tf_op jit(solution)/shard_map/pallas_call | solution.py:117
  (25 shorter events, 0.0 us)
Async XLA Ops:
  0.8 0.8 %copy-start.15 = (f32[128,128]{1,0:T(8,128)S(1)}, f32[128,128]{1,0:T(8,128)}, u32[]{:S(2)}) copy-start(f32[128,128]{1,0:T(8,128)} %constant.110.clone.refs_1_) | copy-start | bytes 196612
  1.6 0.7 copy-start.18
  2.3 1.6 %copy-start.6 = (f32[4,1024,128]{2,1,0:T(8,128)S(1)}, f32[4,1024,128]{2,1,0:T(8,128)}, u32[]{:S(2)}) copy-start(f32[4,1024,128]{2,1,0:T(8,128)} %source.1) | copy-start | bytes 6291460
  3.9 2.3 %copy-start.3 = (bf16[2,512,512]{2,1,0:T(8,128)(2,1)S(1)}, bf16[2,512,512]{2,1,0:T(8,128)(2,1)}, u32[]{:S(2)}) copy-start(bf16[2,512,512]{2,1,0:T(8,128)(2,1)} %constant.102.clone.refs_4_.refs_5_) | copy-start | bytes 3145732
  3.9 2.3 %copy-start.4 = (bf16[2,512,512]{2,1,0:T(8,128)(2,1)S(1)}, bf16[2,512,512]{2,1,0:T(8,128)(2,1)}, u32[]{:S(2)}) copy-start(bf16[2,512,512]{2,1,0:T(8,128)(2,1)} %constant.101.clone.refs_3_.refs_4_) | copy-start | bytes 3145732
  3.9 2.3 %copy-start.11 = (bf16[256,256]{1,0:T(8,128)(2,1)S(1)}, bf16[256,256]{1,0:T(8,128)(2,1)}, u32[]{:S(2)}) copy-start(bf16[256,256]{1,0:T(8,128)(2,1)} %constant.106.clone.refs_2_.refs_3_) | copy-start | bytes 393220
  3.9 2.3 %copy-start.12 = (bf16[256,256]{1,0:T(8,128)(2,1)S(1)}, bf16[256,256]{1,0:T(8,128)(2,1)}, u32[]{:S(2)}) copy-start(bf16[256,256]{1,0:T(8,128)(2,1)} %constant.105.clone.refs_1_.refs_2_) | copy-start | bytes 393220
  4.7 6.6 %collective-permute-start.1 = (f32[4,512,128]{2,1,0:T(8,128)S(1)}, f32[4,512,128]{2,1,0:T(8,128)S(1)}, u32[]{:S(2)}, u32[]{:S(2)}) collective-permute-start(f32[4,512,128]{2,1,0:T(8,128)S(1)} %get-tuple-element.30), channel_id=1, source_target_pairs={{0,32},{1,33},{2,34},{3,35},{4,36},{5,37},{6,38},{7,39},{8,40},{9,... | collective-permute-start | bytes 3145736 | tf_op jit(solution)/shard_map/ppermute | solution.py:873
  6.2 2.1 %copy-start = (f32[16,256,128]{2,1,0:T(8,128)S(1)}, f32[16,256,128]{2,1,0:T(8,128)}, u32[]{:S(2)}) copy-start(f32[16,256,128]{2,1,0:T(8,128)} %refs_5_.4) | copy-start | bytes 6291460
  6.2 2.1 %copy-start.5 = (f32[256,128]{1,0:T(8,128)S(1)}, f32[256,128]{1,0:T(8,128)}, u32[]{:S(2)}) copy-start(f32[256,128]{1,0:T(8,128)} %refs_7_.4) | copy-start | bytes 393220
  6.3 2.2 %copy-start.7 = (s32[16,256,128]{2,1,0:T(8,128)S(1)}, s32[16,256,128]{2,1,0:T(8,128)}, u32[]{:S(2)}) copy-start(s32[16,256,128]{2,1,0:T(8,128)} %refs_3_.5) | copy-start | bytes 6291460
  6.3 2.2 %copy-start.19 = (f32[2]{0:T(128)S(1)}, f32[2]{0:T(128)}, u32[]{:S(2)}) copy-start(f32[2]{0:T(128)} %refs_0_.2) | copy-start | bytes 28
  8.5 2.9 %copy-start.13 = (f32[128,128]{1,0:T(8,128)S(1)}, f32[128,128]{1,0:T(8,128)}, u32[]{:S(2)}) copy-start(f32[128,128]{1,0:T(8,128)} %constant.111.clone.refs_7_.refs_15_) | copy-start | bytes 196612
  8.5 2.9 %copy-start.14 = (f32[2,16,512]{2,1,0:T(8,128)S(1)}, f32[2,16,512]{2,1,0:T(8,128)}, u32[]{:S(2)}) copy-start(f32[2,16,512]{2,1,0:T(8,128)} %constant.115.clone.refs_9_) | copy-start | bytes 196612
  8.5 2.9 %copy-start.17 = (f32[2,16,16]{2,1,0:T(8,128)S(1)}, f32[2,16,16]{2,1,0:T(8,128)}, u32[]{:S(2)}) copy-start(f32[2,16,16]{2,1,0:T(8,128)} %constant.113.clone.refs_8_) | copy-start | bytes 6148
  14.9 17.4 %collective-permute-start.2 = (f32[128,512]{1,0:T(8,128)S(1)}, f32[128,512]{1,0:T(8,128)S(1)}, u32[]{:S(2)}, u32[]{:S(2)}) collective-permute-start(f32[128,512]{1,0:T(8,128)S(1)} %get-tuple-element.31), channel_id=1, source_target_pairs={{0,64},{1,65},{2,66},{3,67},{4,68},{5,69},{6,70},{7,71},{8,72},{9,... | collective-permute-start | bytes 786440 | tf_op jit(solution)/shard_map/ppermute | solution.py:873
  17.9 14.4 %collective-permute-start.3 = (f32[400,128]{1,0:T(8,128)S(1)}, f32[400,128]{1,0:T(8,128)S(1)}, u32[]{:S(2)}, u32[]{:S(2)}) collective-permute-start(f32[400,128]{1,0:T(8,128)S(1)} %get-tuple-element.35), channel_id=1, source_target_pairs={{0,1},{1,0},{2,3},{3,2},{4,5},{5,4},{6,7},{7,6},{8,9},{9,8},{10,11... | collective-permute-start | bytes 614408 | tf_op jit(solution)/shard_map/ppermute | solution.py:873
  19.6 8.4 %collective-permute-start = (f32[272,128]{1,0:T(8,128)S(1)}, f32[272,128]{1,0:T(8,128)S(1)}, u32[]{:S(2)}, u32[]{:S(2)}) collective-permute-start(f32[272,128]{1,0:T(8,128)S(1)} %get-tuple-element.29.refs_10_.refs_2_.refs_6_.refs_8_), channel_id=1, source_target_pairs={{0,31},{1,2},{2,1},{3,4},{4,3},{5,6},{6,5},{7,8},{8,7},{9,10},{10,... | collective-permute-start | bytes 417800 | tf_op jit(solution)/shard_map/ppermute | solution.py:873
  24.1 8.1 %collective-permute-start.5 = (f32[2,16,512]{2,1,0:T(8,128)S(1)}, f32[2,16,512]{2,1,0:T(8,128)S(1)}, u32[]{:S(2)}, u32[]{:S(2)}) collective-permute-start(f32[2,16,512]{2,1,0:T(8,128)S(1)} %get-tuple-element.32.refs_0_.refs_3_), channel_id=1, source_target_pairs={{0,3},{1,2},{2,1},{3,0},{4,7},{5,6},{6,5},{7,4},{8,11},{9,10},{10,... | collective-permute-start | bytes 196616 | tf_op jit(solution)/shard_map/ppermute | solution.py:873
  24.1 8.1 %collective-permute-start.4 = (f32[2,16,512]{2,1,0:T(8,128)S(1)}, f32[2,16,512]{2,1,0:T(8,128)S(1)}, u32[]{:S(2)}, u32[]{:S(2)}) collective-permute-start(f32[2,16,512]{2,1,0:T(8,128)S(1)} %get-tuple-element.32.refs_0_.refs_3_), channel_id=1, source_target_pairs={{0,2},{1,3},{2,0},{3,1},{4,6},{5,7},{6,4},{7,5},{8,10},{9,11},{10,... | collective-permute-start | bytes 196616 | tf_op jit(solution)/shard_map/ppermute | solution.py:873
  24.3 8.0 %copy-start.8 = (f32[2,16,512]{2,1,0:T(8,128)S(1)}, f32[2,16,512]{2,1,0:T(8,128)}, u32[]{:S(2)}) copy-start(f32[2,16,512]{2,1,0:T(8,128)} %constant.114.clone.refs_7_.refs_9_) | copy-start | bytes 196612
  33.0 11.1 %collective-permute-start.8 = (f32[4,16,512]{2,1,0:T(8,128)S(1)}, f32[4,16,512]{2,1,0:T(8,128)S(1)}, u32[]{:S(2)}, u32[]{:S(2)}) collective-permute-start(f32[4,16,512]{2,1,0:T(8,128)S(1)} %get-tuple-element.40.refs_3_), channel_id=1, source_target_pairs={{0,64},{1,65},{2,66},{3,67},{4,68},{5,69},{6,70},{7,71},{8,72},{9,... | collective-permute-start | bytes 393224 | tf_op jit(solution)/shard_map/ppermute | solution.py:873
  33.7 10.3 %collective-permute-start.7 = (f32[152,128]{1,0:T(8,128)S(1)}, f32[152,128]{1,0:T(8,128)S(1)}, u32[]{:S(2)}, u32[]{:S(2)}) collective-permute-start(f32[152,128]{1,0:T(8,128)S(1)} %shard_map.210.refs_0_), channel_id=1, source_target_pairs={{0,96},{1,97},{2,98},{3,99},{4,100},{5,101},{6,102},{7,103},{8,104... | collective-permute-start | bytes 233480 | tf_op jit(solution)/shard_map/ppermute | solution.py:873
  37.4 6.6 %collective-permute-start.6 = (f32[152,128]{1,0:T(8,128)S(1)}, f32[152,128]{1,0:T(8,128)S(1)}, u32[]{:S(2)}, u32[]{:S(2)}) collective-permute-start(f32[152,128]{1,0:T(8,128)S(1)} %shard_map.210.refs_0_), channel_id=1, source_target_pairs={{0,32},{1,33},{2,34},{3,35},{4,36},{5,37},{6,38},{7,39},{8,40},{9,... | collective-permute-start | bytes 233480 | tf_op jit(solution)/shard_map/ppermute | solution.py:873
  37.4 6.6 %collective-permute-start.10 = (f32[2,16,512]{2,1,0:T(8,128)S(1)}, f32[2,16,512]{2,1,0:T(8,128)S(1)}, u32[]{:S(2)}, u32[]{:S(2)}) collective-permute-start(f32[2,16,512]{2,1,0:T(8,128)S(1)} %get-tuple-element.36.refs_0_), channel_id=1, source_target_pairs={{0,68},{1,69},{2,70},{3,71},{4,64},{5,65},{6,66},{7,67},{8,76},{9,... | collective-permute-start | bytes 196616 | tf_op jit(solution)/shard_map/ppermute | solution.py:873
  38.3 5.6 %collective-permute-start.9 = (f32[2,16,512]{2,1,0:T(8,128)S(1)}, f32[2,16,512]{2,1,0:T(8,128)S(1)}, u32[]{:S(2)}, u32[]{:S(2)}) collective-permute-start(f32[2,16,512]{2,1,0:T(8,128)S(1)} %get-tuple-element.36.refs_0_), channel_id=1, source_target_pairs={{0,4},{1,5},{2,6},{3,7},{4,0},{5,1},{6,2},{7,3},{8,12},{9,13},{10,... | collective-permute-start | bytes 196616 | tf_op jit(solution)/shard_map/ppermute | solution.py:873
  44.6 12.4 %collective-permute-start.11 = (f32[128,512]{1,0:T(8,128)S(1)}, f32[128,512]{1,0:T(8,128)S(1)}, u32[]{:S(2)}, u32[]{:S(2)}) collective-permute-start(f32[128,512]{1,0:T(8,128)S(1)} %get-tuple-element.47), channel_id=1, source_target_pairs={{0,64},{1,65},{2,66},{3,67},{4,68},{5,69},{6,70},{7,71},{8,72},{9,... | collective-permute-start | bytes 786440 | tf_op jit(solution)/shard_map/ppermute | solution.py:873
  47.3 9.7 %collective-permute-start.14 = (f32[2,16,512]{2,1,0:T(8,128)S(1)}, f32[2,16,512]{2,1,0:T(8,128)S(1)}, u32[]{:S(2)}, u32[]{:S(2)}) collective-permute-start(f32[2,16,512]{2,1,0:T(8,128)S(1)} %get-tuple-element.42.refs_0_.refs_4_), channel_id=1, source_target_pairs={{0,24},{1,25},{2,26},{3,27},{4,28},{5,29},{6,30},{7,31},{8,0},{9,1... | collective-permute-start | bytes 196616 | tf_op jit(solution)/shard_map/ppermute | solution.py:873
  48.5 8.5 %collective-permute-start.13 = (f32[2,16,512]{2,1,0:T(8,128)S(1)}, f32[2,16,512]{2,1,0:T(8,128)S(1)}, u32[]{:S(2)}, u32[]{:S(2)}) collective-permute-start(f32[2,16,512]{2,1,0:T(8,128)S(1)} %get-tuple-element.42.refs_0_.refs_4_), channel_id=1, source_target_pairs={{0,16},{1,17},{2,18},{3,19},{4,20},{5,21},{6,22},{7,23},{8,24},{9,... | collective-permute-start | bytes 196616 | tf_op jit(solution)/shard_map/ppermute | solution.py:873
  49.5 7.5 %collective-permute-start.12 = (f32[2,16,512]{2,1,0:T(8,128)S(1)}, f32[2,16,512]{2,1,0:T(8,128)S(1)}, u32[]{:S(2)}, u32[]{:S(2)}) collective-permute-start(f32[2,16,512]{2,1,0:T(8,128)S(1)} %get-tuple-element.42.refs_0_.refs_4_), channel_id=1, source_target_pairs={{0,8},{1,9},{2,10},{3,11},{4,12},{5,13},{6,14},{7,15},{8,16},{9,17... | collective-permute-start | bytes 196616 | tf_op jit(solution)/shard_map/ppermute | solution.py:873
  50.0 7.0 %copy-start.1 = (bf16[2,512,512]{2,1,0:T(8,128)(2,1)S(1)}, bf16[2,512,512]{2,1,0:T(8,128)(2,1)}, u32[]{:S(2)}) copy-start(bf16[2,512,512]{2,1,0:T(8,128)(2,1)} %constant.104.clone.refs_12_.refs_2_) | copy-start | bytes 3145732
  50.0 7.0 %copy-start.2 = (bf16[2,512,512]{2,1,0:T(8,128)(2,1)S(1)}, bf16[2,512,512]{2,1,0:T(8,128)(2,1)}, u32[]{:S(2)}) copy-start(bf16[2,512,512]{2,1,0:T(8,128)(2,1)} %constant.103.clone.refs_11_.refs_1_) | copy-start | bytes 3145732
  50.0 7.1 %copy-start.9 = (bf16[256,256]{1,0:T(8,128)(2,1)S(1)}, bf16[256,256]{1,0:T(8,128)(2,1)}, u32[]{:S(2)}) copy-start(bf16[256,256]{1,0:T(8,128)(2,1)} %constant.108.clone.refs_14_.refs_4_) | copy-start | bytes 393220
  50.0 7.1 %copy-start.10 = (bf16[256,256]{1,0:T(8,128)(2,1)S(1)}, bf16[256,256]{1,0:T(8,128)(2,1)}, u32[]{:S(2)}) copy-start(bf16[256,256]{1,0:T(8,128)(2,1)} %constant.107.clone.refs_13_.refs_3_) | copy-start | bytes 393220
  50.0 7.1 %copy-start.16 = (f32[2,16,16]{2,1,0:T(8,128)S(1)}, f32[2,16,16]{2,1,0:T(8,128)}, u32[]{:S(2)}) copy-start(f32[2,16,16]{2,1,0:T(8,128)} %constant.112.clone.refs_16_) | copy-start | bytes 6148
  61.7 5.0 %collective-permute-start.16 = (f32[4,512,128]{2,1,0:T(8,128)S(1)}, f32[4,512,128]{2,1,0:T(8,128)S(1)}, u32[]{:S(2)}, u32[]{:S(2)}) collective-permute-start(f32[4,512,128]{2,1,0:T(8,128)S(1)} %get-tuple-element.52), channel_id=1, source_target_pairs={{0,32},{1,33},{2,34},{3,35},{4,36},{5,37},{6,38},{7,39},{8,40},{9,... | collective-permute-start | bytes 3145736 | tf_op jit(solution)/shard_map/ppermute | solution.py:873
  63.7 3.0 %collective-permute-start.15 = (f32[512,256]{1,0:T(8,128)S(1)}, f32[512,256]{1,0:T(8,128)S(1)}, u32[]{:S(2)}, u32[]{:S(2)}) collective-permute-start(f32[512,256]{1,0:T(8,128)S(1)} %get-tuple-element.49.refs_0_), channel_id=1, source_target_pairs={{0,32},{1,33},{2,34},{3,35},{4,36},{5,37},{6,38},{7,39},{8,40},{9,... | collective-permute-start | bytes 1572872 | tf_op jit(solution)/shard_map/ppermute | solution.py:873

commit v5 on v4

--- a/solution.py
+++ b/solution.py
@@ -191,7 +191,7 @@
         out[3 * own + 1, rows] = 1.0 / other[own]
         return nothing
 
-    lax.fori_loop(0, width // 8, tile, 0)
+    lax.fori_loop(0, width // 16, lambda k, c: tile(2 * k + 1, tile(2 * k, c)), 0)
 
 
 def arrived_body(
@@ -234,7 +234,7 @@
             sums[parity, own + i] += term if (own - i) % 2 == 0 else -term
         return nothing
 
-    lax.fori_loop(0, width // 8, tile, 0)
+    lax.fori_loop(0, width // 16, lambda k, c: tile(2 * k + 1, tile(2 * k, c)), 0)
     total = jnp.sum(sums[...], axis=2)
     modal = lambda v: jnp.dot(
         basis_t[s_ref[1]], v, precision=HIGHEST, preferred_element_type=jnp.float32
@@ -408,7 +408,7 @@
         first[rows] = jnp.where(is_low, far_first, value)
         return nothing
 
-    lax.fori_loop(0, width // 8, tile, 0)
+    lax.fori_loop(0, width // 16, lambda k, c: tile(2 * k + 1, tile(2 * k, c)), 0)
     table_high = span_t_high[s_ref[0]]
     table_low = span_t_low[s_ref[0]]
     line = times(first[...], table_high, table_low).T

time: 69.2 us -> 69.2 us (level)
  no operation moved by 1% of the time
where the time goes in v5:
time: 69.2 us; the launch traced here: 68.9 us
  Pallas kernels  37.3 us (54%)
  starting transfers between devices  23.5 us (34%)
  waiting for transfers between devices  5.02 us (7%)
  local copies, waits for them, and re-layouts  2.04 us (3%)
  between operations  1.04 us (2%)
    pallas_call x13, Pallas kernels, run(): pl.pallas_call(inner, out_shape=outs, in_specs=specs, out_specs=out_specs...  36.5 us
    ppermute x17, starting transfers between devices, move(): return lax.ppermute(value, ('grp', 'pen'), pairs)  23.5 us
    ppermute x17, waiting for transfers between devices, move(): return lax.ppermute(value, ('grp', 'pen'), pairs)  5.02 us
    unnamed x40, local copies, waits for them, and re-layouts  1.96 us
  transfers between devices with their start and end apart: 17, of which 2 were waited for; matrix products, arithmetic and copies ran while one was open for 0% of the time, Pallas kernels for 34%

profile of v5, /device:TPU:1, one launch (start us, length us, event | category | flops | bytes accessed | tf_op | source)
XLA Modules:
  0.0 68.9 jit_solution(4355730322197962854)
XLA Ops:
  0.7 0.1 stack.33.s_ref
  0.8 0.8 %copy-done.15 = f32[128,128]{1,0:T(8,128)S(1)} copy-done((f32[128,128]{1,0:T(8,128)S(1)}, f32[128,128]{1,0:T(8,128)}, u32[]{:S(2)}) %copy-start.15) | copy-done | bytes 65560
  1.6 0.7 copy-done.18
  2.3 1.4 %shard_map.203.after.refs_6_.refs_10_ = f32[26,128,512]{2,1,0:T(8,128)S(1)} custom-call(s32[9]{0:T(128)S(1)} %stack.33.s_ref, f32[2,1,512]{2,1,0:T(1,128)S(1)} %copy-done.18, f32[128,128]{1,0:T(8,128)S(1)} %copy-done.15), custom_call_target="tpu_custom_call" | custom-call | flops 1 | bytes 442800 | tf_op jit(solution)/shard_map/pallas_call | solution.py:117
  3.7 0.2 copy-done.6
  3.9 0.8 %shard_map.204 = (f32[4,512,128]{2,1,0:T(8,128)S(1)}, f32[4,512,128]{2,1,0:T(8,128)S(1)}) custom-call(s32[9]{0:T(128)S(1)} %stack.33.s_ref, f32[26,128,512]{2,1,0:T(8,128)S(1)} %shard_map.203.after.refs_6_.refs_10_, f32[4,1024,128]{2,1,0:T(8,128)S(1)} %copy-done.6), custom_call_target="tpu_custom_call" | custom-call | flops 1 | bytes 295200 | tf_op jit(solution)/shard_map/pallas_call | solution.py:130
  4.7 1.5 %collective-permute-start.1 = (f32[4,512,128]{2,1,0:T(8,128)S(1)}, f32[4,512,128]{2,1,0:T(8,128)S(1)}, u32[]{:S(2)}, u32[]{:S(2)}) collective-permute-start(f32[4,512,128]{2,1,0:T(8,128)S(1)} %get-tuple-element.30), channel_id=1, source_target_pairs={{0,32},{1,33},{2,34},{3,35},{4,36},{5,37},{6,38},{7,39},{8,40},{9,... | collective-permute-start | bytes 3145736 | tf_op jit(solution)/shard_map/ppermute | solution.py:873
  6.2 0.0 copy-done.3
  6.2 0.0 copy-done.4
  6.2 0.0 copy-done.11
  6.2 0.0 copy-done.12
  6.2 0.0 copy-start
  6.2 0.0 copy-start.5
  6.3 0.0 copy-start.7
  6.3 0.0 copy-start.19
  6.3 2.1 %shard_map.205.refs_1_ = f32[4,128,512]{2,1,0:T(8,128)S(1)} custom-call(s32[9]{0:T(128)S(1)} %stack.33.s_ref, f32[4,512,128]{2,1,0:T(8,128)S(1)} %get-tuple-element.28.refs_0_, bf16[256,256]{1,0:T(8,128)(2,1)S(1)} %copy-done.12, bf16[256,256]{1,0:T(8,128)(2,1)S(1)} %copy-done.11, bf16[2,512,512]{2,1,0:T(8,128)(2,1)S(1)} %copy-done.4, ...), custom_call_target="tpu_custom_call" | custom-call | flops 1 | bytes 774900 | tf_op jit(solution)/shard_map/pallas_call | solution.py:117
  8.3 0.0 copy-done
  8.4 0.1 copy-done.7
  8.5 2.8 %shard_map.206 = (f32[16,256,128]{2,1,0:T(8,128)S(1)}, f32[272,128]{1,0:T(8,128)S(1)}, f32[136,128]{1,0:T(8,128)S(1)}) custom-call(s32[9]{0:T(128)S(1)} %stack.33.s_ref, f32[2]{0:T(128)S(1)} %copy-done.19, f32[4,128,512]{2,1,0:T(8,128)S(1)} %shard_map.205.refs_1_, f32[16,256,128]{2,1,0:T(8,128)S(1)} %copy-done, s32[16,256,128]{2,1,0:T(8,128)S(1)} %copy-done.7, ...), custom_call_target="tpu_custom_call" | custom-call | flops 1 | bytes 1033200 | tf_op jit(solution)/shard_map/pallas_call | solution.py:117
  11.4 0.0 collective-permute-done.1.refs_0_
  11.4 3.4 %shard_map.207 = (f32[8,128,512]{2,1,0:T(8,128)S(1)}, f32[2,16,512]{2,1,0:T(8,128)S(1)}, f32[128,512]{1,0:T(8,128)S(1)}, f32[128,512]{1,0:T(8,128)S(1)}, f32[400,128]{1,0:T(8,128)S(1)}) custom-call(s32[9]{0:T(128)S(1)} %stack.33.s_ref, f32[4,512,128]{2,1,0:T(8,128)S(1)} %collective-permute-done.1.refs_0_, f32[4,128,512]{2,1,0:T(8,128)S(1)} %shard_map.205.refs_1_, ...), custom_call_target="tpu_custom_call" | custom-call | flops 1 | bytes 1254600 | tf_op jit(solution)/shard_map/pallas_call | solution.py:117
  14.8 3.1 %collective-permute-start.2 = (f32[128,512]{1,0:T(8,128)S(1)}, f32[128,512]{1,0:T(8,128)S(1)}, u32[]{:S(2)}, u32[]{:S(2)}) collective-permute-start(f32[128,512]{1,0:T(8,128)S(1)} %get-tuple-element.31), channel_id=1, source_target_pairs={{0,64},{1,65},{2,66},{3,67},{4,68},{5,69},{6,70},{7,71},{8,72},{9,... | collective-permute-start | bytes 786440 | tf_op jit(solution)/shard_map/ppermute | solution.py:873
  17.9 1.7 %collective-permute-start.3 = (f32[400,128]{1,0:T(8,128)S(1)}, f32[400,128]{1,0:T(8,128)S(1)}, u32[]{:S(2)}, u32[]{:S(2)}) collective-permute-start(f32[400,128]{1,0:T(8,128)S(1)} %get-tuple-element.35), channel_id=1, source_target_pairs={{0,1},{1,0},{2,3},{3,2},{4,5},{5,4},{6,7},{7,6},{8,9},{9,8},{10,11... | collective-permute-start | bytes 614408 | tf_op jit(solution)/shard_map/ppermute | solution.py:873
  19.5 4.5 %collective-permute-start = (f32[272,128]{1,0:T(8,128)S(1)}, f32[272,128]{1,0:T(8,128)S(1)}, u32[]{:S(2)}, u32[]{:S(2)}) collective-permute-start(f32[272,128]{1,0:T(8,128)S(1)} %get-tuple-element.29.refs_10_.refs_2_.refs_6_.refs_8_), channel_id=1, source_target_pairs={{0,31},{1,2},{2,1},{3,4},{4,3},{5,6},{6,5},{7,8},{8,7},{9,10},{10,... | collective-permute-start | bytes 417800 | tf_op jit(solution)/shard_map/ppermute | solution.py:873
  24.1 0.0 collective-permute-start.5
  24.1 0.2 collective-permute-start.4
  24.3 3.7 %shard_map.208 = (f32[16,256,128]{2,1,0:T(8,128)S(1)}, f32[16,256,128]{2,1,0:T(8,128)S(1)}) custom-call(s32[9]{0:T(128)S(1)} %stack.33.s_ref, f32[2,16,512]{2,1,0:T(8,128)S(1)} %get-tuple-element.32.refs_0_.refs_3_, f32[16,256,128]{2,1,0:T(8,128)S(1)} %copy-done, f32[16,256,128]{2,1,0:T(8,128)S(1)} %get-tuple-element.33.refs_2_.refs_3_.refs_6_, ...), custom_call_target="tpu_custom_call" | custom-call | flops 1 | bytes 1660500 | tf_op jit(solution)/shard_map/pallas_call | solution.py:117
  28.0 0.0 collective-permute-done.refs_0_.refs_4_.refs_8_.refs_11_
  28.0 4.3 %collective-permute-done.5.refs_6_ = f32[2,16,512]{2,1,0:T(8,128)S(1)} collective-permute-done((f32[2,16,512]{2,1,0:T(8,128)S(1)}, f32[2,16,512]{2,1,0:T(8,128)S(1)}, u32[]{:S(2)}, u32[]{:S(2)}) %collective-permute-start.5) | collective-permute-done | bytes 65568 | tf_op jit(solution)/shard_map/ppermute | solution.py:873
  32.2 0.0 collective-permute-done.4.refs_5_
  32.2 0.0 collective-permute-done.3.refs_4_.refs_3_.refs_7_.refs_10_
  32.2 0.0 collective-permute-done.2.refs_1_.refs_2_
  32.2 0.0 copy-done.8
  32.3 0.6 shard_map.209
  32.9 0.1 collective-permute-start.8
  33.0 0.6 shard_map.210.refs_0_
  33.6 3.7 %collective-permute-start.7 = (f32[152,128]{1,0:T(8,128)S(1)}, f32[152,128]{1,0:T(8,128)S(1)}, u32[]{:S(2)}, u32[]{:S(2)}) collective-permute-start(f32[152,128]{1,0:T(8,128)S(1)} %shard_map.210.refs_0_), channel_id=1, source_target_pairs={{0,96},{1,97},{2,98},{3,99},{4,100},{5,101},{6,102},{7,103},{8,104... | collective-permute-start | bytes 233480 | tf_op jit(solution)/shard_map/ppermute | solution.py:873
  37.3 0.0 collective-permute-start.6
  37.3 1.0 %collective-permute-start.10 = (f32[2,16,512]{2,1,0:T(8,128)S(1)}, f32[2,16,512]{2,1,0:T(8,128)S(1)}, u32[]{:S(2)}, u32[]{:S(2)}) collective-permute-start(f32[2,16,512]{2,1,0:T(8,128)S(1)} %get-tuple-element.36.refs_0_), channel_id=1, source_target_pairs={{0,68},{1,69},{2,70},{3,71},{4,64},{5,65},{6,66},{7,67},{8,76},{9,... | collective-permute-start | bytes 196616 | tf_op jit(solution)/shard_map/ppermute | solution.py:873
  38.3 0.4 collective-permute-start.9
  38.7 5.3 %shard_map.211 = (f32[16,256,128]{2,1,0:T(8,128)S(1)}, f32[16,256,128]{2,1,0:T(8,128)S(1)}, f32[5,256,128]{2,1,0:T(8,128)S(1)}) custom-call(s32[9]{0:T(128)S(1)} %stack.33.s_ref, f32[152,128]{1,0:T(8,128)S(1)} %shard_map.210.refs_0_, f32[16,256,128]{2,1,0:T(8,128)S(1)} %get-tuple-element.34.refs_2_.refs_1_, ...), custom_call_target="tpu_custom_call", output_to_operand_aliasing={{0}: (2, {})} | custom-call | flops 1 | bytes 1660500 | tf_op jit(solution)/shard_map/pallas_call | solution.py:117
  43.9 0.0 collective-permute-done.10.refs_6_
  43.9 0.0 collective-permute-done.9.refs_5_
  43.9 0.0 collective-permute-done.7.refs_2_.refs_13_
  44.0 0.0 collective-permute-done.6.refs_1_.refs_12_
  44.0 0.0 collective-permute-done.8.refs_4_
  44.0 0.6 shard_map.212
  44.6 2.6 %collective-permute-start.11 = (f32[128,512]{1,0:T(8,128)S(1)}, f32[128,512]{1,0:T(8,128)S(1)}, u32[]{:S(2)}, u32[]{:S(2)}) collective-permute-start(f32[128,512]{1,0:T(8,128)S(1)} %get-tuple-element.47), channel_id=1, source_target_pairs={{0,64},{1,65},{2,66},{3,67},{4,68},{5,69},{6,70},{7,71},{8,72},{9,... | collective-permute-start | bytes 786440 | tf_op jit(solution)/shard_map/ppermute | solution.py:873
  47.2 1.3 %collective-permute-start.14 = (f32[2,16,512]{2,1,0:T(8,128)S(1)}, f32[2,16,512]{2,1,0:T(8,128)S(1)}, u32[]{:S(2)}, u32[]{:S(2)}) collective-permute-start(f32[2,16,512]{2,1,0:T(8,128)S(1)} %get-tuple-element.42.refs_0_.refs_4_), channel_id=1, source_target_pairs={{0,24},{1,25},{2,26},{3,27},{4,28},{5,29},{6,30},{7,31},{8,0},{9,1... | collective-permute-start | bytes 196616 | tf_op jit(solution)/shard_map/ppermute | solution.py:873
  48.5 1.0 %collective-permute-start.13 = (f32[2,16,512]{2,1,0:T(8,128)S(1)}, f32[2,16,512]{2,1,0:T(8,128)S(1)}, u32[]{:S(2)}, u32[]{:S(2)}) collective-permute-start(f32[2,16,512]{2,1,0:T(8,128)S(1)} %get-tuple-element.42.refs_0_.refs_4_), channel_id=1, source_target_pairs={{0,16},{1,17},{2,18},{3,19},{4,20},{5,21},{6,22},{7,23},{8,24},{9,... | collective-permute-start | bytes 196616 | tf_op jit(solution)/shard_map/ppermute | solution.py:873
  49.4 0.5 collective-permute-start.12
  49.9 0.0 copy-start.16
  49.9 7.0 %shard_map.213 = (f32[16,256,128]{2,1,0:T(8,128)S(1)}, f32[16,256,128]{2,1,0:T(8,128)S(1)}, f32[5,256,128]{2,1,0:T(8,128)S(1)}, f32[16,256,128]{2,1,0:T(8,128)S(...) custom-call(s32[9]{0:T(128)S(1)} %stack.33.s_ref, ...), custom_call_target="tpu_custom_call", output_to_operand_aliasing={{0}: (2, {}), {1}: (3, {}), {2}: (4, {}), {3}: (5, {})} | custom-call | flops 1 | bytes 2029500 | tf_op jit(solution)/shard_map/pallas_call | solution.py:117
  56.9 0.0 collective-permute-done.14.refs_8_
  56.9 0.0 collective-permute-done.13.refs_7_
  56.9 0.0 collective-permute-done.12.refs_6_
  56.9 0.0 collective-permute-done.11.refs_3_
  57.0 4.6 %shard_map.214 = (f32[512,256]{1,0:T(8,128)S(1)}, f32[4,512,128]{2,1,0:T(8,128)S(1)}, f32[4,128,512]{2,1,0:T(8,128)S(1)}) custom-call(s32[9]{0:T(128)S(1)} %stack.33.s_ref, f32[5,256,128]{2,1,0:T(8,128)S(1)} %get-tuple-element.45.refs_0_.refs_2_, f32[8,128,512]{2,1,0:T(8,128)S(1)} %get-tuple-element.46.refs_1_, ...), custom_call_target="tpu_custom_call" | custom-call | flops 1 | bytes 2546100 | tf_op jit(solution)/shard_map/pallas_call | solution.py:117
  61.6 2.0 %collective-permute-start.16 = (f32[4,512,128]{2,1,0:T(8,128)S(1)}, f32[4,512,128]{2,1,0:T(8,128)S(1)}, u32[]{:S(2)}, u32[]{:S(2)}) collective-permute-start(f32[4,512,128]{2,1,0:T(8,128)S(1)} %get-tuple-element.52), channel_id=1, source_target_pairs={{0,32},{1,33},{2,34},{3,35},{4,36},{5,37},{6,38},{7,39},{8,40},{9,... | collective-permute-start | bytes 3145736 | tf_op jit(solution)/shard_map/ppermute | solution.py:873
  63.6 0.1 collective-permute-start.15
  63.7 2.2 %shard_map.215.refs_4_ = f32[4,512,128]{2,1,0:T(8,128)S(1)} custom-call(s32[9]{0:T(128)S(1)} %stack.33.s_ref, f32[4,128,512]{2,1,0:T(8,128)S(1)} %get-tuple-element.51.refs_0_, bf16[2,512,512]{2,1,0:T(8,128)(2,1)S(1)} %copy-done.2, bf16[2,512,512]{2,1,0:T(8,128)(2,1)S(1)} %copy-done.1, bf16[256,256]{1,0:T(8,128)(2,1)S(1)} %copy-done.10, ...), custom_call_target="tpu_custom_call" | custom-call | flops 1 | bytes 811800 | tf_op jit(solution)/shard_map/pallas_call | solution.py:117
  65.9 0.7 %collective-permute-done.15.refs_1_ = f32[512,256]{1,0:T(8,128)S(1)} collective-permute-done((f32[512,256]{1,0:T(8,128)S(1)}, f32[512,256]{1,0:T(8,128)S(1)}, u32[]{:S(2)}, u32[]{:S(2)}) %collective-permute-start.15) | collective-permute-done | bytes 524320 | tf_op jit(solution)/shard_map/ppermute | solution.py:873
  66.6 0.0 collective-permute-done.16.refs_5_
  66.6 2.3 %shard_map.216 = (f32[4,1024,128]{2,1,0:T(8,128)}, f32[16,256,128]{2,1,0:T(8,128)}) custom-call(s32[9]{0:T(128)S(1)} %stack.33.s_ref, f32[512,256]{1,0:T(8,128)S(1)} %get-tuple-element.49.refs_0_, f32[512,256]{1,0:T(8,128)S(1)} %collective-permute-done.15.refs_1_, ...), custom_call_target="tpu_custom_call", output_to_operand_aliasing={{1}: (7, {})} | custom-call | flops 1 | bytes 922500 | tf_op jit(solution)/shard_map/pallas_call | solution.py:117
  (25 shorter events, 0.0 us)
Async XLA Ops:
  0.8 0.8 %copy-start.15 = (f32[128,128]{1,0:T(8,128)S(1)}, f32[128,128]{1,0:T(8,128)}, u32[]{:S(2)}) copy-start(f32[128,128]{1,0:T(8,128)} %constant.110.clone.refs_1_) | copy-start | bytes 196612
  1.6 0.7 copy-start.18
  2.3 1.6 %copy-start.6 = (f32[4,1024,128]{2,1,0:T(8,128)S(1)}, f32[4,1024,128]{2,1,0:T(8,128)}, u32[]{:S(2)}) copy-start(f32[4,1024,128]{2,1,0:T(8,128)} %source.1) | copy-start | bytes 6291460
  3.9 2.3 %copy-start.3 = (bf16[2,512,512]{2,1,0:T(8,128)(2,1)S(1)}, bf16[2,512,512]{2,1,0:T(8,128)(2,1)}, u32[]{:S(2)}) copy-start(bf16[2,512,512]{2,1,0:T(8,128)(2,1)} %constant.102.clone.refs_4_.refs_5_) | copy-start | bytes 3145732
  3.9 2.3 %copy-start.4 = (bf16[2,512,512]{2,1,0:T(8,128)(2,1)S(1)}, bf16[2,512,512]{2,1,0:T(8,128)(2,1)}, u32[]{:S(2)}) copy-start(bf16[2,512,512]{2,1,0:T(8,128)(2,1)} %constant.101.clone.refs_3_.refs_4_) | copy-start | bytes 3145732
  3.9 2.3 %copy-start.11 = (bf16[256,256]{1,0:T(8,128)(2,1)S(1)}, bf16[256,256]{1,0:T(8,128)(2,1)}, u32[]{:S(2)}) copy-start(bf16[256,256]{1,0:T(8,128)(2,1)} %constant.106.clone.refs_2_.refs_3_) | copy-start | bytes 393220
  3.9 2.3 %copy-start.12 = (bf16[256,256]{1,0:T(8,128)(2,1)S(1)}, bf16[256,256]{1,0:T(8,128)(2,1)}, u32[]{:S(2)}) copy-start(bf16[256,256]{1,0:T(8,128)(2,1)} %constant.105.clone.refs_1_.refs_2_) | copy-start | bytes 393220
  4.7 6.6 %collective-permute-start.1 = (f32[4,512,128]{2,1,0:T(8,128)S(1)}, f32[4,512,128]{2,1,0:T(8,128)S(1)}, u32[]{:S(2)}, u32[]{:S(2)}) collective-permute-start(f32[4,512,128]{2,1,0:T(8,128)S(1)} %get-tuple-element.30), channel_id=1, source_target_pairs={{0,32},{1,33},{2,34},{3,35},{4,36},{5,37},{6,38},{7,39},{8,40},{9,... | collective-permute-start | bytes 3145736 | tf_op jit(solution)/shard_map/ppermute | solution.py:873
  6.2 2.1 %copy-start = (f32[16,256,128]{2,1,0:T(8,128)S(1)}, f32[16,256,128]{2,1,0:T(8,128)}, u32[]{:S(2)}) copy-start(f32[16,256,128]{2,1,0:T(8,128)} %refs_5_.4) | copy-start | bytes 6291460
  6.2 2.1 %copy-start.5 = (f32[256,128]{1,0:T(8,128)S(1)}, f32[256,128]{1,0:T(8,128)}, u32[]{:S(2)}) copy-start(f32[256,128]{1,0:T(8,128)} %refs_7_.4) | copy-start | bytes 393220
  6.3 2.2 %copy-start.7 = (s32[16,256,128]{2,1,0:T(8,128)S(1)}, s32[16,256,128]{2,1,0:T(8,128)}, u32[]{:S(2)}) copy-start(s32[16,256,128]{2,1,0:T(8,128)} %refs_3_.5) | copy-start | bytes 6291460
  6.3 2.2 %copy-start.19 = (f32[2]{0:T(128)S(1)}, f32[2]{0:T(128)}, u32[]{:S(2)}) copy-start(f32[2]{0:T(128)} %refs_0_.2) | copy-start | bytes 28
  8.5 2.9 %copy-start.13 = (f32[128,128]{1,0:T(8,128)S(1)}, f32[128,128]{1,0:T(8,128)}, u32[]{:S(2)}) copy-start(f32[128,128]{1,0:T(8,128)} %constant.111.clone.refs_7_.refs_15_) | copy-start | bytes 196612
  8.5 2.9 %copy-start.14 = (f32[2,16,512]{2,1,0:T(8,128)S(1)}, f32[2,16,512]{2,1,0:T(8,128)}, u32[]{:S(2)}) copy-start(f32[2,16,512]{2,1,0:T(8,128)} %constant.115.clone.refs_9_) | copy-start | bytes 196612
  8.5 2.9 %copy-start.17 = (f32[2,16,16]{2,1,0:T(8,128)S(1)}, f32[2,16,16]{2,1,0:T(8,128)}, u32[]{:S(2)}) copy-start(f32[2,16,16]{2,1,0:T(8,128)} %constant.113.clone.refs_8_) | copy-start | bytes 6148
  14.8 17.4 %collective-permute-start.2 = (f32[128,512]{1,0:T(8,128)S(1)}, f32[128,512]{1,0:T(8,128)S(1)}, u32[]{:S(2)}, u32[]{:S(2)}) collective-permute-start(f32[128,512]{1,0:T(8,128)S(1)} %get-tuple-element.31), channel_id=1, source_target_pairs={{0,64},{1,65},{2,66},{3,67},{4,68},{5,69},{6,70},{7,71},{8,72},{9,... | collective-permute-start | bytes 786440 | tf_op jit(solution)/shard_map/ppermute | solution.py:873
  17.9 14.4 %collective-permute-start.3 = (f32[400,128]{1,0:T(8,128)S(1)}, f32[400,128]{1,0:T(8,128)S(1)}, u32[]{:S(2)}, u32[]{:S(2)}) collective-permute-start(f32[400,128]{1,0:T(8,128)S(1)} %get-tuple-element.35), channel_id=1, source_target_pairs={{0,1},{1,0},{2,3},{3,2},{4,5},{5,4},{6,7},{7,6},{8,9},{9,8},{10,11... | collective-permute-start | bytes 614408 | tf_op jit(solution)/shard_map/ppermute | solution.py:873
  19.5 8.4 %collective-permute-start = (f32[272,128]{1,0:T(8,128)S(1)}, f32[272,128]{1,0:T(8,128)S(1)}, u32[]{:S(2)}, u32[]{:S(2)}) collective-permute-start(f32[272,128]{1,0:T(8,128)S(1)} %get-tuple-element.29.refs_10_.refs_2_.refs_6_.refs_8_), channel_id=1, source_target_pairs={{0,31},{1,2},{2,1},{3,4},{4,3},{5,6},{6,5},{7,8},{8,7},{9,10},{10,... | collective-permute-start | bytes 417800 | tf_op jit(solution)/shard_map/ppermute | solution.py:873
  24.1 8.2 %collective-permute-start.5 = (f32[2,16,512]{2,1,0:T(8,128)S(1)}, f32[2,16,512]{2,1,0:T(8,128)S(1)}, u32[]{:S(2)}, u32[]{:S(2)}) collective-permute-start(f32[2,16,512]{2,1,0:T(8,128)S(1)} %get-tuple-element.32.refs_0_.refs_3_), channel_id=1, source_target_pairs={{0,3},{1,2},{2,1},{3,0},{4,7},{5,6},{6,5},{7,4},{8,11},{9,10},{10,... | collective-permute-start | bytes 196616 | tf_op jit(solution)/shard_map/ppermute | solution.py:873
  24.1 8.2 %collective-permute-start.4 = (f32[2,16,512]{2,1,0:T(8,128)S(1)}, f32[2,16,512]{2,1,0:T(8,128)S(1)}, u32[]{:S(2)}, u32[]{:S(2)}) collective-permute-start(f32[2,16,512]{2,1,0:T(8,128)S(1)} %get-tuple-element.32.refs_0_.refs_3_), channel_id=1, source_target_pairs={{0,2},{1,3},{2,0},{3,1},{4,6},{5,7},{6,4},{7,5},{8,10},{9,11},{10,... | collective-permute-start | bytes 196616 | tf_op jit(solution)/shard_map/ppermute | solution.py:873
  24.3 7.9 %copy-start.8 = (f32[2,16,512]{2,1,0:T(8,128)S(1)}, f32[2,16,512]{2,1,0:T(8,128)}, u32[]{:S(2)}) copy-start(f32[2,16,512]{2,1,0:T(8,128)} %constant.114.clone.refs_7_.refs_9_) | copy-start | bytes 196612
  32.9 11.1 %collective-permute-start.8 = (f32[4,16,512]{2,1,0:T(8,128)S(1)}, f32[4,16,512]{2,1,0:T(8,128)S(1)}, u32[]{:S(2)}, u32[]{:S(2)}) collective-permute-start(f32[4,16,512]{2,1,0:T(8,128)S(1)} %get-tuple-element.40.refs_3_), channel_id=1, source_target_pairs={{0,64},{1,65},{2,66},{3,67},{4,68},{5,69},{6,70},{7,71},{8,72},{9,... | collective-permute-start | bytes 393224 | tf_op jit(solution)/shard_map/ppermute | solution.py:873
  33.6 10.3 %collective-permute-start.7 = (f32[152,128]{1,0:T(8,128)S(1)}, f32[152,128]{1,0:T(8,128)S(1)}, u32[]{:S(2)}, u32[]{:S(2)}) collective-permute-start(f32[152,128]{1,0:T(8,128)S(1)} %shard_map.210.refs_0_), channel_id=1, source_target_pairs={{0,96},{1,97},{2,98},{3,99},{4,100},{5,101},{6,102},{7,103},{8,104... | collective-permute-start | bytes 233480 | tf_op jit(solution)/shard_map/ppermute | solution.py:873
  37.3 6.6 %collective-permute-start.6 = (f32[152,128]{1,0:T(8,128)S(1)}, f32[152,128]{1,0:T(8,128)S(1)}, u32[]{:S(2)}, u32[]{:S(2)}) collective-permute-start(f32[152,128]{1,0:T(8,128)S(1)} %shard_map.210.refs_0_), channel_id=1, source_target_pairs={{0,32},{1,33},{2,34},{3,35},{4,36},{5,37},{6,38},{7,39},{8,40},{9,... | collective-permute-start | bytes 233480 | tf_op jit(solution)/shard_map/ppermute | solution.py:873
  37.3 6.6 %collective-permute-start.10 = (f32[2,16,512]{2,1,0:T(8,128)S(1)}, f32[2,16,512]{2,1,0:T(8,128)S(1)}, u32[]{:S(2)}, u32[]{:S(2)}) collective-permute-start(f32[2,16,512]{2,1,0:T(8,128)S(1)} %get-tuple-element.36.refs_0_), channel_id=1, source_target_pairs={{0,68},{1,69},{2,70},{3,71},{4,64},{5,65},{6,66},{7,67},{8,76},{9,... | collective-permute-start | bytes 196616 | tf_op jit(solution)/shard_map/ppermute | solution.py:873
  38.3 5.6 %collective-permute-start.9 = (f32[2,16,512]{2,1,0:T(8,128)S(1)}, f32[2,16,512]{2,1,0:T(8,128)S(1)}, u32[]{:S(2)}, u32[]{:S(2)}) collective-permute-start(f32[2,16,512]{2,1,0:T(8,128)S(1)} %get-tuple-element.36.refs_0_), channel_id=1, source_target_pairs={{0,4},{1,5},{2,6},{3,7},{4,0},{5,1},{6,2},{7,3},{8,12},{9,13},{10,... | collective-permute-start | bytes 196616 | tf_op jit(solution)/shard_map/ppermute | solution.py:873
  44.6 12.4 %collective-permute-start.11 = (f32[128,512]{1,0:T(8,128)S(1)}, f32[128,512]{1,0:T(8,128)S(1)}, u32[]{:S(2)}, u32[]{:S(2)}) collective-permute-start(f32[128,512]{1,0:T(8,128)S(1)} %get-tuple-element.47), channel_id=1, source_target_pairs={{0,64},{1,65},{2,66},{3,67},{4,68},{5,69},{6,70},{7,71},{8,72},{9,... | collective-permute-start | bytes 786440 | tf_op jit(solution)/shard_map/ppermute | solution.py:873
  47.2 9.7 %collective-permute-start.14 = (f32[2,16,512]{2,1,0:T(8,128)S(1)}, f32[2,16,512]{2,1,0:T(8,128)S(1)}, u32[]{:S(2)}, u32[]{:S(2)}) collective-permute-start(f32[2,16,512]{2,1,0:T(8,128)S(1)} %get-tuple-element.42.refs_0_.refs_4_), channel_id=1, source_target_pairs={{0,24},{1,25},{2,26},{3,27},{4,28},{5,29},{6,30},{7,31},{8,0},{9,1... | collective-permute-start | bytes 196616 | tf_op jit(solution)/shard_map/ppermute | solution.py:873
  48.5 8.4 %collective-permute-start.13 = (f32[2,16,512]{2,1,0:T(8,128)S(1)}, f32[2,16,512]{2,1,0:T(8,128)S(1)}, u32[]{:S(2)}, u32[]{:S(2)}) collective-permute-start(f32[2,16,512]{2,1,0:T(8,128)S(1)} %get-tuple-element.42.refs_0_.refs_4_), channel_id=1, source_target_pairs={{0,16},{1,17},{2,18},{3,19},{4,20},{5,21},{6,22},{7,23},{8,24},{9,... | collective-permute-start | bytes 196616 | tf_op jit(solution)/shard_map/ppermute | solution.py:873
  49.4 7.5 %collective-permute-start.12 = (f32[2,16,512]{2,1,0:T(8,128)S(1)}, f32[2,16,512]{2,1,0:T(8,128)S(1)}, u32[]{:S(2)}, u32[]{:S(2)}) collective-permute-start(f32[2,16,512]{2,1,0:T(8,128)S(1)} %get-tuple-element.42.refs_0_.refs_4_), channel_id=1, source_target_pairs={{0,8},{1,9},{2,10},{3,11},{4,12},{5,13},{6,14},{7,15},{8,16},{9,17... | collective-permute-start | bytes 196616 | tf_op jit(solution)/shard_map/ppermute | solution.py:873
  49.9 7.0 %copy-start.1 = (bf16[2,512,512]{2,1,0:T(8,128)(2,1)S(1)}, bf16[2,512,512]{2,1,0:T(8,128)(2,1)}, u32[]{:S(2)}) copy-start(bf16[2,512,512]{2,1,0:T(8,128)(2,1)} %constant.104.clone.refs_12_.refs_2_) | copy-start | bytes 3145732
  49.9 7.0 %copy-start.2 = (bf16[2,512,512]{2,1,0:T(8,128)(2,1)S(1)}, bf16[2,512,512]{2,1,0:T(8,128)(2,1)}, u32[]{:S(2)}) copy-start(bf16[2,512,512]{2,1,0:T(8,128)(2,1)} %constant.103.clone.refs_11_.refs_1_) | copy-start | bytes 3145732
  49.9 7.1 %copy-start.9 = (bf16[256,256]{1,0:T(8,128)(2,1)S(1)}, bf16[256,256]{1,0:T(8,128)(2,1)}, u32[]{:S(2)}) copy-start(bf16[256,256]{1,0:T(8,128)(2,1)} %constant.108.clone.refs_14_.refs_4_) | copy-start | bytes 393220
  49.9 7.1 %copy-start.10 = (bf16[256,256]{1,0:T(8,128)(2,1)S(1)}, bf16[256,256]{1,0:T(8,128)(2,1)}, u32[]{:S(2)}) copy-start(bf16[256,256]{1,0:T(8,128)(2,1)} %constant.107.clone.refs_13_.refs_3_) | copy-start | bytes 393220
  49.9 7.1 %copy-start.16 = (f32[2,16,16]{2,1,0:T(8,128)S(1)}, f32[2,16,16]{2,1,0:T(8,128)}, u32[]{:S(2)}) copy-start(f32[2,16,16]{2,1,0:T(8,128)} %constant.112.clone.refs_16_) | copy-start | bytes 6148
  61.6 5.0 %collective-permute-start.16 = (f32[4,512,128]{2,1,0:T(8,128)S(1)}, f32[4,512,128]{2,1,0:T(8,128)S(1)}, u32[]{:S(2)}, u32[]{:S(2)}) collective-permute-start(f32[4,512,128]{2,1,0:T(8,128)S(1)} %get-tuple-element.52), channel_id=1, source_target_pairs={{0,32},{1,33},{2,34},{3,35},{4,36},{5,37},{6,38},{7,39},{8,40},{9,... | collective-permute-start | bytes 3145736 | tf_op jit(solution)/shard_map/ppermute | solution.py:873
  63.6 3.0 %collective-permute-start.15 = (f32[512,256]{1,0:T(8,128)S(1)}, f32[512,256]{1,0:T(8,128)S(1)}, u32[]{:S(2)}, u32[]{:S(2)}) collective-permute-start(f32[512,256]{1,0:T(8,128)S(1)} %get-tuple-element.49.refs_0_), channel_id=1, source_target_pairs={{0,32},{1,33},{2,34},{3,35},{4,36},{5,37},{6,38},{7,39},{8,40},{9,... | collective-permute-start | bytes 1572872 | tf_op jit(solution)/shard_map/ppermute | solution.py:873
